TPU v7x, 32 devices: a whole 2x2x4 slice. The times are simulated.
32 devices in a mesh: replica: 4 (over z), fsdp: 8 (over y, x, core).
Axes of the slice: x: 2, y: 2, z: 4, core: 2. Of those that a mesh axis runs over, the one named last changes fastest.
Arguments:
- node_feats: bfloat16 [4096, 1024], P(('replica', 'fsdp')), may hold values from -6 to 6
- neighbor_src: int32 [12, 4096], P(None, ('replica', 'fsdp')), may hold values from 0 to 1023, as said below
- distances: float32 [12, 4096], P(None, ('replica', 'fsdp')), may hold values from 0.8 to 5
- graph_ids: int32 [4, 1024], P('replica', 'fsdp'), may hold values from 0 to 7, never falling along the last dimension, each value on 1 to 256 neighbouring positions
- msg_weight: bfloat16 [1024, 1024], P('fsdp'), may hold values from -0.1875 to 0.1875
- out_weight: bfloat16 [1024, 1024], P('fsdp'), may hold values from -0.1875 to 0.1875
- radial_weight: float32 [8, 1024], replicated, may hold values from -6 to 6
- cotangent: bfloat16 [4096, 1024], P(('replica', 'fsdp')), may hold values from -6 to 6
- fragment: int32 [1], replicated, may hold values from 0 to 7
Outputs:
- node_out: bfloat16 [4096, 1024], P(('replica', 'fsdp'))
- grad_msg: bfloat16 [4, 1024, 1024], P('replica', 'fsdp')
- grad_out: bfloat16 [4, 1024, 1024], P('replica', 'fsdp')
- outer_sum: float32 [2, 1024, 128], P(None, 'fsdp')
Inputs may be any that keep to these rules, and one draw needn't show every extreme that they name: `neighbor_src`: each neighbour index lies within 32 positions of its own atom's index in the group, never equal to it, and inside the group. `graph_ids`: within each group the graph numbers never fall and every graph has at least one atom.
All inputs are finite; a program needn't handle non-finite values. Where the computation divides by a largest or mean magnitude, that divisor is 1e-20 or more.
Results may differ from a plain program's by a relative error of at most 0.02.
Values may be sent and summed in bfloat16 or wider, within the bound.
No kernel may reach another device: no remote copies, remote signals or barrier semaphores. Data moves between devices by JAX's collectives and lax.ppermute only.
A program may use at most 64 MiB of HBM per device.

v0:
```python
import math

import jax
import jax.numpy as jnp
from jax import lax
from jax.sharding import PartitionSpec as P

FRAG = 128
GRAPHS = 8


cutoff = 5.0
sharpness = 2.0
tiny = 1e-06


def with_halo(cells, sides, width):
    for axis, dim in sides:
        count = lax.axis_size(axis)
        ends = count - 1
        head = lax.slice_in_dim(cells, 0, width, axis=dim)
        tail = lax.slice_in_dim(cells, cells.shape[dim] - width, cells.shape[dim], axis=dim)
        cells = jnp.concatenate(
            [
                lax.ppermute(tail, axis, [(i, (i + 1) % count) for i in range(ends)]),
                cells,
                lax.ppermute(head, axis, [((i + 1) % count, i) for i in range(ends)]),
            ],
            axis=dim,
        )
    return cells


def passed_along(value, axis, steps):
    count = lax.axis_size(axis)
    leading, last = (max(0, -steps), min(count, count - steps))
    return lax.ppermute(value, axis, [(source, source + steps) for source in range(leading, last)])


def radial(dist_row, radial_weight):
    basis_count = radial_weight.shape[0]
    centers = cutoff * jnp.arange(basis_count).astype(jnp.float32) / (basis_count - 1)
    envelope = 0.5 * (jnp.cos(jnp.pi * dist_row / cutoff) + 1.0)
    basis = jnp.exp(-sharpness * (dist_row[:, None] - centers[None, :]) ** 2) * envelope[:, None]
    return jnp.dot(
        basis, radial_weight, precision=lax.Precision.HIGHEST, preferred_element_type=jnp.float32
    )


def contract_rows(left, right):
    return lax.dot_general(
        left, right, (((0,), (0,)), ((), ())), preferred_element_type=jnp.float32
    )


def shards(
    node_feats,
    neighbor_src,
    distances,
    graph_ids,
    msg_weight,
    out_weight,
    radial_weight,
    cotangent,
    fragment,
):
    atoms = node_feats.shape[0]
    width = node_feats.shape[1]
    neighbors = neighbor_src.shape[0]
    margin = atoms // 4
    norm = 1.0 / math.sqrt(neighbors)
    first_atom = lax.axis_index("fsdp") * atoms
    empty = jnp.zeros((atoms, width), jnp.float32)
    inputs = node_feats
    projected = jnp.dot(
        inputs,
        lax.all_gather(msg_weight, "fsdp", axis=0, tiled=True),
        preferred_element_type=jnp.float32,
    ).astype(jnp.bfloat16)
    extended = with_halo(projected, (("fsdp", 0),), margin)
    local_src = neighbor_src - first_atom + margin

    def gather_step(k, acc):
        rows = jnp.take(extended, local_src[k], axis=0).astype(jnp.float32)
        return acc + radial(distances[k], radial_weight) * rows

    agg = lax.fori_loop(0, neighbors, gather_step, empty) * norm
    act = jax.nn.silu(agg).astype(jnp.bfloat16)
    inputs = act
    branch_sum = jnp.dot(
        inputs,
        lax.all_gather(out_weight, "fsdp", axis=0, tiled=True),
        preferred_element_type=jnp.float32,
    )
    node_out = (node_feats.astype(jnp.float32) + branch_sum).astype(jnp.bfloat16)
    ids = graph_ids[0]
    onehot = (ids[:, None] == jnp.arange(GRAPHS, dtype=jnp.int32)[None, :]).astype(jnp.float32)
    own_counts = jnp.sum(onehot, axis=0).astype(jnp.int32)
    counts = lax.psum(own_counts, "fsdp")
    weight = jnp.sum(onehot * lax.rsqrt(counts.astype(jnp.float32))[None, :], axis=1)
    dout = (weight[:, None] * cotangent.astype(jnp.float32)).astype(jnp.bfloat16)
    out_rows = lax.psum_scatter(
        contract_rows(act, dout).astype(jnp.bfloat16), "fsdp", scatter_dimension=0, tiled=True
    ).astype(jnp.float32)
    dact = lax.dot_general(
        dout,
        lax.all_gather(out_weight, "fsdp", axis=0, tiled=True),
        (((1,), (1,)), ((), ())),
        preferred_element_type=jnp.float32,
    )
    sig = jax.nn.sigmoid(agg)
    dagg = dact * sig * (1.0 + agg * (1.0 - sig))

    def spread_step(k, acc):
        return acc.at[local_src[k]].add(radial(distances[k], radial_weight) * dagg * norm)

    spread = lax.fori_loop(
        0, neighbors, spread_step, jnp.zeros((atoms + 2 * margin, width), jnp.float32)
    )
    lower_rim = spread[:margin]
    upper_rim = spread[margin + atoms :]
    from_below = passed_along(upper_rim.astype(jnp.bfloat16), "fsdp", 1).astype(upper_rim.dtype)
    from_above = passed_along(lower_rim.astype(jnp.bfloat16), "fsdp", -1).astype(lower_rim.dtype)
    dproj = spread[margin : margin + atoms]
    dproj = dproj.at[:margin].add(from_below)
    dproj = dproj.at[atoms - margin :].add(from_above)
    dproj = dproj.astype(jnp.bfloat16)
    msg_rows = lax.psum_scatter(
        contract_rows(node_feats, dproj).astype(jnp.bfloat16),
        "fsdp",
        scatter_dimension=0,
        tiled=True,
    ).astype(jnp.float32)
    column = fragment[0] * FRAG
    pieces = jnp.stack(
        [
            lax.dynamic_slice_in_dim(msg_rows, column, FRAG, 1),
            lax.dynamic_slice_in_dim(out_rows, column, FRAG, 1),
        ]
    )
    scale = (jnp.max(jnp.abs(pieces), axis=-1, keepdims=True) + tiny).astype(jnp.bfloat16)
    code = (pieces / scale.astype(jnp.float32)).astype(jnp.bfloat16)
    codes, scales = (
        lax.all_gather(code[None], "replica", axis=0, tiled=True),
        lax.all_gather(scale[None], "replica", axis=0, tiled=True),
    )
    outer_sum = jnp.sum(scales.astype(jnp.float32) * codes.astype(jnp.float32), axis=0)
    return (
        node_out,
        msg_rows.astype(jnp.bfloat16)[None],
        out_rows.astype(jnp.bfloat16)[None],
        outer_sum,
    )


def solution(mesh):
    placed = (
        P(("replica", "fsdp"), None),
        P(None, ("replica", "fsdp")),
        P(None, ("replica", "fsdp")),
        P("replica", "fsdp"),
        P("fsdp", None),
        P("fsdp", None),
        P(),
        P(("replica", "fsdp"), None),
        P(),
    )
    return jax.shard_map(
        shards,
        mesh=mesh,
        in_specs=placed,
        out_specs=(
            P(("replica", "fsdp"), None),
            P("replica", "fsdp", None),
            P("replica", "fsdp", None),
            P(None, "fsdp", None),
        ),
        check_vma=False,
    )
```

profile of v0, /device:TPU:0, one launch (start us, length us, event | category | flops | bytes accessed | tf_op | source)
XLA Modules:
  0.0 217.0 jit_solution(8497567208238725777)
XLA Ops:
  9.5 9.5 %psum.7 = s32[8]{0:T(128)S(1)} all-reduce(s32[8]{0:T(128)S(1)} %convert_element_type.139), channel_id=1, replica_groups=mesh['replica'=4,'fsdp'=8] {'fsdp'}, use_global_device_ids=true, to_apply=%region_3.4 | all-reduce | flops 8 | bytes 64 | tf_op jit(solution)/shard_map/psum | solution.py:99
  19.7 20.8 %all-gather.5.cloned.1.call-done = bf16[1024,1024]{1,0:T(8,128)(2,1)} async-done(((bf16[128,1024]{1,0:T(8,128)(2,1)}), bf16[1024,1024]{1,0:T(8,128)(2,1)}) %all-gather.5.cloned.1.call-update) | async-done | bytes 2097168 | tf_op jit(solution)/shard_map/all_gather | solution.py:77
  40.5 2.1 convolution_convert_fusion.1
  42.7 2.2 %collective-permute-start = (bf16[32,1024]{1,0:T(8,128)(2,1)S(1)}, bf16[32,1024]{1,0:T(8,128)(2,1)S(1)}, u32[]{:S(2)}, u32[]{:S(2)}) collective-permute-start(bf16[32,1024]{1,0:T(8,128)(2,1)S(1)} %get-tuple-element.419), channel_id=1, source_target_pairs={{0,1},{1,2},{2,3},{3,4},{4,5},{5,6},{6,7},{8,9},{9,10},{10,11},{11... | collective-permute-start | bytes 196616 | tf_op jit(solution)/shard_map/ppermute | solution.py:25
  46.3 2.6 %collective-permute-done.1 = bf16[32,1024]{1,0:T(8,128)(2,1)S(1)} collective-permute-done((bf16[32,1024]{1,0:T(8,128)(2,1)S(1)}, bf16[32,1024]{1,0:T(8,128)(2,1)S(1)}, u32[]{:S(2)}, u32[]{:S(2)}) %collective-permute-start.1) | collective-permute-done | bytes 65568 | tf_op jit(solution)/shard_map/ppermute | solution.py:27
  48.9 29.7 %while.34 = (s32[]{:T(128)}, f32[128,1024]{1,0:T(8,128)S(1)}, f32[12,128]{1,0:T(8,128)}, f32[8,1024]{1,0:T(8,128)S(1)}, s32[12,128]{1,0:T(8,128)S(1)}, /*index=5*/bf16[192,1024]{1,0:T(8,128)(2,1)S(1)}, s32[]{:T(128)}, s32[]{:T(128)}) while((s32[]{:T(128)}, f32[128,1024]{1,0:T(8,128)S(1)}, f32[12,128]{1,0:T(8,128)}, ...), condition=%wide.region_1.0_spmd.clone, body=%wide.region_0.1_spmd.clone.sunk | while | flops 13244947 | bytes 1877427 | solution.py:87
  78.7 2.1 convolution_convert_fusion
  80.9 2.5 %fusion.24 = f32[128,1024]{1,0:T(8,128)S(1)} fusion(bf16[1024,1024]{1,0:T(8,128)(2,1)} %all-gather.7.cloned.1.call-done, f32[128,1024]{1,0:T(8,128)S(1)} %get-tuple-element.338, bf16[128,1024]{1,0:T(8,128)(2,1)S(1)} %copy-done.3, f32[128]{0:T(128)S(1)} %select_reduce_fusion), kind=kOutput, calls=%fused_computation.43 | convolution fusion | flops 270008320 | bytes 3408384 | tf_op jit(solution)/shard_map/dot_general | solution.py:105
  83.4 41.1 %while.33 = (s32[]{:T(128)}, f32[192,1024]{1,0:T(8,128)S(1)}, s32[12,128]{1,0:T(8,128)S(1)}, f32[12,128]{1,0:T(8,128)}, f32[8,1024]{1,0:T(8,128)S(1)}, /*index=5*/f32[128,1024]{1,0:T(8,128)S(1)}, s32[]{:T(128)}) while((s32[]{:T(128)}, f32[192,1024]{1,0:T(8,128)S(1)}, s32[12,128]{1,0:T(8,128)S(1)}, f32[12,128]{1,0:T(8,128)}, ...), condition=%wide.region_7.8_spmd, body=%wide.region_5.7_spmd.sunk | while | flops 12981010 | bytes 2658461 | solution.py:117
  84.9 1.9 scatter_fusion
  88.3 1.9 scatter_fusion
  91.7 1.9 scatter_fusion
  95.2 1.9 scatter_fusion
  98.6 1.9 scatter_fusion
  102.0 1.9 scatter_fusion
  108.9 1.9 scatter_fusion
  112.3 1.9 scatter_fusion
  115.7 1.9 scatter_fusion
  119.1 1.9 scatter_fusion
  124.6 4.8 %collective-permute-start.2 = (bf16[32,1024]{1,0:T(8,128)(2,1)S(1)}, bf16[32,1024]{1,0:T(8,128)(2,1)S(1)}, u32[]{:S(2)}, u32[]{:S(2)}) collective-permute-start(bf16[32,1024]{1,0:T(8,128)(2,1)S(1)} %get-tuple-element.414), channel_id=1, source_target_pairs={{0,1},{1,2},{2,3},{3,4},{4,5},{5,6},{6,7},{8,9},{9,10},{10,11},{11... | collective-permute-start | bytes 196616 | tf_op jit(solution)/shard_map/ppermute | solution.py:37
  133.4 2.6 %copy.24 = bf16[1024,1024]{1,0:T(8,128)(2,1)} copy(bf16[1024,1024]{0,1:T(8,128)(2,1)S(1)} %convert_bitcast_fusion) | data formatting | bytes 4194304
  139.5 42.4 %reduce-scatter.7.cloned.1.call-done = bf16[128,1024]{1,0:T(8,128)(2,1)} async-done(((bf16[1024,1024]{1,0:T(8,128)(2,1)}), bf16[128,1024]{1,0:T(8,128)(2,1)}) %reduce-scatter.7.cloned.1.call-update) | async-done | bytes 262160 | tf_op jit(solution)/shard_map/reduce_scatter | solution.py:128
  184.8 10.8 %all-gather.1 = bf16[4,2,128]{2,1,0:T(2,128)(2,1)S(1)} all-gather(bf16[1,2,128]{2,1,0:T(2,128)(2,1)S(1)} %get-tuple-element.421), channel_id=2, replica_groups=mesh['replica'=4,'fsdp'=8] {'replica'}, dimensions={0}, use_global_device_ids=true | all-gather | bytes 2560 | tf_op jit(solution)/shard_map/all_gather | solution.py:145
  195.7 13.9 %all_gather.16 = bf16[4,2,128,128]{3,2,1,0:T(8,128)(2,1)S(1)} all-gather(bf16[1,2,128,128]{3,2,1,0:T(8,128)(2,1)S(1)} %fusion.29), channel_id=1, replica_groups=mesh['replica'=4,'fsdp'=8] {'replica'}, dimensions={0}, use_global_device_ids=true | all-gather | bytes 327680 | tf_op jit(solution)/shard_map/all_gather | solution.py:144
  (184 shorter events, 65.6 us)
Async XLA Ops:
  7.2 39.0 %copy-start.4 = (s32[1,128]{1,0:T(1,128)S(1)}, s32[1,128]{1,0:T(1,128)}, u32[]{:S(2)}) copy-start(s32[1,128]{1,0:T(1,128)} %param.20) | copy-start | bytes 1540
  7.2 41.7 %copy-start = (f32[8,1024]{1,0:T(8,128)S(1)}, f32[8,1024]{1,0:T(8,128)}, u32[]{:S(2)}) copy-start(f32[8,1024]{1,0:T(8,128)} %param.23) | copy-start | bytes 98308
  7.2 33.4 %all-gather.5.cloned.1.call-start = ((), (), s32[]{:S(2)}) async-start(), calls=%async_computation.2 | async-start | bytes 2359296 | tf_op jit(solution)/shard_map/all_gather | solution.py:77
  7.9 72.9 %all-gather.7.cloned.1.call-start = ((), (), s32[]{:S(2)}) async-start(), calls=%async_computation.3 | async-start | bytes 2359296 | tf_op jit(solution)/shard_map/all_gather | solution.py:92
  8.7 130.1 %reduce-scatter.5.cloned.1.call-start = ((), (), s32[]{:S(2)}) async-start(), calls=%async_computation.4 | async-start | bytes 2359296 | tf_op jit(solution)/shard_map/reduce_scatter | solution.py:102
  42.7 3.6 %collective-permute-start = (bf16[32,1024]{1,0:T(8,128)(2,1)S(1)}, bf16[32,1024]{1,0:T(8,128)(2,1)S(1)}, u32[]{:S(2)}, u32[]{:S(2)}) collective-permute-start(bf16[32,1024]{1,0:T(8,128)(2,1)S(1)} %get-tuple-element.419), channel_id=1, source_target_pairs={{0,1},{1,2},{2,3},{3,4},{4,5},{5,6},{6,7},{8,9},{9,10},{10,11},{11... | collective-permute-start | bytes 196616 | tf_op jit(solution)/shard_map/ppermute | solution.py:25
  44.9 4.0 %collective-permute-start.1 = (bf16[32,1024]{1,0:T(8,128)(2,1)S(1)}, bf16[32,1024]{1,0:T(8,128)(2,1)S(1)}, u32[]{:S(2)}, u32[]{:S(2)}) collective-permute-start(bf16[32,1024]{1,0:T(8,128)(2,1)S(1)} %get-tuple-element.420), channel_id=1, source_target_pairs={{1,0},{2,1},{3,2},{4,3},{5,4},{6,5},{7,6},{9,8},{10,9},{11,10},{12... | collective-permute-start | bytes 196616 | tf_op jit(solution)/shard_map/ppermute | solution.py:27
  48.9 29.8 %copy-start.3 = (bf16[128,1024]{1,0:T(8,128)(2,1)S(1)}, bf16[128,1024]{1,0:T(8,128)(2,1)}, u32[]{:S(2)}) copy-start(bf16[128,1024]{1,0:T(8,128)(2,1)} %param.24) | copy-start | bytes 786436
  80.8 101.1 %reduce-scatter.7.cloned.1.call-start = ((), (), s32[]{:S(2)}) async-start(), calls=%async_computation.5 | async-start | bytes 2359296 | tf_op jit(solution)/shard_map/reduce_scatter | solution.py:128
  124.5 8.1 %copy-start.1 = (bf16[128,1024]{1,0:T(8,128)(2,1)S(1)}, bf16[128,1024]{1,0:T(8,128)(2,1)}, u32[]{:S(2)}) copy-start(bf16[128,1024]{1,0:T(8,128)(2,1)} %param.17) | copy-start | bytes 786436
  124.6 6.1 %collective-permute-start.2 = (bf16[32,1024]{1,0:T(8,128)(2,1)S(1)}, bf16[32,1024]{1,0:T(8,128)(2,1)S(1)}, u32[]{:S(2)}, u32[]{:S(2)}) collective-permute-start(bf16[32,1024]{1,0:T(8,128)(2,1)S(1)} %get-tuple-element.414), channel_id=1, source_target_pairs={{0,1},{1,2},{2,3},{3,4},{4,5},{5,6},{6,7},{8,9},{9,10},{10,11},{11... | collective-permute-start | bytes 196616 | tf_op jit(solution)/shard_map/ppermute | solution.py:37
  129.4 3.1 %collective-permute-start.3 = (bf16[32,1024]{1,0:T(8,128)(2,1)S(1)}, bf16[32,1024]{1,0:T(8,128)(2,1)S(1)}, u32[]{:S(2)}, u32[]{:S(2)}) collective-permute-start(bf16[32,1024]{1,0:T(8,128)(2,1)S(1)} %get-tuple-element.413), channel_id=1, source_target_pairs={{1,0},{2,1},{3,2},{4,3},{5,4},{6,5},{7,6},{9,8},{10,9},{11,10},{12... | collective-permute-start | bytes 196616 | tf_op jit(solution)/shard_map/ppermute | solution.py:37
  135.9 1.6 copy-start.2
Sparse Core Ops, SparseCore 0:
  9.9 30.5 all-gather.4
  42.4 28.1 all-gather.6
  80.9 45.3 reduce-scatter.4
  136.1 45.7 reduce-scatter.6
where the time goes:
time: 218 us; the launch traced here: 217 us
  waiting for transfers between devices  69 us (32%)
  other arithmetic  45.8 us (21%)
  blocking collectives  34.2 us (16%)
  matrix products  26.5 us (12%)
  local copies, waits for them, and re-layouts  15.8 us (7%)
  between operations  14.8 us (7%)
  starting transfers between devices  9.7 us (4%)
    reduce_scatter x1, waiting for transfers between devices, shards(): lax.psum_scatter(contract_rows(node_feats, dproj).astype(jnp.bfloat16), '...  42.4 us
    scatter-add x12, other arithmetic, spread_step(): acc.at[local_src[k]].add(radial(distances[k], radial_weight) * dagg * norm)  23.1 us
    all_gather x1, waiting for transfers between devices, shards(): lax.all_gather(msg_weight, 'fsdp', axis=0, tiled=True)  20.8 us
    dot_general x24, matrix products, radial(): jnp.dot(basis, radial_weight, precision=lax.Precision.HIGHEST, preferred_...  17.8 us
    mul x24, other arithmetic, radial(): envelope = 0.5 * (jnp.cos(jnp.pi * dist_row / cutoff) + 1.0)  17.8 us
    all_gather x1, blocking collectives, shards(): lax.all_gather(code[None], 'replica', axis=0, tiled=True)  13.9 us
    all_gather x1, blocking collectives, shards(): lax.all_gather(scale[None], 'replica', axis=0, tiled=True)  10.8 us
    gather x12, local copies, waits for them, and re-layouts, gather_step(): rows = jnp.take(extended, local_src[k], axis=0).astype(jnp.float32)  10.3 us
  transfers between devices with their start and end apart: 8, of which 4 were waited for; matrix products, arithmetic and copies ran while one was open for 38% of the time, Pallas kernels for 0%

commit v1 on v0

v1 whole, which is shorter than its diff:
```python
import functools
import math

import jax
import jax.numpy as jnp
from jax import lax
from jax.experimental import pallas as pl
from jax.experimental.pallas import tpu as pltpu
from jax.sharding import PartitionSpec as P

FRAG = 128
GRAPHS = 8
LANES = 128
SLOT = 16

cutoff = 5.0
sharpness = 2.0
tiny = 1e-06

bf16 = jnp.bfloat16
f32 = jnp.float32


def rows_at(index, count):
    return pl.ds(pl.multiple_of(index * count, count), count)


def column_of(k, neighbors):
    free = SLOT - neighbors
    return (k // free) * SLOT + neighbors + k % free


def pack_kernel(n, width, weight, src, dist, ids, radial_weight, *rest):
    packed, own_radial, (blocks, radials, group) = rest[: n // 2], rest[n // 2], rest[n // 2 + 1 :]
    me = lax.axis_index("fsdp")
    rows = weight.shape[0]
    neighbors, atoms = src.shape
    if width < LANES:
        blocks[...] = jnp.zeros_like(blocks)
        radials[...] = jnp.zeros_like(radials)
    for e in range(n):
        blocks[e, :, :width] = weight[:, e * width : (e + 1) * width]
        radials[e, :, :width] = radial_weight[:, e * width : (e + 1) * width]
    own_radial[...] = radials[me]
    position = lax.broadcasted_iota(jnp.int32, src.shape, 1) + me * atoms
    group[...] = jnp.zeros_like(group)
    group[:neighbors] = (src[...] - position).astype(f32)
    group[neighbors : neighbors + 1] = ids[...].astype(f32)
    meta = [group[...].astype(bf16)]
    group[...] = jnp.ones_like(group)
    group[:neighbors] = dist[...]
    left = group[...]
    for _ in range(3):
        part = left.astype(bf16)
        meta.append(part)
        left = left - part.astype(f32)
    for c in range(n // 2):
        packed[c][:rows] = blocks[me ^ (2 * c)]
        packed[c][rows : 2 * rows] = blocks[me ^ (2 * c + 1)]
        for i, part in enumerate(meta):
            packed[c][2 * rows + i * SLOT : 2 * rows + (i + 1) * SLOT] = part


def fill_filters(neighbors, own_radial, filters, filters_low):
    basis = own_radial.shape[0]
    row = lax.broadcasted_iota(jnp.int32, (basis * SLOT, LANES), 0)
    spread = jnp.concatenate(
        [jnp.broadcast_to(own_radial[b : b + 1], (SLOT, LANES)) for b in range(basis)], axis=0
    )
    high = spread.astype(bf16).astype(f32)
    low = spread - high
    for k in range(neighbors):
        mine = row % SLOT == k
        lanes = slice(k * LANES, (k + 1) * LANES)
        part = jnp.where(mine, high, 0.0).astype(bf16)
        filters[: basis * SLOT, lanes] = part
        filters[basis * SLOT :, lanes] = part
        filters_low[:, lanes] = jnp.where(mine, low, 0.0).astype(bf16)


def filter_block(split, filters, filters_low, out):
    span = 2 * LANES
    half = split.shape[1] // 2

    def step(j, _):
        lanes = pl.ds(pl.multiple_of(j * span, span), span)
        out[:, lanes] = jnp.dot(
            split, filters[:, lanes], preferred_element_type=f32
        ) + jnp.dot(split[:, :half], filters_low[:, lanes], preferred_element_type=f32)
        return 0

    lax.fori_loop(0, out.shape[1] // span, step, 0)


def forward_kernel(n, margin, group_blocks, norm, *refs):
    m = n // 2
    feats, near, far, own_radial = refs[:n], refs[n : n + m], refs[n + m : 2 * n], refs[2 * n]
    outs = refs[2 * n + 1 :]
    sends, (weighted, slope, split, offsets) = outs[:m], outs[m : m + 4]
    (
        weights,
        dists,
        graph_weight,
        stacked,
        columns,
        projected,
        filters,
        filters_low,
        values,
        onehot,
        act,
    ) = outs[m + 4 :]
    me = lax.axis_index("fsdp")
    atoms = feats[0].shape[0]
    basis = own_radial.shape[0]
    neighbors = onehot.shape[0] // (2 * margin)
    rows = weights.shape[0] // n
    fill_filters(neighbors, own_radial, filters, filters_low)

    for d in range(n):
        e = me ^ d
        block = near[d // 2] if d % 2 == 0 else far[d // 2]
        first = (d % 2) * rows
        weights[rows_at(e, rows)] = block[first : first + rows]
        meta = block[2 * rows :].astype(f32)
        offsets[rows_at(e, SLOT)] = meta[:SLOT]
        dists[rows_at(e, SLOT)] = (
            meta[SLOT : 2 * SLOT] + meta[2 * SLOT : 3 * SLOT] + meta[3 * SLOT :]
        )
    slots = lax.broadcasted_iota(jnp.int32, offsets.shape, 0) % SLOT
    ids = jnp.where(slots == neighbors, offsets[...], -1.0)
    weight = jnp.zeros_like(ids)
    for g in range(GRAPHS):
        member = ids == float(g)
        count = jnp.sum(jnp.where(member, 1.0, 0.0), axis=(0, 1), keepdims=True)
        weight = weight + jnp.where(member, lax.rsqrt(jnp.maximum(count, 1.0)), 0.0)
    graph_weight[...] = weight

    def columns_step(e, _):
        dist = dists[rows_at(e, SLOT)]
        envelope = 0.5 * (jnp.cos(jnp.pi * dist / cutoff) + 1.0)
        for b in range(basis):
            center = cutoff * b / (basis - 1)
            stacked[b * SLOT : (b + 1) * SLOT] = (
                jnp.exp(-sharpness * (dist - center) ** 2) * envelope
            )
        offset = offsets[rows_at(e, SLOT)]
        for k in range(neighbors):
            at = column_of(k, neighbors)
            stacked[at : at + 1] = offset[k : k + 1]
        at = column_of(neighbors, neighbors)
        stacked[at : at + 1] = graph_weight[rows_at(e, SLOT)][neighbors : neighbors + 1]
        turned = stacked[...].T
        columns[rows_at(e, atoms)] = turned
        high = turned.astype(bf16)
        split[rows_at(e, atoms), : basis * SLOT] = high
        split[rows_at(e, atoms), basis * SLOT :] = (turned - high.astype(f32)).astype(bf16)
        return 0

    lax.fori_loop(0, n, columns_step, 0)

    projected[...] = jnp.zeros_like(projected)
    for d in range(n):
        e = me ^ d
        start = pl.multiple_of(e * atoms + margin, margin)
        projected[pl.ds(start, atoms)] = jnp.dot(
            feats[d][...], weights[...], preferred_element_type=f32
        ).astype(bf16)

    tile = 2 * margin
    shift = (
        lax.broadcasted_iota(jnp.int32, (tile, 2 * tile), 1)
        - lax.broadcasted_iota(jnp.int32, (tile, 2 * tile), 0)
        - margin
    ).astype(f32)
    span = group_blocks * atoms

    def group_step(group, _):
        filter_block(split[rows_at(group, span)], filters, filters_low, values)

        def tile_step(t, _):
            where = group * (span // tile) + t
            turned = columns[rows_at(where, tile)]
            for k in range(neighbors):
                at = column_of(k, neighbors)
                onehot[k * tile : (k + 1) * tile] = jnp.where(
                    turned[:, at : at + 1] == shift, 1.0, 0.0
                ).astype(bf16)
            window = projected[pl.ds(pl.multiple_of(where * tile, tile), 2 * tile)]
            gathered = jnp.dot(onehot[...], window, preferred_element_type=f32)
            total = jnp.zeros((tile, LANES), f32)
            for k in range(neighbors):
                total = total + (
                    values[rows_at(t, tile), k * LANES : (k + 1) * LANES]
                    * gathered[k * tile : (k + 1) * tile]
                )
            agg = total * norm
            sig = 1.0 / (1.0 + jnp.exp(-agg))
            active = (agg * sig).astype(bf16)
            at = column_of(neighbors, neighbors)
            graph = turned[:, at : at + 1]
            act[rows_at(where, tile)] = active
            weighted[rows_at(where, tile)] = (active.astype(f32) * graph).astype(bf16)
            slope[rows_at(where, tile)] = sig * (1.0 + agg * (1.0 - sig)) * (graph * norm)
            return 0

        lax.fori_loop(0, span // tile, tile_step, 0)
        return 0

    lax.fori_loop(0, n // group_blocks, group_step, 0)
    for c in range(m):
        sends[c][:atoms] = act[rows_at(me ^ (2 * c), atoms)]
        sends[c][atoms:] = act[rows_at(me ^ (2 * c + 1), atoms)]


def backward_kernel(n, margin, group_blocks, *refs):
    m = n // 2
    cots, feats, (out_weight, own_radial, slope, split, offsets) = (
        refs[:n],
        refs[n : 2 * n],
        refs[2 * n : 2 * n + 5],
    )
    sends = refs[2 * n + 5 : 2 * n + 5 + m]
    (rows_padded, dagg, filters, filters_low, values, terms, onehot, spread, turned, grads) = refs[
        2 * n + 5 + m :
    ]
    me = lax.axis_index("fsdp")
    atoms = feats[0].shape[0]
    neighbors = terms.shape[0] // atoms
    rows = out_weight.shape[0]
    fill_filters(neighbors, own_radial, filters, filters_low)
    if rows < LANES:
        rows_padded[...] = jnp.zeros_like(rows_padded)
    rows_padded[:rows] = out_weight[...]
    for d in range(n):
        e = me ^ d
        dact = lax.dot_general(
            cots[d][...],
            rows_padded[...],
            (((1,), (1,)), ((), ())),
            preferred_element_type=f32,
        )
        dagg[rows_at(e, atoms)] = dact * slope[rows_at(e, atoms)]
    spread[...] = jnp.zeros_like(spread)
    reach = atoms + 2 * margin
    shift = (
        lax.broadcasted_iota(jnp.int32, (reach, atoms), 0)
        - lax.broadcasted_iota(jnp.int32, (reach, atoms), 1)
        - margin
    ).astype(f32)
    span = group_blocks * atoms

    def group_step(group, _):
        filter_block(split[rows_at(group, span)], filters, filters_low, values)

        def block_step(i, _):
            e = group * group_blocks + i
            flow = dagg[rows_at(e, atoms)]
            offset = offsets[rows_at(e, SLOT)]
            for k in range(neighbors):
                lanes = slice(k * LANES, (k + 1) * LANES)
                terms[k * atoms : (k + 1) * atoms] = (
                    values[rows_at(i, atoms), lanes] * flow
                ).astype(bf16)
                onehot[:, k * atoms : (k + 1) * atoms] = jnp.where(
                    offset[k : k + 1] == shift, 1.0, 0.0
                ).astype(bf16)
            window = pl.ds(pl.multiple_of(e * atoms, atoms), reach)
            spread[window] += jnp.dot(onehot[...], terms[...], preferred_element_type=f32)
            return 0

        lax.fori_loop(0, group_blocks, block_step, 0)
        return 0

    lax.fori_loop(0, n // group_blocks, group_step, 0)

    for d in range(n):
        e = me ^ d
        start = pl.multiple_of(e * atoms + margin, margin)
        turned[:, d * atoms : (d + 1) * atoms] = spread[pl.ds(start, atoms)].T.astype(bf16)
    total = jnp.zeros((LANES, feats[0].shape[1]), f32)
    for d in range(n):
        total = total + jnp.dot(
            turned[:, d * atoms : (d + 1) * atoms], feats[d][...], preferred_element_type=f32
        )
    for q in range(total.shape[1] // LANES):
        grads[q * LANES : (q + 1) * LANES] = total[:, q * LANES : (q + 1) * LANES].T.astype(bf16)
    for c in range(m):
        sends[c][:rows] = grads[rows_at(me ^ (2 * c), rows)]
        sends[c][rows:] = grads[rows_at(me ^ (2 * c + 1), rows)]


def write_code(piece, code):
    rows = piece.shape[0]
    scale = (jnp.max(jnp.abs(piece), axis=-1, keepdims=True) + tiny).astype(bf16)
    wide = jnp.broadcast_to(scale.astype(f32), piece.shape)
    code[:rows] = (piece / wide).astype(bf16)
    if rows < LANES:
        wide = jnp.concatenate([wide, jnp.zeros((LANES - rows, LANES), f32)], axis=0)
    code[rows:] = wide.T[:SLOT].astype(bf16)


def out_grad_kernel(n, fragment, weighted, *refs):
    cots, grad, code, total = refs[:n], refs[n], refs[n + 1], refs[n + 2]
    me = lax.axis_index("fsdp")
    atoms = cots[0].shape[0]
    rows = grad.shape[1]
    for d in range(n):
        e = me ^ d
        left = weighted[rows_at(e, atoms)].astype(f32).T.astype(bf16)
        term = jnp.dot(left, cots[d][...], preferred_element_type=f32)
        total[...] = term if d == 0 else total[...] + term
    grad[0] = total[:rows].astype(bf16)
    lanes = pl.ds(pl.multiple_of(fragment[0] * FRAG, FRAG), FRAG)
    write_code(total[:rows, lanes], code)


def msg_grad_kernel(n, fragment, *refs):
    m = n // 2
    near, far, grad, code, blocks = refs[:m], refs[m:n], refs[n], refs[n + 1], refs[n + 2]
    me = lax.axis_index("fsdp")
    rows = grad.shape[1]
    width = grad.shape[2] // n
    for c in range(m):
        blocks[me ^ (2 * c)] = near[c][:rows]
        blocks[me ^ (2 * c + 1)] = far[c][rows:]
    for e in range(n):
        grad[0, :, e * width : (e + 1) * width] = blocks[e][:, :width]
    lanes = pl.ds(pl.multiple_of(fragment[0] * FRAG, FRAG), FRAG)
    write_code(grad[0, :, lanes].astype(f32), code)


def node_kernel(n, feats, *refs):
    m = n // 2
    near, far, weights, out = refs[:m], refs[m:n], refs[n : 2 * n], refs[2 * n]
    atoms = feats.shape[0]
    rows = weights[0].shape[0]
    total = feats[...].astype(f32)
    for d in range(n):
        left = near[d // 2][:atoms, :rows] if d % 2 == 0 else far[d // 2][atoms:, :rows]
        total = total + jnp.dot(left, weights[d][...], preferred_element_type=f32)
    out[...] = total.astype(bf16)


def outer_kernel(count, *refs):
    codes, out = refs[: 2 * count], refs[2 * count]
    rows = out.shape[1]
    for piece in range(2):
        total = jnp.zeros((rows, FRAG), f32)
        for r in range(count):
            code = codes[piece * count + r]
            wide = jnp.broadcast_to(code[rows:].astype(f32)[:1], (LANES, LANES)).T
            total = total + wide[:rows] * code[:rows].astype(f32)
        out[piece] = total


def run(kernel, outs, scratch, args, memory=48, scalars=0):
    whole = pl.BlockSpec(memory_space=pltpu.VMEM)
    scalar = pl.BlockSpec(memory_space=pltpu.SMEM)
    return pl.pallas_call(
        kernel,
        out_shape=[jax.ShapeDtypeStruct(shape, dtype) for shape, dtype in outs],
        in_specs=[scalar] * scalars + [whole] * (len(args) - scalars),
        out_specs=[whole] * len(outs),
        scratch_shapes=[pltpu.VMEM(shape, dtype) for shape, dtype in scratch],
        compiler_params=pltpu.CompilerParams(vmem_limit_bytes=memory << 20),
    )(*args)


def hop(value, axis, step):
    count = lax.axis_size(axis)
    return lax.ppermute(value, axis, [(i, i ^ step) for i in range(count)])


def from_chips(sends):
    near = [sends[0]] + [hop(sends[c], "fsdp", 2 * c) for c in range(1, len(sends))]
    return near, [hop(value, "fsdp", 1) for value in near]


def gathered(value, n):
    near, far = from_chips([value] * (n // 2))
    return [piece for pair in zip(near, far) for piece in pair]


def shards(
    node_feats,
    neighbor_src,
    distances,
    graph_ids,
    msg_weight,
    out_weight,
    radial_weight,
    cotangent,
    fragment,
):
    n = lax.axis_size("fsdp")
    replicas = lax.axis_size("replica")
    m = n // 2
    atoms, channels = node_feats.shape
    neighbors = neighbor_src.shape[0]
    basis = radial_weight.shape[0]
    rows = msg_weight.shape[0]
    width = channels // n
    margin = atoms // 4
    norm = 1.0 / math.sqrt(neighbors)
    group_blocks = min(n, 8)
    all_atoms = n * atoms
    lanes = neighbors * LANES
    filter_scratch = [
        ((2 * basis * SLOT, lanes), bf16),
        ((basis * SLOT, lanes), bf16),
        ((group_blocks * atoms, lanes), f32),
    ]

    feats = gathered(node_feats, n)
    *packed, own_radial = run(
        functools.partial(pack_kernel, n, width),
        [((2 * rows + 4 * SLOT, LANES), bf16)] * m + [((basis, LANES), f32)],
        [((n, rows, LANES), bf16), ((n, basis, LANES), f32), ((SLOT, LANES), f32)],
        [msg_weight, neighbor_src, distances, graph_ids, radial_weight],
    )
    near, far = from_chips(packed)
    *act_sends, weighted, slope, split, offsets = run(
        functools.partial(forward_kernel, n, margin, group_blocks, norm),
        [((2 * atoms, LANES), bf16)] * m
        + [
            ((all_atoms, LANES), bf16),
            ((all_atoms, LANES), f32),
            ((all_atoms, 2 * basis * SLOT), bf16),
            ((n * SLOT, LANES), f32),
        ],
        [
            ((channels, LANES), bf16),
            ((n * SLOT, LANES), f32),
            ((n * SLOT, LANES), f32),
            ((basis * SLOT, LANES), f32),
            ((all_atoms, basis * SLOT), f32),
            ((all_atoms + 2 * margin, LANES), bf16),
        ]
        + filter_scratch
        + [((neighbors * 2 * margin, 4 * margin), bf16), ((all_atoms, LANES), bf16)],
        [*feats, *near, *far, own_radial],
    )
    cots = gathered(cotangent, n)
    grad_sends = run(
        functools.partial(backward_kernel, n, margin, group_blocks),
        [((2 * rows, LANES), bf16)] * m,
        [((LANES, channels), bf16), ((all_atoms, LANES), f32)]
        + filter_scratch
        + [
            ((neighbors * atoms, LANES), bf16),
            ((atoms + 2 * margin, neighbors * atoms), bf16),
            ((all_atoms + 2 * margin, LANES), f32),
            ((LANES, all_atoms), bf16),
            ((channels, LANES), bf16),
        ],
        [*cots, *feats, out_weight, own_radial, slope, split, offsets],
    )
    grad_out, out_code = run(
        functools.partial(out_grad_kernel, n),
        [((1, rows, channels), bf16), ((rows + SLOT, FRAG), bf16)],
        [((LANES, channels), f32)],
        [fragment, weighted, *cots],
        scalars=1,
    )
    near, far = from_chips(grad_sends)
    grad_msg, msg_code = run(
        functools.partial(msg_grad_kernel, n),
        [((1, rows, channels), bf16), ((rows + SLOT, FRAG), bf16)],
        [((n, rows, LANES), bf16)],
        [fragment, *near, *far],
        scalars=1,
    )
    near, far = from_chips(act_sends)
    (node_out,) = run(
        functools.partial(node_kernel, n),
        [((atoms, channels), bf16)],
        [],
        [node_feats, *near, *far, *gathered(out_weight, n)],
    )
    codes = [
        piece if d == 0 else hop(piece, "replica", d)
        for piece in (msg_code, out_code)
        for d in range(replicas)
    ]
    (outer_sum,) = run(
        functools.partial(outer_kernel, replicas), [((2, rows, FRAG), f32)], [], codes
    )
    return node_out, grad_msg, grad_out, outer_sum


def solution(mesh):
    placed = (
        P(("replica", "fsdp"), None),
        P(None, ("replica", "fsdp")),
        P(None, ("replica", "fsdp")),
        P("replica", "fsdp"),
        P("fsdp", None),
        P("fsdp", None),
        P(),
        P(("replica", "fsdp"), None),
        P(),
    )
    return jax.shard_map(
        shards,
        mesh=mesh,
        in_specs=placed,
        out_specs=(
            P(("replica", "fsdp"), None),
            P("replica", "fsdp", None),
            P("replica", "fsdp", None),
            P(None, "fsdp", None),
        ),
        check_vma=False,
    )
```

time: 218 us -> 105 us (0.48)
  other arithmetic: 45.8 us -> 0 us
  blocking collectives: 34.2 us -> 0 us
  waiting for transfers between devices: 69 us -> 39.9 us
  starting transfers between devices: 9.7 us -> 36.2 us
  matrix products: 26.5 us -> 0 us
  Pallas kernels: 0 us -> 23.1 us
  between operations: 14.8 us -> 1.42 us
  local copies, waits for them, and re-layouts: 15.8 us -> 3.77 us
    reduce_scatter x2 -> x0, waiting for transfers between devices: 42.4 us -> none  [the longest x1 42.4 us: shards(): lax.psum_scatter(contract_rows(node_feats, dproj).astype(jnp.bfloat16), '...]
    ppermute x4 -> x48, waiting for transfers between devices: 4.39 us -> 39.9 us  [hop(): return lax.ppermute(value, axis, [(i, i ^ step) for i in range(count)])]
    ppermute x4 -> x48, starting transfers between devices: 9.54 us -> 36.2 us  [hop(): return lax.ppermute(value, axis, [(i, i ^ step) for i in range(count)])]
    dot_general x29 -> x0, matrix products: 26.5 us -> none  [the longest x24 17.8 us: radial(): jnp.dot(basis, radial_weight, precision=lax.Precision.HIGHEST, preferred_...]
    all_gather x2 -> x0, blocking collectives: 24.7 us -> none  [the longest x1 13.9 us: shards(): lax.all_gather(code[None], 'replica', axis=0, tiled=True)]
    pallas_call x0 -> x7, Pallas kernels: none -> 23.1 us  [run(): pl.pallas_call(kernel, out_shape=[jax.ShapeDtypeStruct(shape, dtype) for...]
    scatter-add x14 -> x0, other arithmetic: 23.1 us -> none  [the longest x12 23.1 us: spread_step(): acc.at[local_src[k]].add(radial(distances[k], radial_weight) * dagg * norm)]
    all_gather x2 -> x0, waiting for transfers between devices: 20.9 us -> none  [the longest x1 20.8 us: shards(): lax.all_gather(msg_weight, 'fsdp', axis=0, tiled=True)]
  transfers between devices with their start and end apart: 8 -> 48, of which waited for: 4 -> 14; matrix products, arithmetic and copies ran while one was open for 38% -> 0% of each run, Pallas kernels for 0% -> 21%
where the time goes in v1:
time: 105 us; the launch traced here: 104 us
  waiting for transfers between devices  39.9 us (38%)
  starting transfers between devices  36.2 us (34%)
  Pallas kernels  23.1 us (22%)
  local copies, waits for them, and re-layouts  3.77 us (4%)
  between operations  1.42 us (1%)
    ppermute x48, waiting for transfers between devices, hop(): return lax.ppermute(value, axis, [(i, i ^ step) for i in range(count)])  39.9 us
    ppermute x48, starting transfers between devices, hop(): return lax.ppermute(value, axis, [(i, i ^ step) for i in range(count)])  36.2 us
    pallas_call x7, Pallas kernels, run(): pl.pallas_call(kernel, out_shape=[jax.ShapeDtypeStruct(shape, dtype) for...  23.1 us
    unnamed x16, local copies, waits for them, and re-layouts  3.77 us
  transfers between devices with their start and end apart: 48, of which 14 were waited for; matrix products, arithmetic and copies ran while one was open for 0% of the time, Pallas kernels for 21%

profile of v1, /device:TPU:0, one launch (start us, length us, event | category | flops | bytes accessed | tf_op | source)
XLA Modules:
  0.0 104.4 jit_solution(11704952616952297118)
XLA Ops:
  0.6 3.0 %collective-permute-start.1 = (bf16[128,1024]{1,0:T(8,128)(2,1)}, bf16[128,1024]{1,0:T(8,128)(2,1)S(1)}, u32[]{:S(2)}, u32[]{:S(2)}) collective-permute-start(bf16[128,1024]{1,0:T(8,128)(2,1)} %refs_8_.3), channel_id=1, source_target_pairs={{0,2},{1,3},{2,0},{3,1},{4,6},{5,7},{6,4},{7,5},{8,10},{9,11},{10,... | collective-permute-start | bytes 786440 | tf_op jit(solution)/shard_map/ppermute | solution.py:372
  7.6 2.0 %collective-permute-start.8 = (bf16[320,128]{1,0:T(8,128)(2,1)S(1)}, bf16[320,128]{1,0:T(8,128)(2,1)S(1)}, u32[]{:S(2)}, u32[]{:S(2)}) collective-permute-start(bf16[320,128]{1,0:T(8,128)(2,1)S(1)} %get-tuple-element.27), channel_id=1, source_target_pairs={{0,4},{1,5},{2,6},{3,7},{4,0},{5,1},{6,2},{7,3},{8,12},{9,13},{10,... | collective-permute-start | bytes 245768 | tf_op jit(solution)/shard_map/ppermute | solution.py:372
  9.6 1.4 %collective-permute-start.9 = (bf16[320,128]{1,0:T(8,128)(2,1)S(1)}, bf16[320,128]{1,0:T(8,128)(2,1)S(1)}, u32[]{:S(2)}, u32[]{:S(2)}) collective-permute-start(bf16[320,128]{1,0:T(8,128)(2,1)S(1)} %get-tuple-element.28), channel_id=1, source_target_pairs={{0,6},{1,7},{2,4},{3,5},{4,2},{5,3},{6,0},{7,1},{8,14},{9,15},{10,... | collective-permute-start | bytes 245768 | tf_op jit(solution)/shard_map/ppermute | solution.py:372
  11.0 1.7 %collective-permute-done.7.refs_9_ = bf16[320,128]{1,0:T(8,128)(2,1)S(1)} collective-permute-done((bf16[320,128]{1,0:T(8,128)(2,1)S(1)}, bf16[320,128]{1,0:T(8,128)(2,1)S(1)}, u32[]{:S(2)}, u32[]{:S(2)}) %collective-permute-start.7) | collective-permute-done | bytes 81952 | tf_op jit(solution)/shard_map/ppermute | solution.py:372
  13.3 1.6 %collective-permute-done.9.refs_11_ = bf16[320,128]{1,0:T(8,128)(2,1)S(1)} collective-permute-done((bf16[320,128]{1,0:T(8,128)(2,1)S(1)}, bf16[320,128]{1,0:T(8,128)(2,1)S(1)}, u32[]{:S(2)}, u32[]{:S(2)}) %collective-permute-start.9) | collective-permute-done | bytes 81952 | tf_op jit(solution)/shard_map/ppermute | solution.py:372
  15.9 2.1 %collective-permute-start.5 = (bf16[128,1024]{1,0:T(8,128)(2,1)S(1)}, bf16[128,1024]{1,0:T(8,128)(2,1)S(1)}, u32[]{:S(2)}, u32[]{:S(2)}) collective-permute-start(bf16[128,1024]{1,0:T(8,128)(2,1)S(1)} %copy-done), channel_id=1, source_target_pairs={{0,6},{1,7},{2,4},{3,5},{4,2},{5,3},{6,0},{7,1},{8,14},{9,15},{10,... | collective-permute-start | bytes 786440 | tf_op jit(solution)/shard_map/ppermute | solution.py:372
  19.5 10.3 %collective-permute-done.3.refs_4_.refs_12_ = bf16[128,1024]{1,0:T(8,128)(2,1)S(1)} collective-permute-done((bf16[128,1024]{1,0:T(8,128)(2,1)S(1)}, bf16[128,1024]{1,0:T(8,128)(2,1)S(1)}, u32[]{:S(2)}, u32[]{:S(2)}) %collective-permute-start.3) | collective-permute-done | bytes 262176 | tf_op jit(solution)/shard_map/ppermute | solution.py:372
  29.8 1.5 %collective-permute-start.33 = (bf16[128,1024]{1,0:T(8,128)(2,1)}, bf16[128,1024]{1,0:T(8,128)(2,1)S(1)}, u32[]{:S(2)}, u32[]{:S(2)}) collective-permute-start(bf16[128,1024]{1,0:T(8,128)(2,1)} %refs_0_.5), channel_id=1, source_target_pairs={{0,6},{1,7},{2,4},{3,5},{4,2},{5,3},{6,0},{7,1},{8,14},{9,15},{10,... | collective-permute-start | bytes 786440 | tf_op jit(solution)/shard_map/ppermute | solution.py:372
  33.3 7.7 %collective-permute-done.31.refs_4_ = bf16[128,1024]{1,0:T(8,128)(2,1)S(1)} collective-permute-done((bf16[128,1024]{1,0:T(8,128)(2,1)}, bf16[128,1024]{1,0:T(8,128)(2,1)S(1)}, u32[]{:S(2)}, u32[]{:S(2)}) %collective-permute-start.31) | collective-permute-done | bytes 262176 | tf_op jit(solution)/shard_map/ppermute | solution.py:372
  41.0 1.5 %collective-permute-start.26 = (bf16[128,1024]{1,0:T(8,128)(2,1)}, bf16[128,1024]{1,0:T(8,128)(2,1)S(1)}, u32[]{:S(2)}, u32[]{:S(2)}) collective-permute-start(bf16[128,1024]{1,0:T(8,128)(2,1)} %refs_16_.1), channel_id=1, source_target_pairs={{0,6},{1,7},{2,4},{3,5},{4,2},{5,3},{6,0},{7,1},{8,14},{9,15},{10,... | collective-permute-start | bytes 786440 | tf_op jit(solution)/shard_map/ppermute | solution.py:372
  43.1 8.7 %collective-permute-done.24.refs_12_ = bf16[128,1024]{1,0:T(8,128)(2,1)S(1)} collective-permute-done((bf16[128,1024]{1,0:T(8,128)(2,1)}, bf16[128,1024]{1,0:T(8,128)(2,1)S(1)}, u32[]{:S(2)}, u32[]{:S(2)}) %collective-permute-start.24) | collective-permute-done | bytes 262176 | tf_op jit(solution)/shard_map/ppermute | solution.py:372
  53.8 11.1 %shard_map.121 = (bf16[256,128]{1,0:T(8,128)(2,1)S(1)}, bf16[256,128]{1,0:T(8,128)(2,1)S(1)}, bf16[256,128]{1,0:T(8,128)(2,1)S(1)}, bf16[256,128]{1,0:T(8,128)(2...) custom-call(bf16[128,1024]{1,0:T(8,128)(2,1)S(1)} %copy-done, ...), custom_call_target="tpu_custom_call" | custom-call | tf_op jit(solution)/shard_map/pallas_call | solution.py:360
  65.0 7.4 %shard_map.123 = (bf16[256,128]{1,0:T(8,128)(2,1)S(1)}, bf16[256,128]{1,0:T(8,128)(2,1)S(1)}, bf16[256,128]{1,0:T(8,128)(2,1)S(1)}, bf16[256,128]{1,0:T(8,128)(2,1)S(1)}) custom-call(bf16[128,1024]{1,0:T(8,128)(2,1)S(1)} %copy-done.1, bf16[128,1024]{1,0:T(8,128)(2,1)S(1)} %collective-permute-done.28.refs_1_, ...), custom_call_target="tpu_custom_call" | custom-call | tf_op jit(solution)/shard_map/pallas_call | solution.py:360
  72.4 1.6 %collective-permute-start.35 = (bf16[256,128]{1,0:T(8,128)(2,1)S(1)}, bf16[256,128]{1,0:T(8,128)(2,1)S(1)}, u32[]{:S(2)}, u32[]{:S(2)}) collective-permute-start(bf16[256,128]{1,0:T(8,128)(2,1)S(1)} %get-tuple-element.38), channel_id=1, source_target_pairs={{0,2},{1,3},{2,0},{3,1},{4,6},{5,7},{6,4},{7,5},{8,10},{9,11},{10,... | collective-permute-start | bytes 196616 | tf_op jit(solution)/shard_map/ppermute | solution.py:372
  76.0 1.5 %collective-permute-start.14 = (bf16[256,128]{1,0:T(8,128)(2,1)S(1)}, bf16[256,128]{1,0:T(8,128)(2,1)S(1)}, u32[]{:S(2)}, u32[]{:S(2)}) collective-permute-start(bf16[256,128]{1,0:T(8,128)(2,1)S(1)} %get-tuple-element.31), channel_id=1, source_target_pairs={{0,2},{1,3},{2,0},{3,1},{4,6},{5,7},{6,4},{7,5},{8,10},{9,11},{10,... | collective-permute-start | bytes 196616 | tf_op jit(solution)/shard_map/ppermute | solution.py:372
  81.1 1.4 %collective-permute-done.15.refs_2_ = bf16[256,128]{1,0:T(8,128)(2,1)S(1)} collective-permute-done((bf16[256,128]{1,0:T(8,128)(2,1)S(1)}, bf16[256,128]{1,0:T(8,128)(2,1)S(1)}, u32[]{:S(2)}, u32[]{:S(2)}) %collective-permute-start.15) | collective-permute-done | bytes 65568 | tf_op jit(solution)/shard_map/ppermute | solution.py:372
  82.5 1.6 %collective-permute-done.16.refs_3_ = bf16[256,128]{1,0:T(8,128)(2,1)S(1)} collective-permute-done((bf16[256,128]{1,0:T(8,128)(2,1)S(1)}, bf16[256,128]{1,0:T(8,128)(2,1)S(1)}, u32[]{:S(2)}, u32[]{:S(2)}) %collective-permute-start.16) | collective-permute-done | bytes 65568 | tf_op jit(solution)/shard_map/ppermute | solution.py:372
  85.3 1.5 %shard_map.125 = (bf16[1,128,1024]{2,1,0:T(8,128)(2,1)}, bf16[144,128]{1,0:T(8,128)(2,1)S(1)}) custom-call(s32[1]{0:T(128)S(6)} %copy.13.fragment, bf16[1024,128]{1,0:T(8,128)(2,1)S(1)} %get-tuple-element.42.weighted, bf16[128,1024]{1,0:T(8,128)(2,1)S(1)} %copy-done.1, bf16[128,1024]{1,0:T(8,128)(2,1)S(1)} %collective-permute-done.28.refs_1_, ...), custom_call_target="tpu_custom_call" | custom-call | tf_op jit(solution)/shard_map/pallas_call | solution.py:360
  86.8 1.6 %collective-permute-start.45 = (bf16[144,128]{1,0:T(8,128)(2,1)S(1)}, bf16[144,128]{1,0:T(8,128)(2,1)S(1)}, u32[]{:S(2)}, u32[]{:S(2)}) collective-permute-start(bf16[144,128]{1,0:T(8,128)(2,1)S(1)} %get-tuple-element.45.refs_4_), channel_id=1, source_target_pairs={{0,8},{8,0},{16,24},{24,16},{1,9},{9,1},{17,25},{25,17},{2,10},{10... | collective-permute-start | bytes 110600 | tf_op jit(solution)/shard_map/ppermute | solution.py:372
  89.2 1.6 %collective-permute-done.45.refs_5_ = bf16[144,128]{1,0:T(8,128)(2,1)S(1)} collective-permute-done((bf16[144,128]{1,0:T(8,128)(2,1)S(1)}, bf16[144,128]{1,0:T(8,128)(2,1)S(1)}, u32[]{:S(2)}, u32[]{:S(2)}) %collective-permute-start.45) | collective-permute-done | bytes 36896 | tf_op jit(solution)/shard_map/ppermute | solution.py:372
  90.8 2.6 %collective-permute-start.46 = (bf16[144,128]{1,0:T(8,128)(2,1)S(1)}, bf16[144,128]{1,0:T(8,128)(2,1)S(1)}, u32[]{:S(2)}, u32[]{:S(2)}) collective-permute-start(bf16[144,128]{1,0:T(8,128)(2,1)S(1)} %get-tuple-element.45.refs_4_), channel_id=1, source_target_pairs={{0,16},{8,24},{16,0},{24,8},{1,17},{9,25},{17,1},{25,9},{2,18},{10... | collective-permute-start | bytes 110600 | tf_op jit(solution)/shard_map/ppermute | solution.py:372
  95.0 2.7 %collective-permute-start.43 = (bf16[144,128]{1,0:T(8,128)(2,1)S(1)}, bf16[144,128]{1,0:T(8,128)(2,1)S(1)}, u32[]{:S(2)}, u32[]{:S(2)}) collective-permute-start(bf16[144,128]{1,0:T(8,128)(2,1)S(1)} %get-tuple-element.44.refs_0_), channel_id=1, source_target_pairs={{0,16},{8,24},{16,0},{24,8},{1,17},{9,25},{17,1},{25,9},{2,18},{10... | collective-permute-start | bytes 110600 | tf_op jit(solution)/shard_map/ppermute | solution.py:372
  99.1 1.4 %shard_map.122 = bf16[128,1024]{1,0:T(8,128)(2,1)} custom-call(bf16[128,1024]{1,0:T(8,128)(2,1)S(1)} %copy-done, bf16[256,128]{1,0:T(8,128)(2,1)S(1)} %get-tuple-element.30.refs_0_, bf16[256,128]{1,0:T(8,128)(2,1)S(1)} %collective-permute-done.14.refs_1_, bf16[256,128]{1,0:T(8,128)(2,1)S(1)} %collective-permute-done.15.refs_2_, ...), custom_call_target="tpu_custom_call" | custom-call | tf_op jit(solution)/shard_map/pallas_call | solution.py:360
  100.5 3.0 %collective-permute-done.44.refs_3_ = bf16[144,128]{1,0:T(8,128)(2,1)S(1)} collective-permute-done((bf16[144,128]{1,0:T(8,128)(2,1)S(1)}, bf16[144,128]{1,0:T(8,128)(2,1)S(1)}, u32[]{:S(2)}, u32[]{:S(2)}) %collective-permute-start.44) | collective-permute-done | bytes 36896 | tf_op jit(solution)/shard_map/ppermute | solution.py:372
  (95 shorter events, 22.4 us)
Async XLA Ops:
  0.6 18.0 %collective-permute-start.1 = (bf16[128,1024]{1,0:T(8,128)(2,1)}, bf16[128,1024]{1,0:T(8,128)(2,1)S(1)}, u32[]{:S(2)}, u32[]{:S(2)}) collective-permute-start(bf16[128,1024]{1,0:T(8,128)(2,1)} %refs_8_.3), channel_id=1, source_target_pairs={{0,2},{1,3},{2,0},{3,1},{4,6},{5,7},{6,4},{7,5},{8,10},{9,11},{10,... | collective-permute-start | bytes 786440 | tf_op jit(solution)/shard_map/ppermute | solution.py:372
  15.0 14.8 %collective-permute-start.3 = (bf16[128,1024]{1,0:T(8,128)(2,1)S(1)}, bf16[128,1024]{1,0:T(8,128)(2,1)S(1)}, u32[]{:S(2)}, u32[]{:S(2)}) collective-permute-start(bf16[128,1024]{1,0:T(8,128)(2,1)S(1)} %copy-done), channel_id=1, source_target_pairs={{0,4},{1,5},{2,6},{3,7},{4,0},{5,1},{6,2},{7,3},{8,12},{9,13},{10,... | collective-permute-start | bytes 786440 | tf_op jit(solution)/shard_map/ppermute | solution.py:372
  15.9 15.4 %collective-permute-start.5 = (bf16[128,1024]{1,0:T(8,128)(2,1)S(1)}, bf16[128,1024]{1,0:T(8,128)(2,1)S(1)}, u32[]{:S(2)}, u32[]{:S(2)}) collective-permute-start(bf16[128,1024]{1,0:T(8,128)(2,1)S(1)} %copy-done), channel_id=1, source_target_pairs={{0,6},{1,7},{2,4},{3,5},{4,2},{5,3},{6,0},{7,1},{8,14},{9,15},{10,... | collective-permute-start | bytes 786440 | tf_op jit(solution)/shard_map/ppermute | solution.py:372
  18.0 13.3 %collective-permute-start = (bf16[128,1024]{1,0:T(8,128)(2,1)S(1)}, bf16[128,1024]{1,0:T(8,128)(2,1)S(1)}, u32[]{:S(2)}, u32[]{:S(2)}) collective-permute-start(bf16[128,1024]{1,0:T(8,128)(2,1)S(1)} %copy-done), channel_id=1, source_target_pairs={{0,1},{1,0},{2,3},{3,2},{4,5},{5,4},{6,7},{7,6},{8,9},{9,8},{10,11... | collective-permute-start | bytes 786440 | tf_op jit(solution)/shard_map/ppermute | solution.py:372
  18.0 14.3 %collective-permute-start.29 = (bf16[128,1024]{1,0:T(8,128)(2,1)}, bf16[128,1024]{1,0:T(8,128)(2,1)S(1)}, u32[]{:S(2)}, u32[]{:S(2)}) collective-permute-start(bf16[128,1024]{1,0:T(8,128)(2,1)} %refs_0_.5), channel_id=1, source_target_pairs={{0,2},{1,3},{2,0},{3,1},{4,6},{5,7},{6,4},{7,5},{8,10},{9,11},{10,... | collective-permute-start | bytes 786440 | tf_op jit(solution)/shard_map/ppermute | solution.py:372
  18.6 22.4 %collective-permute-start.31 = (bf16[128,1024]{1,0:T(8,128)(2,1)}, bf16[128,1024]{1,0:T(8,128)(2,1)S(1)}, u32[]{:S(2)}, u32[]{:S(2)}) collective-permute-start(bf16[128,1024]{1,0:T(8,128)(2,1)} %refs_0_.5), channel_id=1, source_target_pairs={{0,4},{1,5},{2,6},{3,7},{4,0},{5,1},{6,2},{7,3},{8,12},{9,13},{10,... | collective-permute-start | bytes 786440 | tf_op jit(solution)/shard_map/ppermute | solution.py:372
  29.8 12.8 %collective-permute-start.33 = (bf16[128,1024]{1,0:T(8,128)(2,1)}, bf16[128,1024]{1,0:T(8,128)(2,1)S(1)}, u32[]{:S(2)}, u32[]{:S(2)}) collective-permute-start(bf16[128,1024]{1,0:T(8,128)(2,1)} %refs_0_.5), channel_id=1, source_target_pairs={{0,6},{1,7},{2,4},{3,5},{4,2},{5,3},{6,0},{7,1},{8,14},{9,15},{10,... | collective-permute-start | bytes 786440 | tf_op jit(solution)/shard_map/ppermute | solution.py:372
  31.3 11.2 %collective-permute-start.28 = (bf16[128,1024]{1,0:T(8,128)(2,1)}, bf16[128,1024]{1,0:T(8,128)(2,1)S(1)}, u32[]{:S(2)}, u32[]{:S(2)}) collective-permute-start(bf16[128,1024]{1,0:T(8,128)(2,1)} %refs_0_.5), channel_id=1, source_target_pairs={{0,1},{1,0},{2,3},{3,2},{4,5},{5,4},{6,7},{7,6},{8,9},{9,8},{10,11... | collective-permute-start | bytes 786440 | tf_op jit(solution)/shard_map/ppermute | solution.py:372
  31.3 11.7 %collective-permute-start.22 = (bf16[128,1024]{1,0:T(8,128)(2,1)}, bf16[128,1024]{1,0:T(8,128)(2,1)S(1)}, u32[]{:S(2)}, u32[]{:S(2)}) collective-permute-start(bf16[128,1024]{1,0:T(8,128)(2,1)} %refs_16_.1), channel_id=1, source_target_pairs={{0,2},{1,3},{2,0},{3,1},{4,6},{5,7},{6,4},{7,5},{8,10},{9,11},{10,... | collective-permute-start | bytes 786440 | tf_op jit(solution)/shard_map/ppermute | solution.py:372
  32.2 19.5 %collective-permute-start.24 = (bf16[128,1024]{1,0:T(8,128)(2,1)}, bf16[128,1024]{1,0:T(8,128)(2,1)S(1)}, u32[]{:S(2)}, u32[]{:S(2)}) collective-permute-start(bf16[128,1024]{1,0:T(8,128)(2,1)} %refs_16_.1), channel_id=1, source_target_pairs={{0,4},{1,5},{2,6},{3,7},{4,0},{5,1},{6,2},{7,3},{8,12},{9,13},{10,... | collective-permute-start | bytes 786440 | tf_op jit(solution)/shard_map/ppermute | solution.py:372
  41.0 10.8 %collective-permute-start.26 = (bf16[128,1024]{1,0:T(8,128)(2,1)}, bf16[128,1024]{1,0:T(8,128)(2,1)S(1)}, u32[]{:S(2)}, u32[]{:S(2)}) collective-permute-start(bf16[128,1024]{1,0:T(8,128)(2,1)} %refs_16_.1), channel_id=1, source_target_pairs={{0,6},{1,7},{2,4},{3,5},{4,2},{5,3},{6,0},{7,1},{8,14},{9,15},{10,... | collective-permute-start | bytes 786440 | tf_op jit(solution)/shard_map/ppermute | solution.py:372
  42.5 9.8 %collective-permute-start.2 = (bf16[128,1024]{1,0:T(8,128)(2,1)S(1)}, bf16[128,1024]{1,0:T(8,128)(2,1)S(1)}, u32[]{:S(2)}, u32[]{:S(2)}) collective-permute-start(bf16[128,1024]{1,0:T(8,128)(2,1)S(1)} %collective-permute-done.1.refs_2_.refs_10_), channel_id=1, source_target_pairs={{0,1},{1,0},{2,3},{3,2},{4,5},{5,4},{6,7},{7,6},{8,9},{9,8},{10,11... | collective-permute-start | bytes 786440 | tf_op jit(solution)/shard_map/ppermute | solution.py:372
  42.5 9.8 %collective-permute-start.4 = (bf16[128,1024]{1,0:T(8,128)(2,1)S(1)}, bf16[128,1024]{1,0:T(8,128)(2,1)S(1)}, u32[]{:S(2)}, u32[]{:S(2)}) collective-permute-start(bf16[128,1024]{1,0:T(8,128)(2,1)S(1)} %collective-permute-done.3.refs_4_.refs_12_), channel_id=1, source_target_pairs={{0,1},{1,0},{2,3},{3,2},{4,5},{5,4},{6,7},{7,6},{8,9},{9,8},{10,11... | collective-permute-start | bytes 786440 | tf_op jit(solution)/shard_map/ppermute | solution.py:372
  43.0 9.8 %collective-permute-start.6 = (bf16[128,1024]{1,0:T(8,128)(2,1)S(1)}, bf16[128,1024]{1,0:T(8,128)(2,1)S(1)}, u32[]{:S(2)}, u32[]{:S(2)}) collective-permute-start(bf16[128,1024]{1,0:T(8,128)(2,1)S(1)} %collective-permute-done.5.refs_6_.refs_14_), channel_id=1, source_target_pairs={{0,1},{1,0},{2,3},{3,2},{4,5},{5,4},{6,7},{7,6},{8,9},{9,8},{10,11... | collective-permute-start | bytes 786440 | tf_op jit(solution)/shard_map/ppermute | solution.py:372
  52.3 12.7 %collective-permute-start.34 = (bf16[128,1024]{1,0:T(8,128)(2,1)S(1)}, bf16[128,1024]{1,0:T(8,128)(2,1)S(1)}, u32[]{:S(2)}, u32[]{:S(2)}) collective-permute-start(bf16[128,1024]{1,0:T(8,128)(2,1)S(1)} %collective-permute-done.33.refs_6_), channel_id=1, source_target_pairs={{0,1},{1,0},{2,3},{3,2},{4,5},{5,4},{6,7},{7,6},{8,9},{9,8},{10,11... | collective-permute-start | bytes 786440 | tf_op jit(solution)/shard_map/ppermute | solution.py:372
  52.4 21.6 %collective-permute-start.21 = (bf16[128,1024]{1,0:T(8,128)(2,1)}, bf16[128,1024]{1,0:T(8,128)(2,1)S(1)}, u32[]{:S(2)}, u32[]{:S(2)}) collective-permute-start(bf16[128,1024]{1,0:T(8,128)(2,1)} %refs_16_.1), channel_id=1, source_target_pairs={{0,1},{1,0},{2,3},{3,2},{4,5},{5,4},{6,7},{7,6},{8,9},{9,8},{10,11... | collective-permute-start | bytes 786440 | tf_op jit(solution)/shard_map/ppermute | solution.py:372
  52.8 21.8 %collective-permute-start.23 = (bf16[128,1024]{1,0:T(8,128)(2,1)S(1)}, bf16[128,1024]{1,0:T(8,128)(2,1)S(1)}, u32[]{:S(2)}, u32[]{:S(2)}) collective-permute-start(bf16[128,1024]{1,0:T(8,128)(2,1)S(1)} %collective-permute-done.22.refs_10_), channel_id=1, source_target_pairs={{0,1},{1,0},{2,3},{3,2},{4,5},{5,4},{6,7},{7,6},{8,9},{9,8},{10,11... | collective-permute-start | bytes 786440 | tf_op jit(solution)/shard_map/ppermute | solution.py:372
  53.3 22.7 %collective-permute-start.25 = (bf16[128,1024]{1,0:T(8,128)(2,1)S(1)}, bf16[128,1024]{1,0:T(8,128)(2,1)S(1)}, u32[]{:S(2)}, u32[]{:S(2)}) collective-permute-start(bf16[128,1024]{1,0:T(8,128)(2,1)S(1)} %collective-permute-done.24.refs_12_), channel_id=1, source_target_pairs={{0,1},{1,0},{2,3},{3,2},{4,5},{5,4},{6,7},{7,6},{8,9},{9,8},{10,11... | collective-permute-start | bytes 786440 | tf_op jit(solution)/shard_map/ppermute | solution.py:372
  53.7 22.3 %collective-permute-start.27 = (bf16[128,1024]{1,0:T(8,128)(2,1)S(1)}, bf16[128,1024]{1,0:T(8,128)(2,1)S(1)}, u32[]{:S(2)}, u32[]{:S(2)}) collective-permute-start(bf16[128,1024]{1,0:T(8,128)(2,1)S(1)} %collective-permute-done.26.refs_14_), channel_id=1, source_target_pairs={{0,1},{1,0},{2,3},{3,2},{4,5},{5,4},{6,7},{7,6},{8,9},{9,8},{10,11... | collective-permute-start | bytes 786440 | tf_op jit(solution)/shard_map/ppermute | solution.py:372
  82.5 10.9 %collective-permute-start.17 = (bf16[256,128]{1,0:T(8,128)(2,1)S(1)}, bf16[256,128]{1,0:T(8,128)(2,1)S(1)}, u32[]{:S(2)}, u32[]{:S(2)}) collective-permute-start(bf16[256,128]{1,0:T(8,128)(2,1)S(1)} %get-tuple-element.30.refs_0_), channel_id=1, source_target_pairs={{0,1},{1,0},{2,3},{3,2},{4,5},{5,4},{6,7},{7,6},{8,9},{9,8},{10,11... | collective-permute-start | bytes 196616 | tf_op jit(solution)/shard_map/ppermute | solution.py:372
  84.1 10.6 %collective-permute-start.18 = (bf16[256,128]{1,0:T(8,128)(2,1)S(1)}, bf16[256,128]{1,0:T(8,128)(2,1)S(1)}, u32[]{:S(2)}, u32[]{:S(2)}) collective-permute-start(bf16[256,128]{1,0:T(8,128)(2,1)S(1)} %collective-permute-done.14.refs_1_), channel_id=1, source_target_pairs={{0,1},{1,0},{2,3},{3,2},{4,5},{5,4},{6,7},{7,6},{8,9},{9,8},{10,11... | collective-permute-start | bytes 196616 | tf_op jit(solution)/shard_map/ppermute | solution.py:372
  84.1 10.9 %collective-permute-start.19 = (bf16[256,128]{1,0:T(8,128)(2,1)S(1)}, bf16[256,128]{1,0:T(8,128)(2,1)S(1)}, u32[]{:S(2)}, u32[]{:S(2)}) collective-permute-start(bf16[256,128]{1,0:T(8,128)(2,1)S(1)} %collective-permute-done.15.refs_2_), channel_id=1, source_target_pairs={{0,1},{1,0},{2,3},{3,2},{4,5},{5,4},{6,7},{7,6},{8,9},{9,8},{10,11... | collective-permute-start | bytes 196616 | tf_op jit(solution)/shard_map/ppermute | solution.py:372
  84.6 13.1 %collective-permute-start.20 = (bf16[256,128]{1,0:T(8,128)(2,1)S(1)}, bf16[256,128]{1,0:T(8,128)(2,1)S(1)}, u32[]{:S(2)}, u32[]{:S(2)}) collective-permute-start(bf16[256,128]{1,0:T(8,128)(2,1)S(1)} %collective-permute-done.16.refs_3_), channel_id=1, source_target_pairs={{0,1},{1,0},{2,3},{3,2},{4,5},{5,4},{6,7},{7,6},{8,9},{9,8},{10,11... | collective-permute-start | bytes 196616 | tf_op jit(solution)/shard_map/ppermute | solution.py:372
  90.8 9.7 %collective-permute-start.46 = (bf16[144,128]{1,0:T(8,128)(2,1)S(1)}, bf16[144,128]{1,0:T(8,128)(2,1)S(1)}, u32[]{:S(2)}, u32[]{:S(2)}) collective-permute-start(bf16[144,128]{1,0:T(8,128)(2,1)S(1)} %get-tuple-element.45.refs_4_), channel_id=1, source_target_pairs={{0,16},{8,24},{16,0},{24,8},{1,17},{9,25},{17,1},{25,9},{2,18},{10... | collective-permute-start | bytes 110600 | tf_op jit(solution)/shard_map/ppermute | solution.py:372
  (32 other events, 152.3 us)

commit v2 on v1

v2 whole, which is shorter than its diff:
```python
import functools
import math

import jax
import jax.numpy as jnp
from jax import lax
from jax.experimental import pallas as pl
from jax.experimental.pallas import tpu as pltpu
from jax.sharding import PartitionSpec as P

FRAG = 128
GRAPHS = 8
LANES = 128
SLOT = 16

cutoff = 5.0
sharpness = 2.0
tiny = 1e-06

bf16 = jnp.bfloat16
f32 = jnp.float32


def rows_at(index, count):
    return pl.ds(pl.multiple_of(index * count, count), count)


def column_of(k, neighbors):
    free = SLOT - neighbors
    return (k // free) * SLOT + neighbors + k % free


def pack_kernel(n, width, weight, src, dist, ids, radial_weight, *rest):
    packed, own_radial, (blocks, radials, group) = rest[: n // 2], rest[n // 2], rest[n // 2 + 1 :]
    me = lax.axis_index("fsdp")
    rows = weight.shape[0]
    neighbors, atoms = src.shape
    if width < LANES:
        blocks[...] = jnp.zeros_like(blocks)
        radials[...] = jnp.zeros_like(radials)
    for e in range(n):
        blocks[e, :, :width] = weight[:, e * width : (e + 1) * width]
        radials[e, :, :width] = radial_weight[:, e * width : (e + 1) * width]
    own_radial[...] = radials[me]
    position = lax.broadcasted_iota(jnp.int32, src.shape, 1) + me * atoms
    group[...] = jnp.zeros_like(group)
    group[:neighbors] = (src[...] - position).astype(f32)
    group[neighbors : neighbors + 1] = ids[...].astype(f32)
    meta = [group[...].astype(bf16)]
    group[...] = jnp.ones_like(group)
    group[:neighbors] = dist[...]
    left = group[...]
    for _ in range(3):
        part = left.astype(bf16)
        meta.append(part)
        left = left - part.astype(f32)
    for c in range(n // 2):
        packed[c][:rows] = blocks[me ^ (2 * c)]
        packed[c][rows : 2 * rows] = blocks[me ^ (2 * c + 1)]
        for i, part in enumerate(meta):
            packed[c][2 * rows + i * SLOT : 2 * rows + (i + 1) * SLOT] = part


def fill_filters(neighbors, own_radial, filters):
    basis = own_radial.shape[0]
    half = basis * SLOT
    row = lax.broadcasted_iota(jnp.int32, (half, LANES), 0) % SLOT
    spread = jnp.concatenate(
        [jnp.broadcast_to(own_radial[b : b + 1], (SLOT, LANES)) for b in range(basis)], axis=0
    )
    high = spread.astype(bf16).astype(f32)
    low = spread - high
    for k in range(neighbors):
        lanes = slice(k * LANES, (k + 1) * LANES)
        filters[:half, lanes] = jnp.where(row == k, high, 0.0).astype(bf16)
        filters[half:, lanes] = jnp.where(row == k, low, 0.0).astype(bf16)


def fill_values(columns, filters, values):
    high = columns.astype(bf16)
    both = jnp.concatenate([high, high], axis=1)
    span = 2 * LANES

    def step(j, _):
        lanes = pl.ds(pl.multiple_of(j * span, span), span)
        values[:, lanes] = jnp.dot(both, filters[:, lanes], preferred_element_type=f32)
        return 0

    steps = values.shape[1] // span
    lax.fori_loop(0, steps, step, 0, unroll=steps)


def fill_pick(margin, neighbors, turned, pick):
    tile = 2 * margin
    tiles = turned.shape[0] // tile
    shift = (
        lax.broadcasted_iota(jnp.int32, (tile, 2 * tile), 1)
        - lax.broadcasted_iota(jnp.int32, (tile, 2 * tile), 0)
        - margin
    ).astype(f32)
    for t in range(tiles):
        own = turned[t * tile : (t + 1) * tile]
        for k in range(neighbors):
            at = column_of(k, neighbors)
            pick[k * tile : (k + 1) * tile, t * 2 * tile : (t + 1) * 2 * tile] = jnp.where(
                own[:, at : at + 1] == shift, 1.0, 0.0
            ).astype(bf16)


def fill_place(margin, neighbors, offset, place):
    atoms = offset.shape[1]
    shape = (atoms + 2 * margin, atoms)
    shift = (
        lax.broadcasted_iota(jnp.int32, shape, 0)
        - lax.broadcasted_iota(jnp.int32, shape, 1)
        - margin
    ).astype(f32)
    for k in range(neighbors):
        place[:, k * atoms : (k + 1) * atoms] = jnp.where(
            offset[k : k + 1] == shift, 1.0, 0.0
        ).astype(bf16)


def lists_kernel(n, margin, neighbors, ahead, *refs):
    m = n // 2
    near, far, own_radial = refs[:m], refs[m:n], refs[n]
    weights, columns, offsets = refs[n + 1 : n + 4]
    made = refs[n + 4 : n + 7] if ahead else ()
    dists, graph_weight, stacked, filters = refs[n + 4 + len(made) :]
    me = lax.axis_index("fsdp")
    basis = own_radial.shape[0]
    rows = weights.shape[0] // n
    atoms = columns.shape[0] // n
    for d in range(n):
        e = me ^ d
        block = near[d // 2] if d % 2 == 0 else far[d // 2]
        first = (d % 2) * rows
        weights[rows_at(e, rows)] = block[first : first + rows]
        meta = block[2 * rows :].astype(f32)
        offsets[rows_at(e, SLOT)] = meta[:SLOT]
        dists[rows_at(e, SLOT)] = (
            meta[SLOT : 2 * SLOT] + meta[2 * SLOT : 3 * SLOT] + meta[3 * SLOT :]
        )
    slots = lax.broadcasted_iota(jnp.int32, offsets.shape, 0) % SLOT
    ids = jnp.where(slots == neighbors, offsets[...], -1.0)
    weight = jnp.zeros_like(ids)
    for g in range(GRAPHS):
        member = ids == float(g)
        count = jnp.sum(jnp.where(member, 1.0, 0.0), axis=(0, 1), keepdims=True)
        weight = weight + jnp.where(member, lax.rsqrt(jnp.maximum(count, 1.0)), 0.0)
    graph_weight[...] = weight

    def columns_step(e, _):
        dist = dists[rows_at(e, SLOT)]
        envelope = 0.5 * (jnp.cos(jnp.pi * dist / cutoff) + 1.0)
        own = stacked.at[e % stacked.shape[0]]
        for b in range(basis):
            center = cutoff * b / (basis - 1)
            own[b * SLOT : (b + 1) * SLOT] = jnp.exp(-sharpness * (dist - center) ** 2) * envelope
        offset = offsets[rows_at(e, SLOT)]
        for k in range(neighbors):
            at = column_of(k, neighbors)
            own[at : at + 1] = offset[k : k + 1]
        at = column_of(neighbors, neighbors)
        own[at : at + 1] = graph_weight[rows_at(e, SLOT)][neighbors : neighbors + 1]
        columns[rows_at(e, atoms)] = own[...].T
        return 0

    lax.fori_loop(0, n, columns_step, 0, unroll=stacked.shape[0])
    if ahead:
        values, pick, place = made
        fill_filters(neighbors, own_radial, filters)
        fill_values(columns[...], filters, values)

        def block_step(e, _):
            span = neighbors * 2 * margin
            fill_pick(margin, neighbors, columns[rows_at(e, atoms)], pick.at[rows_at(e, span)])
            fill_place(
                margin,
                neighbors,
                offsets[rows_at(e, SLOT)],
                place.at[rows_at(e, atoms + 2 * margin)],
            )
            return 0

        lax.fori_loop(0, n, block_step, 0, unroll=2)


def block_diagonal(first, second):
    zero = jnp.zeros_like(first)
    return jnp.concatenate(
        [jnp.concatenate([first, zero], axis=1), jnp.concatenate([zero, second], axis=1)], axis=0
    )


def forward_kernel(n, margin, neighbors, norm, ahead, *refs):
    feats, (weights, columns, own_radial) = refs[:n], refs[n : n + 3]
    made = refs[n + 3 : n + 5] if ahead else ()
    keep, give, weighted, slope, projected = refs[n + 3 + len(made) : n + 8 + len(made)]
    scratch = refs[n + 8 + len(made) :]
    me = lax.axis_index("fsdp")
    core = me % 2
    atoms = feats[0].shape[0]
    projected[:margin] = jnp.zeros_like(projected[:margin])
    projected[n * atoms + margin :] = jnp.zeros_like(projected[:margin])
    for d in range(n):
        e = me ^ d
        start = pl.multiple_of(e * atoms + margin, margin)
        projected[pl.ds(start, atoms)] = jnp.dot(
            feats[d][...], weights[...], preferred_element_type=f32
        ).astype(bf16)
    if ahead:
        values, pick = made
    else:
        filters, values, pick = scratch
        fill_filters(neighbors, own_radial, filters)
    tile = 2 * margin
    span = neighbors * tile

    def block_step(e, _):
        turned = columns[rows_at(e, atoms)]
        if ahead:
            own_values = values.at[rows_at(e, atoms)]
            own_pick = pick[rows_at(e, span)]
        else:
            own_values = values
            fill_values(turned, filters, values)
            fill_pick(margin, neighbors, turned, pick)
            own_pick = pick[...]
        start = pl.multiple_of(e * atoms, atoms)
        windows = [projected[pl.ds(start + t * tile, 2 * tile)] for t in range(2)]
        found = jnp.dot(own_pick, block_diagonal(*windows), preferred_element_type=f32)
        halves = []
        for t in range(2):
            total = jnp.zeros((tile, LANES), f32)
            for k in range(neighbors):
                total = total + (
                    own_values[t * tile : (t + 1) * tile, k * LANES : (k + 1) * LANES]
                    * found[k * tile : (k + 1) * tile, t * LANES : (t + 1) * LANES]
                )
            halves.append(total)
        agg = jnp.concatenate(halves, axis=0) * norm
        sig = 1.0 / (1.0 + jnp.exp(-agg))
        active = (agg * sig).astype(bf16)
        at = column_of(neighbors, neighbors)
        graph = turned[:, at : at + 1]
        weighted[rows_at(e, atoms)] = (active.astype(f32) * graph).astype(bf16)
        slope[rows_at(e, atoms)] = sig * (1.0 + agg * (1.0 - sig)) * (graph * norm)

        @pl.when(e % 2 == core)
        def _():
            keep[rows_at(e // 2, atoms)] = active

        @pl.when(e % 2 != core)
        def _():
            give[rows_at(e // 2, atoms)] = active

        return 0

    lax.fori_loop(0, n, block_step, 0, unroll=min(n, 8) if ahead else 1)


def backward_kernel(n, margin, neighbors, ahead, *refs):
    m = n // 2
    cots, feats, (out_weight, own_radial, slope, columns, offsets) = (
        refs[:n],
        refs[n : 2 * n],
        refs[2 * n : 2 * n + 5],
    )
    made = refs[2 * n + 5 : 2 * n + 7] if ahead else ()
    refs = refs[2 * n + 5 + len(made) :]
    sends, (rows_padded, dagg, terms, spread, turned, grads) = refs[:m], refs[m : m + 6]
    scratch = refs[m + 6 :]
    me = lax.axis_index("fsdp")
    atoms = feats[0].shape[0]
    rows = out_weight.shape[0]
    if rows < LANES:
        rows_padded[...] = jnp.zeros_like(rows_padded)
    rows_padded[:rows] = out_weight[...]
    for d in range(n):
        e = me ^ d
        dact = lax.dot_general(
            cots[d][...],
            rows_padded[...],
            (((1,), (1,)), ((), ())),
            preferred_element_type=f32,
        )
        dagg[rows_at(e, atoms)] = dact * slope[rows_at(e, atoms)]
    spread[...] = jnp.zeros_like(spread)
    reach = atoms + 2 * margin
    if ahead:
        values, place = made
    else:
        filters, values, place = scratch
        fill_filters(neighbors, own_radial, filters)

    def block_step(e, _):
        flow = dagg[rows_at(e, atoms)]
        if ahead:
            own_values = values.at[rows_at(e, atoms)]
            own_place = place[rows_at(e, reach)]
        else:
            own_values = values
            fill_values(columns[rows_at(e, atoms)], filters, values)
            fill_place(margin, neighbors, offsets[rows_at(e, SLOT)], place)
            own_place = place[...]
        own = terms.at[e % terms.shape[0]]
        for k in range(neighbors):
            own[k * atoms : (k + 1) * atoms] = (
                own_values[:, k * LANES : (k + 1) * LANES] * flow
            ).astype(bf16)
        window = pl.ds(pl.multiple_of(e * atoms, atoms), reach)
        spread[window] += jnp.dot(own_place, own[...], preferred_element_type=f32)
        return 0

    lax.fori_loop(0, n, block_step, 0, unroll=min(n, 8) if ahead else 1)

    for d in range(n):
        e = me ^ d
        start = pl.multiple_of(e * atoms + margin, margin)
        turned[:, d * atoms : (d + 1) * atoms] = spread[pl.ds(start, atoms)].T.astype(bf16)
    total = jnp.zeros((LANES, feats[0].shape[1]), f32)
    for d in range(n):
        total = total + jnp.dot(
            turned[:, d * atoms : (d + 1) * atoms], feats[d][...], preferred_element_type=f32
        )
    for q in range(total.shape[1] // LANES):
        grads[q * LANES : (q + 1) * LANES] = total[:, q * LANES : (q + 1) * LANES].T.astype(bf16)
    for c in range(m):
        sends[c][:rows] = grads[rows_at(me ^ (2 * c), rows)]
        sends[c][rows:] = grads[rows_at(me ^ (2 * c + 1), rows)]


def write_code(piece, code):
    rows = piece.shape[0]
    scale = (jnp.max(jnp.abs(piece), axis=-1, keepdims=True) + tiny).astype(bf16)
    wide = jnp.broadcast_to(scale.astype(f32), piece.shape)
    code[:rows] = (piece / wide).astype(bf16)
    if rows < LANES:
        wide = jnp.concatenate([wide, jnp.zeros((LANES - rows, LANES), f32)], axis=0)
    code[rows:] = wide.T[:SLOT].astype(bf16)


def out_grad_kernel(n, fragment, weighted, *refs):
    cots, grad, code, total = refs[:n], refs[n], refs[n + 1], refs[n + 2]
    me = lax.axis_index("fsdp")
    atoms = cots[0].shape[0]
    rows = grad.shape[1]
    for d in range(n):
        e = me ^ d
        left = weighted[rows_at(e, atoms)].astype(f32).T.astype(bf16)
        term = jnp.dot(left, cots[d][...], preferred_element_type=f32)
        total[...] = term if d == 0 else total[...] + term
    grad[0] = total[:rows].astype(bf16)
    lanes = pl.ds(pl.multiple_of(fragment[0] * FRAG, FRAG), FRAG)
    write_code(total[:rows, lanes], code)


def msg_grad_kernel(n, fragment, *refs):
    m = n // 2
    near, far, grad, code, blocks = refs[:m], refs[m:n], refs[n], refs[n + 1], refs[n + 2]
    me = lax.axis_index("fsdp")
    rows = grad.shape[1]
    width = grad.shape[2] // n
    for c in range(m):
        blocks[me ^ (2 * c)] = near[c][:rows]
        blocks[me ^ (2 * c + 1)] = far[c][rows:]
    for e in range(n):
        grad[0, :, e * width : (e + 1) * width] = blocks[e][:, :width]
    lanes = pl.ds(pl.multiple_of(fragment[0] * FRAG, FRAG), FRAG)
    write_code(grad[0, :, lanes].astype(f32), code)


def partial_kernel(n, width, keep, got, own_weight, other_weight, *sends):
    me = lax.axis_index("fsdp")
    atoms = keep.shape[0] // (n // 2)
    for c in range(n // 2):
        block = rows_at((me // 2) ^ c, atoms)
        sends[c][...] = (
            jnp.dot(keep[block][:, :width], own_weight[...], preferred_element_type=f32)
            + jnp.dot(got[block][:, :width], other_weight[...], preferred_element_type=f32)
        ).astype(bf16)


def node_kernel(feats, *refs):
    parts, out = refs[:-1], refs[-1]
    total = feats[...].astype(f32)
    for part in parts:
        total = total + part[...].astype(f32)
    out[...] = total.astype(bf16)


def outer_kernel(count, *refs):
    codes, out = refs[: 2 * count], refs[2 * count]
    rows = out.shape[1]
    for piece in range(2):
        total = jnp.zeros((rows, FRAG), f32)
        for r in range(count):
            code = codes[piece * count + r]
            wide = jnp.broadcast_to(code[rows:].astype(f32)[:1], (LANES, LANES)).T
            total = total + wide[:rows] * code[:rows].astype(f32)
        out[piece] = total


def run(kernel, outs, scratch, args, micros, memory=16, scalars=0):
    whole = pl.BlockSpec(memory_space=pltpu.VMEM)
    scalar = pl.BlockSpec(memory_space=pltpu.SMEM)
    return pl.pallas_call(
        kernel,
        out_shape=[jax.ShapeDtypeStruct(shape, dtype) for shape, dtype in outs],
        in_specs=[scalar] * scalars + [whole] * (len(args) - scalars),
        out_specs=[whole] * len(outs),
        scratch_shapes=[pltpu.VMEM(shape, dtype) for shape, dtype in scratch],
        compiler_params=pltpu.CompilerParams(vmem_limit_bytes=memory << 20),
        cost_estimate=pl.CostEstimate(
            flops=int(micros * 1e9), bytes_accessed=int(micros * 3e6), transcendentals=0
        ),
    )(*args)


def hop(value, axis, step):
    count = lax.axis_size(axis)
    return lax.ppermute(value, axis, [(i, i ^ step) for i in range(count)])


def from_chips(sends):
    near = [sends[0]] + [hop(sends[c], "fsdp", 2 * c) for c in range(1, len(sends))]
    return near, [hop(value, "fsdp", 1) for value in near]


def gathered(value, n):
    near, far = from_chips([value] * (n // 2))
    return [piece for pair in zip(near, far) for piece in pair]


def shards(
    node_feats,
    neighbor_src,
    distances,
    graph_ids,
    msg_weight,
    out_weight,
    radial_weight,
    cotangent,
    fragment,
):
    n = lax.axis_size("fsdp")
    replicas = lax.axis_size("replica")
    m = n // 2
    atoms, channels = node_feats.shape
    neighbors = neighbor_src.shape[0]
    basis = radial_weight.shape[0]
    rows = msg_weight.shape[0]
    width = channels // n
    margin = atoms // 4
    reach = atoms + 2 * margin
    norm = 1.0 / math.sqrt(neighbors)
    all_atoms = n * atoms
    lanes = neighbors * LANES
    ahead = all_atoms * lanes * 4 <= 8 << 20
    memory = 24 if ahead else 56
    step_scratch = [
        ((2 * basis * SLOT, lanes), bf16),
        ((atoms, lanes), f32),
    ]

    feats = gathered(node_feats, n)
    *packed, own_radial = run(
        functools.partial(pack_kernel, n, width),
        [((2 * rows + 4 * SLOT, LANES), bf16)] * m + [((basis, LANES), f32)],
        [((n, rows, LANES), bf16), ((n, basis, LANES), f32), ((SLOT, LANES), f32)],
        [msg_weight, neighbor_src, distances, graph_ids, radial_weight],
        1,
    )
    near, far = from_chips(packed)
    weights, columns, offsets, *made = run(
        functools.partial(lists_kernel, n, margin, neighbors, ahead),
        [
            ((channels, LANES), bf16),
            ((all_atoms, LANES), f32),
            ((n * SLOT, LANES), f32),
        ]
        + [
            ((all_atoms, lanes), f32),
            ((n * neighbors * 2 * margin, 8 * margin), bf16),
            ((n * reach, neighbors * atoms), bf16),
        ]
        * ahead,
        [
            ((n * SLOT, LANES), f32),
            ((n * SLOT, LANES), f32),
            ((min(n, 8), basis * SLOT, LANES), f32),
            ((2 * basis * SLOT, lanes), bf16),
        ],
        [*near, *far, own_radial],
        6,
        memory,
    )
    keep, give, weighted, slope = run(
        functools.partial(forward_kernel, n, margin, neighbors, norm, ahead),
        [
            ((all_atoms // 2, LANES), bf16),
            ((all_atoms // 2, LANES), bf16),
            ((all_atoms, LANES), bf16),
            ((all_atoms, LANES), f32),
        ],
        [((all_atoms + 2 * margin, LANES), bf16)]
        + (step_scratch + [((neighbors * 2 * margin, 8 * margin), bf16)]) * (not ahead),
        [*feats, weights, columns, own_radial, *made[:2]],
        4,
        memory,
    )
    cots = gathered(cotangent, n)
    grad_sends = run(
        functools.partial(backward_kernel, n, margin, neighbors, ahead),
        [((2 * rows, LANES), bf16)] * m,
        [
            ((LANES, channels), bf16),
            ((all_atoms, LANES), f32),
            ((min(n, 8) if ahead else 1, neighbors * atoms, LANES), bf16),
            ((all_atoms + 2 * margin, LANES), f32),
            ((LANES, all_atoms), bf16),
            ((channels, LANES), bf16),
        ]
        + (step_scratch + [((reach, neighbors * atoms), bf16)]) * (not ahead),
        [*cots, *feats, out_weight, own_radial, slope, columns, offsets, *made[::2]],
        4,
        memory,
    )
    grad_out, out_code = run(
        functools.partial(out_grad_kernel, n),
        [((1, rows, channels), bf16), ((rows + SLOT, FRAG), bf16)],
        [((LANES, channels), f32)],
        [fragment, weighted, *cots],
        1,
        memory,
        scalars=1,
    )
    near, far = from_chips(grad_sends)
    grad_msg, msg_code = run(
        functools.partial(msg_grad_kernel, n),
        [((1, rows, channels), bf16), ((rows + SLOT, FRAG), bf16)],
        [((n, rows, LANES), bf16)],
        [fragment, *near, *far],
        1,
        memory,
        scalars=1,
    )
    sums = run(
        functools.partial(partial_kernel, n, width),
        [((atoms, channels), bf16)] * m,
        [],
        [keep, hop(give, "fsdp", 1), out_weight, hop(out_weight, "fsdp", 1)],
        1,
        memory,
    )
    (node_out,) = run(
        node_kernel,
        [((atoms, channels), bf16)],
        [],
        [node_feats, sums[0]] + [hop(sums[c], "fsdp", 2 * c) for c in range(1, m)],
        1,
        memory,
    )
    codes = [
        piece if d == 0 else hop(piece, "replica", d)
        for piece in (msg_code, out_code)
        for d in range(replicas)
    ]
    (outer_sum,) = run(
        functools.partial(outer_kernel, replicas), [((2, rows, FRAG), f32)], [], codes, 1, memory
    )
    return node_out, grad_msg, grad_out, outer_sum


def solution(mesh):
    placed = (
        P(("replica", "fsdp"), None),
        P(None, ("replica", "fsdp")),
        P(None, ("replica", "fsdp")),
        P("replica", "fsdp"),
        P("fsdp", None),
        P("fsdp", None),
        P(),
        P(("replica", "fsdp"), None),
        P(),
    )
    return jax.shard_map(
        shards,
        mesh=mesh,
        in_specs=placed,
        out_specs=(
            P(("replica", "fsdp"), None),
            P("replica", "fsdp", None),
            P("replica", "fsdp", None),
            P(None, "fsdp", None),
        ),
        check_vma=False,
    )
```

time: 105 us -> 81.9 us (0.78)
  waiting for transfers between devices: 39.9 us -> 30.2 us
  starting transfers between devices: 36.2 us -> 29.4 us
  Pallas kernels: 23.1 us -> 16.8 us
    ppermute x48 -> x39, waiting for transfers between devices: 39.9 us -> 30.2 us  [hop(): return lax.ppermute(value, axis, [(i, i ^ step) for i in range(count)])]
    ppermute x48 -> x39, starting transfers between devices: 36.2 us -> 29.4 us  [hop(): return lax.ppermute(value, axis, [(i, i ^ step) for i in range(count)])]
    pallas_call x7 -> x9, Pallas kernels: 23.1 us -> 16.8 us  [run(): pl.pallas_call(kernel, out_shape=[jax.ShapeDtypeStruct(shape, dtype) for...]
  transfers between devices with their start and end apart: 48 -> 39, of which waited for: 14 -> 13; matrix products, arithmetic and copies ran while one was open for 0% -> 0% of each run, Pallas kernels for 21% -> 19%
where the time goes in v2:
time: 81.9 us; the launch traced here: 81.6 us
  waiting for transfers between devices  30.2 us (37%)
  starting transfers between devices  29.4 us (36%)
  Pallas kernels  16.8 us (21%)
  local copies, waits for them, and re-layouts  3.76 us (5%)
  between operations  1.41 us (2%)
    ppermute x39, waiting for transfers between devices, hop(): return lax.ppermute(value, axis, [(i, i ^ step) for i in range(count)])  30.2 us
    ppermute x39, starting transfers between devices, hop(): return lax.ppermute(value, axis, [(i, i ^ step) for i in range(count)])  29.4 us
    pallas_call x9, Pallas kernels, run(): pl.pallas_call(kernel, out_shape=[jax.ShapeDtypeStruct(shape, dtype) for...  16.8 us
    unnamed x16, local copies, waits for them, and re-layouts  3.76 us
  transfers between devices with their start and end apart: 39, of which 13 were waited for; matrix products, arithmetic and copies ran while one was open for 0% of the time, Pallas kernels for 19%

profile of v2, /device:TPU:0, one launch (start us, length us, event | category | flops | bytes accessed | tf_op | source)
XLA Modules:
  0.0 81.6 jit_solution(16664919833218345195)
XLA Ops:
  4.5 3.0 %collective-permute-start.7 = (bf16[320,128]{1,0:T(8,128)(2,1)S(1)}, bf16[320,128]{1,0:T(8,128)(2,1)S(1)}, u32[]{:S(2)}, u32[]{:S(2)}) collective-permute-start(bf16[320,128]{1,0:T(8,128)(2,1)S(1)} %get-tuple-element.32), channel_id=1, source_target_pairs={{0,2},{1,3},{2,0},{3,1},{4,6},{5,7},{6,4},{7,5},{8,10},{9,11},{10,... | collective-permute-start | bytes 245768 | tf_op jit(solution)/shard_map/ppermute | solution.py:423
  7.5 1.5 %collective-permute-start.8 = (bf16[320,128]{1,0:T(8,128)(2,1)S(1)}, bf16[320,128]{1,0:T(8,128)(2,1)S(1)}, u32[]{:S(2)}, u32[]{:S(2)}) collective-permute-start(bf16[320,128]{1,0:T(8,128)(2,1)S(1)} %get-tuple-element.33), channel_id=1, source_target_pairs={{0,4},{1,5},{2,6},{3,7},{4,0},{5,1},{6,2},{7,3},{8,12},{9,13},{10,... | collective-permute-start | bytes 245768 | tf_op jit(solution)/shard_map/ppermute | solution.py:423
  10.2 2.6 %collective-permute-done.8.refs_2_ = bf16[320,128]{1,0:T(8,128)(2,1)S(1)} collective-permute-done((bf16[320,128]{1,0:T(8,128)(2,1)S(1)}, bf16[320,128]{1,0:T(8,128)(2,1)S(1)}, u32[]{:S(2)}, u32[]{:S(2)}) %collective-permute-start.8) | collective-permute-done | bytes 81952 | tf_op jit(solution)/shard_map/ppermute | solution.py:423
  12.8 1.5 %collective-permute-done.9.refs_3_ = bf16[320,128]{1,0:T(8,128)(2,1)S(1)} collective-permute-done((bf16[320,128]{1,0:T(8,128)(2,1)S(1)}, bf16[320,128]{1,0:T(8,128)(2,1)S(1)}, u32[]{:S(2)}, u32[]{:S(2)}) %collective-permute-start.9) | collective-permute-done | bytes 81952 | tf_op jit(solution)/shard_map/ppermute | solution.py:423
  16.0 1.8 %collective-permute-start.5 = (bf16[128,1024]{1,0:T(8,128)(2,1)}, bf16[128,1024]{1,0:T(8,128)(2,1)S(1)}, u32[]{:S(2)}, u32[]{:S(2)}) collective-permute-start(bf16[128,1024]{1,0:T(8,128)(2,1)} %refs_8_.1), channel_id=1, source_target_pairs={{0,6},{1,7},{2,4},{3,5},{4,2},{5,3},{6,0},{7,1},{8,14},{9,15},{10,... | collective-permute-start | bytes 786440 | tf_op jit(solution)/shard_map/ppermute | solution.py:423
  18.5 5.2 %collective-permute-done.1.refs_2_.refs_10_ = bf16[128,1024]{1,0:T(8,128)(2,1)S(1)} collective-permute-done((bf16[128,1024]{1,0:T(8,128)(2,1)}, bf16[128,1024]{1,0:T(8,128)(2,1)S(1)}, u32[]{:S(2)}, u32[]{:S(2)}) %collective-permute-start.1) | collective-permute-done | bytes 262176 | tf_op jit(solution)/shard_map/ppermute | solution.py:423
  24.2 4.9 %collective-permute-done.3.refs_4_.refs_12_ = bf16[128,1024]{1,0:T(8,128)(2,1)S(1)} collective-permute-done((bf16[128,1024]{1,0:T(8,128)(2,1)}, bf16[128,1024]{1,0:T(8,128)(2,1)S(1)}, u32[]{:S(2)}, u32[]{:S(2)}) %collective-permute-start.3) | collective-permute-done | bytes 262176 | tf_op jit(solution)/shard_map/ppermute | solution.py:423
  29.1 1.7 %collective-permute-start.24 = (bf16[128,1024]{1,0:T(8,128)(2,1)}, bf16[128,1024]{1,0:T(8,128)(2,1)S(1)}, u32[]{:S(2)}, u32[]{:S(2)}) collective-permute-start(bf16[128,1024]{1,0:T(8,128)(2,1)} %refs_0_.5), channel_id=1, source_target_pairs={{0,6},{1,7},{2,4},{3,5},{4,2},{5,3},{6,0},{7,1},{8,14},{9,15},{10,... | collective-permute-start | bytes 786440 | tf_op jit(solution)/shard_map/ppermute | solution.py:423
  31.3 3.6 %collective-permute-done.20.refs_2_ = bf16[128,1024]{1,0:T(8,128)(2,1)S(1)} collective-permute-done((bf16[128,1024]{1,0:T(8,128)(2,1)}, bf16[128,1024]{1,0:T(8,128)(2,1)S(1)}, u32[]{:S(2)}, u32[]{:S(2)}) %collective-permute-start.20) | collective-permute-done | bytes 262176 | tf_op jit(solution)/shard_map/ppermute | solution.py:423
  34.9 4.8 %shard_map.121 = (bf16[1024,128]{1,0:T(8,128)(2,1)S(1)}, f32[1024,128]{1,0:T(8,128)S(1)}, f32[128,128]{1,0:T(8,128)S(1)}, f32[1024,1536]{1,0:T(8,128)S(1)}, bf16...) custom-call(bf16[320,128]{1,0:T(8,128)(2,1)S(1)} %get-tuple-element.31.refs_0_, ...), custom_call_target="tpu_custom_call" | custom-call | flops 6000000000 | bytes 18000000 | tf_op jit(solution)/shard_map/pallas_call | solution.py:408
  41.5 4.0 %shard_map.122 = (bf16[512,128]{1,0:T(8,128)(2,1)S(1)}, bf16[512,128]{1,0:T(8,128)(2,1)S(1)}, bf16[1024,128]{1,0:T(8,128)(2,1)S(1)}, f32[1024,128]{1,0:T(8,128)S(1)}) custom-call(bf16[128,1024]{1,0:T(8,128)(2,1)S(1)} %copy-done.2, bf16[128,1024]{1,0:T(8,128)(2,1)S(1)} %collective-permute-done.refs_1_.refs_9_, ...), custom_call_target="tpu_custom_call" | custom-call | flops 4000000000 | bytes 12000000 | tf_op jit(solution)/shard_map/pallas_call | solution.py:408
  46.1 3.2 %shard_map.125 = (bf16[256,128]{1,0:T(8,128)(2,1)S(1)}, bf16[256,128]{1,0:T(8,128)(2,1)S(1)}, bf16[256,128]{1,0:T(8,128)(2,1)S(1)}, bf16[256,128]{1,0:T(8,128)(2,1)S(1)}) custom-call(bf16[128,1024]{1,0:T(8,128)(2,1)S(1)} %copy-done.1, bf16[128,1024]{1,0:T(8,128)(2,1)S(1)} %collective-permute-done.19.refs_1_, ...), custom_call_target="tpu_custom_call" | custom-call | flops 4000000000 | bytes 12000000 | tf_op jit(solution)/shard_map/pallas_call | solution.py:408
  49.3 1.6 %collective-permute-start.26 = (bf16[256,128]{1,0:T(8,128)(2,1)S(1)}, bf16[256,128]{1,0:T(8,128)(2,1)S(1)}, u32[]{:S(2)}, u32[]{:S(2)}) collective-permute-start(bf16[256,128]{1,0:T(8,128)(2,1)S(1)} %get-tuple-element.50), channel_id=1, source_target_pairs={{0,2},{1,3},{2,0},{3,1},{4,6},{5,7},{6,4},{7,5},{8,10},{9,11},{10,... | collective-permute-start | bytes 196616 | tf_op jit(solution)/shard_map/ppermute | solution.py:423
  51.4 1.4 %collective-permute-start.28 = (bf16[256,128]{1,0:T(8,128)(2,1)S(1)}, bf16[256,128]{1,0:T(8,128)(2,1)S(1)}, u32[]{:S(2)}, u32[]{:S(2)}) collective-permute-start(bf16[256,128]{1,0:T(8,128)(2,1)S(1)} %get-tuple-element.52), channel_id=1, source_target_pairs={{0,6},{1,7},{2,4},{3,5},{4,2},{5,3},{6,0},{7,1},{8,14},{9,15},{10,... | collective-permute-start | bytes 196616 | tf_op jit(solution)/shard_map/ppermute | solution.py:423
  54.1 1.7 %collective-permute-done.27.refs_2_ = bf16[256,128]{1,0:T(8,128)(2,1)S(1)} collective-permute-done((bf16[256,128]{1,0:T(8,128)(2,1)S(1)}, bf16[256,128]{1,0:T(8,128)(2,1)S(1)}, u32[]{:S(2)}, u32[]{:S(2)}) %collective-permute-start.27) | collective-permute-done | bytes 65568 | tf_op jit(solution)/shard_map/ppermute | solution.py:423
  59.3 1.5 %collective-permute-start.18 = (bf16[128,1024]{1,0:T(8,128)(2,1)S(1)}, bf16[128,1024]{1,0:T(8,128)(2,1)S(1)}, u32[]{:S(2)}, u32[]{:S(2)}) collective-permute-start(bf16[128,1024]{1,0:T(8,128)(2,1)S(1)} %get-tuple-element.45), channel_id=1, source_target_pairs={{0,6},{1,7},{2,4},{3,5},{4,2},{5,3},{6,0},{7,1},{8,14},{9,15},{10,... | collective-permute-start | bytes 786440 | tf_op jit(solution)/shard_map/ppermute | solution.py:423
  60.9 1.5 %shard_map.127 = (bf16[1,128,1024]{2,1,0:T(8,128)(2,1)}, bf16[144,128]{1,0:T(8,128)(2,1)S(1)}) custom-call(s32[1]{0:T(128)S(6)} %copy.13.fragment, bf16[1024,128]{1,0:T(8,128)(2,1)S(1)} %get-tuple-element.54.weighted, bf16[128,1024]{1,0:T(8,128)(2,1)S(1)} %copy-done.1, bf16[128,1024]{1,0:T(8,128)(2,1)S(1)} %collective-permute-done.19.refs_1_, ...), custom_call_target="tpu_custom_call" | custom-call | flops 1000000000 | bytes 3000000 | tf_op jit(solution)/shard_map/pallas_call | solution.py:408
  62.3 1.6 %collective-permute-start.36 = (bf16[144,128]{1,0:T(8,128)(2,1)S(1)}, bf16[144,128]{1,0:T(8,128)(2,1)S(1)}, u32[]{:S(2)}, u32[]{:S(2)}) collective-permute-start(bf16[144,128]{1,0:T(8,128)(2,1)S(1)} %get-tuple-element.57.refs_4_), channel_id=1, source_target_pairs={{0,8},{8,0},{16,24},{24,16},{1,9},{9,1},{17,25},{25,17},{2,10},{10... | collective-permute-start | bytes 110600 | tf_op jit(solution)/shard_map/ppermute | solution.py:423
  63.9 2.6 %collective-permute-start.37 = (bf16[144,128]{1,0:T(8,128)(2,1)S(1)}, bf16[144,128]{1,0:T(8,128)(2,1)S(1)}, u32[]{:S(2)}, u32[]{:S(2)}) collective-permute-start(bf16[144,128]{1,0:T(8,128)(2,1)S(1)} %get-tuple-element.57.refs_4_), channel_id=1, source_target_pairs={{0,16},{8,24},{16,0},{24,8},{1,17},{9,25},{17,1},{25,9},{2,18},{10... | collective-permute-start | bytes 110600 | tf_op jit(solution)/shard_map/ppermute | solution.py:423
  67.3 2.8 %collective-permute-start.38 = (bf16[144,128]{1,0:T(8,128)(2,1)S(1)}, bf16[144,128]{1,0:T(8,128)(2,1)S(1)}, u32[]{:S(2)}, u32[]{:S(2)}) collective-permute-start(bf16[144,128]{1,0:T(8,128)(2,1)S(1)} %get-tuple-element.57.refs_4_), channel_id=1, source_target_pairs={{0,24},{8,16},{16,8},{24,0},{1,25},{9,17},{17,9},{25,1},{2,26},{10... | collective-permute-start | bytes 110600 | tf_op jit(solution)/shard_map/ppermute | solution.py:423
  70.1 3.0 %collective-permute-done.38.refs_7_ = bf16[144,128]{1,0:T(8,128)(2,1)S(1)} collective-permute-done((bf16[144,128]{1,0:T(8,128)(2,1)S(1)}, bf16[144,128]{1,0:T(8,128)(2,1)S(1)}, u32[]{:S(2)}, u32[]{:S(2)}) %collective-permute-start.38) | collective-permute-done | bytes 36896 | tf_op jit(solution)/shard_map/ppermute | solution.py:423
  74.0 1.8 %collective-permute-start.35 = (bf16[144,128]{1,0:T(8,128)(2,1)S(1)}, bf16[144,128]{1,0:T(8,128)(2,1)S(1)}, u32[]{:S(2)}, u32[]{:S(2)}) collective-permute-start(bf16[144,128]{1,0:T(8,128)(2,1)S(1)} %get-tuple-element.56.refs_0_), channel_id=1, source_target_pairs={{0,24},{8,16},{16,8},{24,0},{1,25},{9,17},{17,9},{25,1},{2,26},{10... | collective-permute-start | bytes 110600 | tf_op jit(solution)/shard_map/ppermute | solution.py:423
  75.8 2.3 %collective-permute-done.34.refs_2_ = bf16[144,128]{1,0:T(8,128)(2,1)S(1)} collective-permute-done((bf16[144,128]{1,0:T(8,128)(2,1)S(1)}, bf16[144,128]{1,0:T(8,128)(2,1)S(1)}, u32[]{:S(2)}, u32[]{:S(2)}) %collective-permute-start.34) | collective-permute-done | bytes 36896 | tf_op jit(solution)/shard_map/ppermute | solution.py:423
  78.1 1.7 %collective-permute-done.35.refs_3_ = bf16[144,128]{1,0:T(8,128)(2,1)S(1)} collective-permute-done((bf16[144,128]{1,0:T(8,128)(2,1)S(1)}, bf16[144,128]{1,0:T(8,128)(2,1)S(1)}, u32[]{:S(2)}, u32[]{:S(2)}) %collective-permute-start.35) | collective-permute-done | bytes 36896 | tf_op jit(solution)/shard_map/ppermute | solution.py:423
  (79 shorter events, 18.9 us)
Async XLA Ops:
  4.5 5.7 %collective-permute-start.7 = (bf16[320,128]{1,0:T(8,128)(2,1)S(1)}, bf16[320,128]{1,0:T(8,128)(2,1)S(1)}, u32[]{:S(2)}, u32[]{:S(2)}) collective-permute-start(bf16[320,128]{1,0:T(8,128)(2,1)S(1)} %get-tuple-element.32), channel_id=1, source_target_pairs={{0,2},{1,3},{2,0},{3,1},{4,6},{5,7},{6,4},{7,5},{8,10},{9,11},{10,... | collective-permute-start | bytes 245768 | tf_op jit(solution)/shard_map/ppermute | solution.py:423
  9.0 5.9 %collective-permute-start.10 = (bf16[320,128]{1,0:T(8,128)(2,1)S(1)}, bf16[320,128]{1,0:T(8,128)(2,1)S(1)}, u32[]{:S(2)}, u32[]{:S(2)}) collective-permute-start(bf16[320,128]{1,0:T(8,128)(2,1)S(1)} %get-tuple-element.31.refs_0_), channel_id=1, source_target_pairs={{0,1},{1,0},{2,3},{3,2},{4,5},{5,4},{6,7},{7,6},{8,9},{9,8},{10,11... | collective-permute-start | bytes 245768 | tf_op jit(solution)/shard_map/ppermute | solution.py:423
  10.2 5.8 %collective-permute-start.11 = (bf16[320,128]{1,0:T(8,128)(2,1)S(1)}, bf16[320,128]{1,0:T(8,128)(2,1)S(1)}, u32[]{:S(2)}, u32[]{:S(2)}) collective-permute-start(bf16[320,128]{1,0:T(8,128)(2,1)S(1)} %collective-permute-done.7.refs_1_), channel_id=1, source_target_pairs={{0,1},{1,0},{2,3},{3,2},{4,5},{5,4},{6,7},{7,6},{8,9},{9,8},{10,11... | collective-permute-start | bytes 245768 | tf_op jit(solution)/shard_map/ppermute | solution.py:423
  14.3 9.3 %collective-permute-start.1 = (bf16[128,1024]{1,0:T(8,128)(2,1)}, bf16[128,1024]{1,0:T(8,128)(2,1)S(1)}, u32[]{:S(2)}, u32[]{:S(2)}) collective-permute-start(bf16[128,1024]{1,0:T(8,128)(2,1)} %refs_8_.1), channel_id=1, source_target_pairs={{0,2},{1,3},{2,0},{3,1},{4,6},{5,7},{6,4},{7,5},{8,10},{9,11},{10,... | collective-permute-start | bytes 786440 | tf_op jit(solution)/shard_map/ppermute | solution.py:423
  14.9 14.3 %collective-permute-start.3 = (bf16[128,1024]{1,0:T(8,128)(2,1)}, bf16[128,1024]{1,0:T(8,128)(2,1)S(1)}, u32[]{:S(2)}, u32[]{:S(2)}) collective-permute-start(bf16[128,1024]{1,0:T(8,128)(2,1)} %refs_8_.1), channel_id=1, source_target_pairs={{0,4},{1,5},{2,6},{3,7},{4,0},{5,1},{6,2},{7,3},{8,12},{9,13},{10,... | collective-permute-start | bytes 786440 | tf_op jit(solution)/shard_map/ppermute | solution.py:423
  16.0 14.8 %collective-permute-start.5 = (bf16[128,1024]{1,0:T(8,128)(2,1)}, bf16[128,1024]{1,0:T(8,128)(2,1)S(1)}, u32[]{:S(2)}, u32[]{:S(2)}) collective-permute-start(bf16[128,1024]{1,0:T(8,128)(2,1)} %refs_8_.1), channel_id=1, source_target_pairs={{0,6},{1,7},{2,4},{3,5},{4,2},{5,3},{6,0},{7,1},{8,14},{9,15},{10,... | collective-permute-start | bytes 786440 | tf_op jit(solution)/shard_map/ppermute | solution.py:423
  17.8 13.0 %collective-permute-start = (bf16[128,1024]{1,0:T(8,128)(2,1)}, bf16[128,1024]{1,0:T(8,128)(2,1)S(1)}, u32[]{:S(2)}, u32[]{:S(2)}) collective-permute-start(bf16[128,1024]{1,0:T(8,128)(2,1)} %refs_8_.1), channel_id=1, source_target_pairs={{0,1},{1,0},{2,3},{3,2},{4,5},{5,4},{6,7},{7,6},{8,9},{9,8},{10,11... | collective-permute-start | bytes 786440 | tf_op jit(solution)/shard_map/ppermute | solution.py:423
  17.9 17.1 %collective-permute-start.20 = (bf16[128,1024]{1,0:T(8,128)(2,1)}, bf16[128,1024]{1,0:T(8,128)(2,1)S(1)}, u32[]{:S(2)}, u32[]{:S(2)}) collective-permute-start(bf16[128,1024]{1,0:T(8,128)(2,1)} %refs_0_.5), channel_id=1, source_target_pairs={{0,2},{1,3},{2,0},{3,1},{4,6},{5,7},{6,4},{7,5},{8,10},{9,11},{10,... | collective-permute-start | bytes 786440 | tf_op jit(solution)/shard_map/ppermute | solution.py:423
  23.7 16.7 %collective-permute-start.22 = (bf16[128,1024]{1,0:T(8,128)(2,1)}, bf16[128,1024]{1,0:T(8,128)(2,1)S(1)}, u32[]{:S(2)}, u32[]{:S(2)}) collective-permute-start(bf16[128,1024]{1,0:T(8,128)(2,1)} %refs_0_.5), channel_id=1, source_target_pairs={{0,4},{1,5},{2,6},{3,7},{4,0},{5,1},{6,2},{7,3},{8,12},{9,13},{10,... | collective-permute-start | bytes 786440 | tf_op jit(solution)/shard_map/ppermute | solution.py:423
  29.1 11.3 %collective-permute-start.24 = (bf16[128,1024]{1,0:T(8,128)(2,1)}, bf16[128,1024]{1,0:T(8,128)(2,1)S(1)}, u32[]{:S(2)}, u32[]{:S(2)}) collective-permute-start(bf16[128,1024]{1,0:T(8,128)(2,1)} %refs_0_.5), channel_id=1, source_target_pairs={{0,6},{1,7},{2,4},{3,5},{4,2},{5,3},{6,0},{7,1},{8,14},{9,15},{10,... | collective-permute-start | bytes 786440 | tf_op jit(solution)/shard_map/ppermute | solution.py:423
  30.8 10.1 %collective-permute-start.2 = (bf16[128,1024]{1,0:T(8,128)(2,1)S(1)}, bf16[128,1024]{1,0:T(8,128)(2,1)S(1)}, u32[]{:S(2)}, u32[]{:S(2)}) collective-permute-start(bf16[128,1024]{1,0:T(8,128)(2,1)S(1)} %collective-permute-done.1.refs_2_.refs_10_), channel_id=1, source_target_pairs={{0,1},{1,0},{2,3},{3,2},{4,5},{5,4},{6,7},{7,6},{8,9},{9,8},{10,11... | collective-permute-start | bytes 786440 | tf_op jit(solution)/shard_map/ppermute | solution.py:423
  30.8 10.2 %collective-permute-start.4 = (bf16[128,1024]{1,0:T(8,128)(2,1)S(1)}, bf16[128,1024]{1,0:T(8,128)(2,1)S(1)}, u32[]{:S(2)}, u32[]{:S(2)}) collective-permute-start(bf16[128,1024]{1,0:T(8,128)(2,1)S(1)} %collective-permute-done.3.refs_4_.refs_12_), channel_id=1, source_target_pairs={{0,1},{1,0},{2,3},{3,2},{4,5},{5,4},{6,7},{7,6},{8,9},{9,8},{10,11... | collective-permute-start | bytes 786440 | tf_op jit(solution)/shard_map/ppermute | solution.py:423
  34.9 6.5 %collective-permute-start.6 = (bf16[128,1024]{1,0:T(8,128)(2,1)S(1)}, bf16[128,1024]{1,0:T(8,128)(2,1)S(1)}, u32[]{:S(2)}, u32[]{:S(2)}) collective-permute-start(bf16[128,1024]{1,0:T(8,128)(2,1)S(1)} %collective-permute-done.5.refs_6_.refs_14_), channel_id=1, source_target_pairs={{0,1},{1,0},{2,3},{3,2},{4,5},{5,4},{6,7},{7,6},{8,9},{9,8},{10,11... | collective-permute-start | bytes 786440 | tf_op jit(solution)/shard_map/ppermute | solution.py:423
  40.4 13.1 %collective-permute-start.15 = (bf16[128,1024]{1,0:T(8,128)(2,1)S(1)}, bf16[128,1024]{1,0:T(8,128)(2,1)S(1)}, u32[]{:S(2)}, u32[]{:S(2)}) collective-permute-start(bf16[128,1024]{1,0:T(8,128)(2,1)S(1)} %copy-done), channel_id=1, source_target_pairs={{0,1},{1,0},{2,3},{3,2},{4,5},{5,4},{6,7},{7,6},{8,9},{9,8},{10,11... | collective-permute-start | bytes 786440 | tf_op jit(solution)/shard_map/ppermute | solution.py:423
  45.6 11.0 %collective-permute-start.14 = (bf16[512,128]{1,0:T(8,128)(2,1)S(1)}, bf16[512,128]{1,0:T(8,128)(2,1)S(1)}, u32[]{:S(2)}, u32[]{:S(2)}) collective-permute-start(bf16[512,128]{1,0:T(8,128)(2,1)S(1)} %get-tuple-element.41), channel_id=1, source_target_pairs={{0,1},{1,0},{2,3},{3,2},{4,5},{5,4},{6,7},{7,6},{8,9},{9,8},{10,11... | collective-permute-start | bytes 393224 | tf_op jit(solution)/shard_map/ppermute | solution.py:423
  53.6 5.7 %collective-permute-start.30 = (bf16[256,128]{1,0:T(8,128)(2,1)S(1)}, bf16[256,128]{1,0:T(8,128)(2,1)S(1)}, u32[]{:S(2)}, u32[]{:S(2)}) collective-permute-start(bf16[256,128]{1,0:T(8,128)(2,1)S(1)} %collective-permute-done.26.refs_1_), channel_id=1, source_target_pairs={{0,1},{1,0},{2,3},{3,2},{4,5},{5,4},{6,7},{7,6},{8,9},{9,8},{10,11... | collective-permute-start | bytes 196616 | tf_op jit(solution)/shard_map/ppermute | solution.py:423
  55.8 6.5 %collective-permute-start.31 = (bf16[256,128]{1,0:T(8,128)(2,1)S(1)}, bf16[256,128]{1,0:T(8,128)(2,1)S(1)}, u32[]{:S(2)}, u32[]{:S(2)}) collective-permute-start(bf16[256,128]{1,0:T(8,128)(2,1)S(1)} %collective-permute-done.27.refs_2_), channel_id=1, source_target_pairs={{0,1},{1,0},{2,3},{3,2},{4,5},{5,4},{6,7},{7,6},{8,9},{9,8},{10,11... | collective-permute-start | bytes 196616 | tf_op jit(solution)/shard_map/ppermute | solution.py:423
  56.6 7.3 %collective-permute-start.32 = (bf16[256,128]{1,0:T(8,128)(2,1)S(1)}, bf16[256,128]{1,0:T(8,128)(2,1)S(1)}, u32[]{:S(2)}, u32[]{:S(2)}) collective-permute-start(bf16[256,128]{1,0:T(8,128)(2,1)S(1)} %collective-permute-done.28.refs_3_), channel_id=1, source_target_pairs={{0,1},{1,0},{2,3},{3,2},{4,5},{5,4},{6,7},{7,6},{8,9},{9,8},{10,11... | collective-permute-start | bytes 196616 | tf_op jit(solution)/shard_map/ppermute | solution.py:423
  57.3 23.4 %collective-permute-start.16 = (bf16[128,1024]{1,0:T(8,128)(2,1)S(1)}, bf16[128,1024]{1,0:T(8,128)(2,1)S(1)}, u32[]{:S(2)}, u32[]{:S(2)}) collective-permute-start(bf16[128,1024]{1,0:T(8,128)(2,1)S(1)} %get-tuple-element.43), channel_id=1, source_target_pairs={{0,2},{1,3},{2,0},{3,1},{4,6},{5,7},{6,4},{7,5},{8,10},{9,11},{10,... | collective-permute-start | bytes 786440 | tf_op jit(solution)/shard_map/ppermute | solution.py:423
  58.1 22.6 %collective-permute-start.17 = (bf16[128,1024]{1,0:T(8,128)(2,1)S(1)}, bf16[128,1024]{1,0:T(8,128)(2,1)S(1)}, u32[]{:S(2)}, u32[]{:S(2)}) collective-permute-start(bf16[128,1024]{1,0:T(8,128)(2,1)S(1)} %get-tuple-element.44), channel_id=1, source_target_pairs={{0,4},{1,5},{2,6},{3,7},{4,0},{5,1},{6,2},{7,3},{8,12},{9,13},{10,... | collective-permute-start | bytes 786440 | tf_op jit(solution)/shard_map/ppermute | solution.py:423
  59.3 21.3 %collective-permute-start.18 = (bf16[128,1024]{1,0:T(8,128)(2,1)S(1)}, bf16[128,1024]{1,0:T(8,128)(2,1)S(1)}, u32[]{:S(2)}, u32[]{:S(2)}) collective-permute-start(bf16[128,1024]{1,0:T(8,128)(2,1)S(1)} %get-tuple-element.45), channel_id=1, source_target_pairs={{0,6},{1,7},{2,4},{3,5},{4,2},{5,3},{6,0},{7,1},{8,14},{9,15},{10,... | collective-permute-start | bytes 786440 | tf_op jit(solution)/shard_map/ppermute | solution.py:423
  63.9 6.2 %collective-permute-start.37 = (bf16[144,128]{1,0:T(8,128)(2,1)S(1)}, bf16[144,128]{1,0:T(8,128)(2,1)S(1)}, u32[]{:S(2)}, u32[]{:S(2)}) collective-permute-start(bf16[144,128]{1,0:T(8,128)(2,1)S(1)} %get-tuple-element.57.refs_4_), channel_id=1, source_target_pairs={{0,16},{8,24},{16,0},{24,8},{1,17},{9,25},{17,1},{25,9},{2,18},{10... | collective-permute-start | bytes 110600 | tf_op jit(solution)/shard_map/ppermute | solution.py:423
  67.3 5.8 %collective-permute-start.38 = (bf16[144,128]{1,0:T(8,128)(2,1)S(1)}, bf16[144,128]{1,0:T(8,128)(2,1)S(1)}, u32[]{:S(2)}, u32[]{:S(2)}) collective-permute-start(bf16[144,128]{1,0:T(8,128)(2,1)S(1)} %get-tuple-element.57.refs_4_), channel_id=1, source_target_pairs={{0,24},{8,16},{16,8},{24,0},{1,25},{9,17},{17,9},{25,1},{2,26},{10... | collective-permute-start | bytes 110600 | tf_op jit(solution)/shard_map/ppermute | solution.py:423
  74.0 5.8 %collective-permute-start.35 = (bf16[144,128]{1,0:T(8,128)(2,1)S(1)}, bf16[144,128]{1,0:T(8,128)(2,1)S(1)}, u32[]{:S(2)}, u32[]{:S(2)}) collective-permute-start(bf16[144,128]{1,0:T(8,128)(2,1)S(1)} %get-tuple-element.56.refs_0_), channel_id=1, source_target_pairs={{0,24},{8,16},{16,8},{24,0},{1,25},{9,17},{17,9},{25,1},{2,26},{10... | collective-permute-start | bytes 110600 | tf_op jit(solution)/shard_map/ppermute | solution.py:423
  (23 other events, 93.6 us)

commit v3 on v2

--- a/solution.py
+++ b/solution.py
@@ -30,8 +30,16 @@
     return (k // free) * SLOT + neighbors + k % free
 
 
-def pack_kernel(n, width, weight, src, dist, ids, radial_weight, *rest):
-    packed, own_radial, (blocks, radials, group) = rest[: n // 2], rest[n // 2], rest[n // 2 + 1 :]
+def pack_kernel(n, width, *refs):
+    far, refs = refs[:5], refs[5:]
+    packed, own_radial, (blocks, radials, group) = refs[: n // 2], refs[n // 2], refs[n // 2 + 1 : n // 2 + 4]
+    held, done = refs[n // 2 + 4 : n // 2 + 9], refs[n // 2 + 9]
+    copies = [pltpu.make_async_copy(a, b, done.at[i]) for i, (a, b) in enumerate(zip(far, held))]
+    for copy in copies:
+        copy.start()
+    for copy in copies:
+        copy.wait()
+    weight, src, dist, ids, radial_weight = held
     me = lax.axis_index("fsdp")
     rows = weight.shape[0]
     neighbors, atoms = src.shape
@@ -61,6 +69,17 @@
             packed[c][2 * rows + i * SLOT : 2 * rows + (i + 1) * SLOT] = part
 
 
+def merge_kernel(m, *refs):
+    parts, out = refs[:m], refs[-1]
+    rows = parts[0].shape[0]
+    for c, part in enumerate(parts):
+        out[c * rows : (c + 1) * rows] = part[...]
+
+
+def gate_kernel(_value, _after, _out):
+    pass
+
+
 def fill_filters(neighbors, own_radial, filters):
     basis = own_radial.shape[0]
     half = basis * SLOT
@@ -123,19 +142,22 @@
 
 def lists_kernel(n, margin, neighbors, ahead, *refs):
     m = n // 2
-    near, far, own_radial = refs[:m], refs[m:n], refs[n]
-    weights, columns, offsets = refs[n + 1 : n + 4]
-    made = refs[n + 4 : n + 7] if ahead else ()
-    dists, graph_weight, stacked, filters = refs[n + 4 + len(made) :]
+    near, far, own_radial = refs[:m], refs[m], refs[m + 1]
+    weights, columns, offsets = refs[m + 2 : m + 5]
+    made = refs[m + 5 : m + 8] if ahead else ()
+    dists, graph_weight, stacked, filters = refs[m + 5 + len(made) :]
     me = lax.axis_index("fsdp")
     basis = own_radial.shape[0]
     rows = weights.shape[0] // n
     atoms = columns.shape[0] // n
     for d in range(n):
         e = me ^ d
-        block = near[d // 2] if d % 2 == 0 else far[d // 2]
-        first = (d % 2) * rows
-        weights[rows_at(e, rows)] = block[first : first + rows]
+        head = 2 * rows + 4 * SLOT
+        block = near[d // 2] if d % 2 == 0 else far.at[d // 2 * head : (d // 2 + 1) * head]
+        weights[rows_at(e, rows), d % 2 * LANES : (d % 2 + 1) * LANES] = block[:rows]
+        weights[rows_at(e, rows), (1 - d % 2) * LANES : (2 - d % 2) * LANES] = block[
+            rows : 2 * rows
+        ]
         meta = block[2 * rows :].astype(f32)
         offsets[rows_at(e, SLOT)] = meta[:SLOT]
         dists[rows_at(e, SLOT)] = (
@@ -193,22 +215,49 @@
     )
 
 
+def products_kernel(n, weights, own_weight, other_weight, *refs):
+    m = n // 2
+    feats, cots, (keep, give, held_feats, both) = refs[:m], refs[m : 2 * m], refs[2 * m :]
+    me = lax.axis_index("fsdp")
+    atoms = feats[0].shape[0]
+    half = m * atoms
+    rows = own_weight.shape[0]
+    if rows < LANES:
+        both[...] = jnp.zeros_like(both)
+    both[:rows] = own_weight[...]
+    both[LANES : LANES + rows] = other_weight[...]
+    for c in range(m):
+        held_feats[c * atoms : (c + 1) * atoms] = feats[c][...]
+        projected = jnp.dot(
+            feats[c][...], weights[...], preferred_element_type=f32
+        ).astype(bf16)
+        dact = lax.dot_general(
+            cots[c][...], both[...], (((1,), (1,)), ((), ())), preferred_element_type=f32
+        ).astype(bf16)
+        chip = (me // 2) ^ c
+        keep[rows_at(chip, atoms)] = projected[:, :LANES]
+        give[rows_at(chip, atoms)] = projected[:, LANES:]
+        keep[rows_at(chip + m, atoms)] = dact[:, :LANES]
+        give[rows_at(chip + m, atoms)] = dact[:, LANES:]
+
+
 def forward_kernel(n, margin, neighbors, norm, ahead, *refs):
-    feats, (weights, columns, own_radial) = refs[:n], refs[n : n + 3]
-    made = refs[n + 3 : n + 5] if ahead else ()
-    keep, give, weighted, slope, projected = refs[n + 3 + len(made) : n + 8 + len(made)]
-    scratch = refs[n + 8 + len(made) :]
+    own, got, columns, own_radial = refs[:4]
+    made = refs[4:6] if ahead else ()
+    keep, give, dagg, projected = refs[4 + len(made) : 8 + len(made)]
+    scratch = refs[8 + len(made) :]
     me = lax.axis_index("fsdp")
     core = me % 2
-    atoms = feats[0].shape[0]
+    atoms = columns.shape[0] // n
+    half = n // 2 * atoms
     projected[:margin] = jnp.zeros_like(projected[:margin])
     projected[n * atoms + margin :] = jnp.zeros_like(projected[:margin])
-    for d in range(n):
-        e = me ^ d
-        start = pl.multiple_of(e * atoms + margin, margin)
-        projected[pl.ds(start, atoms)] = jnp.dot(
-            feats[d][...], weights[...], preferred_element_type=f32
-        ).astype(bf16)
+    for c in range(n // 2):
+        for source, parity in ((own, core), (got, 1 - core)):
+            start = pl.multiple_of((2 * c + parity) * atoms + margin, margin)
+            projected[pl.ds(start, atoms)] = source[c * atoms : (c + 1) * atoms]
+            dact = source[half + c * atoms : half + (c + 1) * atoms]
+            dagg[rows_at(2 * c + parity, atoms)] = dact.astype(f32)
     if ahead:
         values, pick = made
     else:
@@ -244,8 +293,8 @@
         active = (agg * sig).astype(bf16)
         at = column_of(neighbors, neighbors)
         graph = turned[:, at : at + 1]
-        weighted[rows_at(e, atoms)] = (active.astype(f32) * graph).astype(bf16)
-        slope[rows_at(e, atoms)] = sig * (1.0 + agg * (1.0 - sig)) * (graph * norm)
+        slope = sig * (1.0 + agg * (1.0 - sig)) * (graph * norm)
+        dagg[rows_at(e, atoms)] = dagg[rows_at(e, atoms)] * slope
 
         @pl.when(e % 2 == core)
         def _():
@@ -260,32 +309,16 @@
     lax.fori_loop(0, n, block_step, 0, unroll=min(n, 8) if ahead else 1)
 
 
-def backward_kernel(n, margin, neighbors, ahead, *refs):
+def backward_kernel(n, margin, neighbors, channels, ahead, *refs):
     m = n // 2
-    cots, feats, (out_weight, own_radial, slope, columns, offsets) = (
-        refs[:n],
-        refs[n : 2 * n],
-        refs[2 * n : 2 * n + 5],
-    )
-    made = refs[2 * n + 5 : 2 * n + 7] if ahead else ()
-    refs = refs[2 * n + 5 + len(made) :]
-    sends, (rows_padded, dagg, terms, spread, turned, grads) = refs[:m], refs[m : m + 6]
-    scratch = refs[m + 6 :]
+    feats, (dagg, own_radial, columns, offsets) = refs[:2], refs[2:6]
+    made = refs[6:8] if ahead else ()
+    refs = refs[6 + len(made) :]
+    sends, (terms, spread, turned, grads) = refs[:m], refs[m : m + 4]
+    scratch = refs[m + 4 :]
     me = lax.axis_index("fsdp")
-    atoms = feats[0].shape[0]
-    rows = out_weight.shape[0]
-    if rows < LANES:
-        rows_padded[...] = jnp.zeros_like(rows_padded)
-    rows_padded[:rows] = out_weight[...]
-    for d in range(n):
-        e = me ^ d
-        dact = lax.dot_general(
-            cots[d][...],
-            rows_padded[...],
-            (((1,), (1,)), ((), ())),
-            preferred_element_type=f32,
-        )
-        dagg[rows_at(e, atoms)] = dact * slope[rows_at(e, atoms)]
+    atoms = columns.shape[0] // n
+    rows = channels // n
     spread[...] = jnp.zeros_like(spread)
     reach = atoms + 2 * margin
     if ahead:
@@ -315,15 +348,16 @@
 
     lax.fori_loop(0, n, block_step, 0, unroll=min(n, 8) if ahead else 1)
 
-    for d in range(n):
-        e = me ^ d
-        start = pl.multiple_of(e * atoms + margin, margin)
-        turned[:, d * atoms : (d + 1) * atoms] = spread[pl.ds(start, atoms)].T.astype(bf16)
-    total = jnp.zeros((LANES, feats[0].shape[1]), f32)
-    for d in range(n):
-        total = total + jnp.dot(
-            turned[:, d * atoms : (d + 1) * atoms], feats[d][...], preferred_element_type=f32
-        )
+    half = m * atoms
+    for k in range(2):
+        for c in range(m):
+            e = me ^ (2 * c + k)
+            start = pl.multiple_of(e * atoms + margin, margin)
+            turned[:, k * half + c * atoms : k * half + (c + 1) * atoms] = (
+                spread[pl.ds(start, atoms)].T.astype(bf16)
+            )
+    total = jnp.dot(turned[:, :half], feats[0][...], preferred_element_type=f32)
+    total = total + jnp.dot(turned[:, half:], feats[1][...], preferred_element_type=f32)
     for q in range(total.shape[1] // LANES):
         grads[q * LANES : (q + 1) * LANES] = total[:, q * LANES : (q + 1) * LANES].T.astype(bf16)
     for c in range(m):
@@ -341,45 +375,47 @@
     code[rows:] = wide.T[:SLOT].astype(bf16)
 
 
-def out_grad_kernel(n, fragment, weighted, *refs):
-    cots, grad, code, total = refs[:n], refs[n], refs[n + 1], refs[n + 2]
+def chip_kernel(n, margin, neighbors, width, *refs):
+    m = n // 2
+    columns, keep, got, own_weight, other_weight, _after = refs[:6]
+    cots, sends, (own, give) = refs[6 : 6 + m], refs[6 + m : 6 + 2 * m], refs[6 + 2 * m :]
     me = lax.axis_index("fsdp")
     atoms = cots[0].shape[0]
-    rows = grad.shape[1]
-    for d in range(n):
-        e = me ^ d
-        left = weighted[rows_at(e, atoms)].astype(f32).T.astype(bf16)
-        term = jnp.dot(left, cots[d][...], preferred_element_type=f32)
-        total[...] = term if d == 0 else total[...] + term
-    grad[0] = total[:rows].astype(bf16)
-    lanes = pl.ds(pl.multiple_of(fragment[0] * FRAG, FRAG), FRAG)
-    write_code(total[:rows, lanes], code)
-
-
-def msg_grad_kernel(n, fragment, *refs):
-    m = n // 2
-    near, far, grad, code, blocks = refs[:m], refs[m:n], refs[n], refs[n + 1], refs[n + 2]
-    me = lax.axis_index("fsdp")
-    rows = grad.shape[1]
-    width = grad.shape[2] // n
+    rows = give.shape[0]
+    at = column_of(neighbors, neighbors)
+    totals = [None, None]
     for c in range(m):
-        blocks[me ^ (2 * c)] = near[c][:rows]
-        blocks[me ^ (2 * c + 1)] = far[c][rows:]
-    for e in range(n):
-        grad[0, :, e * width : (e + 1) * width] = blocks[e][:, :width]
-    lanes = pl.ds(pl.multiple_of(fragment[0] * FRAG, FRAG), FRAG)
-    write_code(grad[0, :, lanes].astype(f32), code)
-
-
-def partial_kernel(n, width, keep, got, own_weight, other_weight, *sends):
-    me = lax.axis_index("fsdp")
-    atoms = keep.shape[0] // (n // 2)
-    for c in range(n // 2):
         block = rows_at((me // 2) ^ c, atoms)
         sends[c][...] = (
             jnp.dot(keep[block][:, :width], own_weight[...], preferred_element_type=f32)
             + jnp.dot(got[block][:, :width], other_weight[...], preferred_element_type=f32)
         ).astype(bf16)
+        graph = columns[rows_at(me ^ (2 * c), atoms)][:, at : at + 1]
+        for i, act in enumerate((keep, got)):
+            left = (act[block].astype(f32) * graph).T.astype(bf16)
+            term = jnp.dot(left, cots[c][...], preferred_element_type=f32)
+            totals[i] = term if c == 0 else totals[i] + term
+    own[...] = totals[0][:rows]
+    give[...] = totals[1][:rows].astype(bf16)
+
+
+def grads_kernel(n, fragment, *refs):
+    m = n // 2
+    near, far, own_part, got_part = refs[:m], refs[m:n], refs[n], refs[n + 1]
+    msg_grad, out_grad, code, blocks, total = refs[n + 2 :]
+    me = lax.axis_index("fsdp")
+    rows = msg_grad.shape[1]
+    width = msg_grad.shape[2] // n
+    lanes = pl.ds(pl.multiple_of(fragment[0] * FRAG, FRAG), FRAG)
+    for c in range(m):
+        blocks[me ^ (2 * c)] = near[c][:rows]
+        blocks[me ^ (2 * c + 1)] = far[c][rows:]
+    for e in range(n):
+        msg_grad[0, :, e * width : (e + 1) * width] = blocks[e][:, :width]
+    write_code(msg_grad[0, :, lanes].astype(f32), code.at[: rows + SLOT])
+    total[...] = own_part[...] + got_part[...].astype(f32)
+    out_grad[0] = total[...].astype(bf16)
+    write_code(total[:, lanes], code.at[rows + SLOT :])
 
 
 def node_kernel(feats, *refs):
@@ -390,27 +426,37 @@
     out[...] = total.astype(bf16)
 
 
-def outer_kernel(count, *refs):
-    codes, out = refs[: 2 * count], refs[2 * count]
+def pair_kernel(*refs):
+    codes, out = refs[:-1], refs[-1]
     rows = out.shape[1]
     for piece in range(2):
         total = jnp.zeros((rows, FRAG), f32)
-        for r in range(count):
-            code = codes[piece * count + r]
-            wide = jnp.broadcast_to(code[rows:].astype(f32)[:1], (LANES, LANES)).T
-            total = total + wide[:rows] * code[:rows].astype(f32)
-        out[piece] = total
-
-
-def run(kernel, outs, scratch, args, micros, memory=16, scalars=0):
+        for code in codes:
+            own = code.at[piece * (rows + SLOT) : (piece + 1) * (rows + SLOT)]
+            wide = jnp.broadcast_to(own[rows:].astype(f32)[:1], (LANES, LANES)).T
+            total = total + wide[:rows] * own[:rows].astype(f32)
+        out[piece] = total.astype(out.dtype)
+
+
+def outer_kernel(own, other, out):
+    out[...] = (own[...].astype(f32) + other[...].astype(f32)).astype(out.dtype)
+
+
+def run(kernel, outs, scratch, args, micros, memory=16, scalars=0, outside=0):
     whole = pl.BlockSpec(memory_space=pltpu.VMEM)
     scalar = pl.BlockSpec(memory_space=pltpu.SMEM)
+    remote = pl.BlockSpec(memory_space=pltpu.HBM)
     return pl.pallas_call(
         kernel,
         out_shape=[jax.ShapeDtypeStruct(shape, dtype) for shape, dtype in outs],
-        in_specs=[scalar] * scalars + [whole] * (len(args) - scalars),
+        in_specs=[scalar] * scalars
+        + [whole] * (len(args) - scalars - outside)
+        + [remote] * outside,
         out_specs=[whole] * len(outs),
-        scratch_shapes=[pltpu.VMEM(shape, dtype) for shape, dtype in scratch],
+        scratch_shapes=[
+            pltpu.SemaphoreType.DMA(shape) if dtype is None else pltpu.VMEM(shape, dtype)
+            for shape, dtype in scratch
+        ],
         compiler_params=pltpu.CompilerParams(vmem_limit_bytes=memory << 20),
         cost_estimate=pl.CostEstimate(
             flops=int(micros * 1e9), bytes_accessed=int(micros * 3e6), transcendentals=0
@@ -423,14 +469,23 @@
     return lax.ppermute(value, axis, [(i, i ^ step) for i in range(count)])
 
 
+def across_chips(sends):
+    return [sends[0]] + [hop(sends[c], "fsdp", 2 * c) for c in range(1, len(sends))]
+
+
+def exchanged(first, second, n):
+    bits = [1 << i for i in range((n // 2).bit_length() - 1)]
+    found = [{0: value} for value in (first, second)]
+    for c in range(1, n // 2):
+        used = [bit for bit in bits if c & bit]
+        for pieces, bit in zip(found, (used[0], used[-1])):
+            pieces[c] = hop(pieces[c ^ bit], "fsdp", 2 * bit)
+    return [[pieces[c] for c in range(n // 2)] for pieces in found]
+
+
 def from_chips(sends):
-    near = [sends[0]] + [hop(sends[c], "fsdp", 2 * c) for c in range(1, len(sends))]
+    near = across_chips(sends)
     return near, [hop(value, "fsdp", 1) for value in near]
-
-
-def gathered(value, n):
-    near, far = from_chips([value] * (n // 2))
-    return [piece for pair in zip(near, far) for piece in pair]
 
 
 def shards(
@@ -464,19 +519,40 @@
         ((atoms, lanes), f32),
     ]
 
-    feats = gathered(node_feats, n)
+    pack_inputs = [
+        msg_weight,
+        neighbor_src,
+        distances,
+        graph_ids,
+        radial_weight,
+    ]
+    bundle = 2 * rows + 4 * SLOT
     *packed, own_radial = run(
         functools.partial(pack_kernel, n, width),
-        [((2 * rows + 4 * SLOT, LANES), bf16)] * m + [((basis, LANES), f32)],
-        [((n, rows, LANES), bf16), ((n, basis, LANES), f32), ((SLOT, LANES), f32)],
-        [msg_weight, neighbor_src, distances, graph_ids, radial_weight],
+        [((bundle, LANES), bf16)] * m + [((basis, LANES), f32)],
+        [((n, rows, LANES), bf16), ((n, basis, LANES), f32), ((SLOT, LANES), f32)]
+        + [(piece.shape, piece.dtype) for piece in pack_inputs]
+        + [((len(pack_inputs),), None)],
+        pack_inputs,
         1,
-    )
-    near, far = from_chips(packed)
+        60,
+        outside=len(pack_inputs),
+    )
+    near = across_chips(packed)
+    feats, cots = exchanged(node_feats, cotangent, n)
+    (give_lists,) = run(
+        functools.partial(merge_kernel, m),
+        [((m * bundle, LANES), bf16)],
+        [],
+        [*near, feats[m // 2], cots[1]],
+        0,
+        memory,
+    )
+    far = hop(give_lists, "fsdp", 1)
     weights, columns, offsets, *made = run(
         functools.partial(lists_kernel, n, margin, neighbors, ahead),
         [
-            ((channels, LANES), bf16),
+            ((channels, 2 * LANES), bf16),
             ((all_atoms, LANES), f32),
             ((n * SLOT, LANES), f32),
         ]
@@ -492,67 +568,81 @@
             ((min(n, 8), basis * SLOT, LANES), f32),
             ((2 * basis * SLOT, lanes), bf16),
         ],
-        [*near, *far, own_radial],
-        6,
-        memory,
-    )
-    keep, give, weighted, slope = run(
+        [*near, far, own_radial],
+        0,
+        memory,
+    )
+    other_weight = hop(out_weight, "fsdp", 1)
+    own_products, give_products, held_feats = run(
+        functools.partial(products_kernel, n),
+        [((all_atoms, LANES), bf16)] * 2 + [((all_atoms // 2, channels), bf16)],
+        [((2 * LANES, channels), bf16)],
+        [weights, out_weight, other_weight, *feats, *cots],
+        1,
+        memory,
+    )
+    got_products = hop(give_products, "fsdp", 1)
+    held_feats = pl.pallas_call(
+        gate_kernel,
+        out_shape=jax.ShapeDtypeStruct(held_feats.shape, bf16),
+        in_specs=[pl.BlockSpec(memory_space=pl.ANY)] * 2,
+        out_specs=pl.BlockSpec(memory_space=pl.ANY),
+        input_output_aliases={0: 0},
+        compiler_params=pltpu.CompilerParams(vmem_limit_bytes=1 << 20),
+    )(held_feats, got_products)
+    keep, give, dagg = run(
         functools.partial(forward_kernel, n, margin, neighbors, norm, ahead),
         [
             ((all_atoms // 2, LANES), bf16),
             ((all_atoms // 2, LANES), bf16),
-            ((all_atoms, LANES), bf16),
             ((all_atoms, LANES), f32),
         ],
         [((all_atoms + 2 * margin, LANES), bf16)]
         + (step_scratch + [((neighbors * 2 * margin, 8 * margin), bf16)]) * (not ahead),
-        [*feats, weights, columns, own_radial, *made[:2]],
-        4,
-        memory,
-    )
-    cots = gathered(cotangent, n)
+        [own_products, got_products, columns, own_radial, *made[:2]],
+        1,
+        memory,
+    )
+    other_act = hop(give, "fsdp", 1)
     grad_sends = run(
-        functools.partial(backward_kernel, n, margin, neighbors, ahead),
+        functools.partial(backward_kernel, n, margin, neighbors, channels, ahead),
         [((2 * rows, LANES), bf16)] * m,
         [
-            ((LANES, channels), bf16),
-            ((all_atoms, LANES), f32),
             ((min(n, 8) if ahead else 1, neighbors * atoms, LANES), bf16),
             ((all_atoms + 2 * margin, LANES), f32),
             ((LANES, all_atoms), bf16),
             ((channels, LANES), bf16),
         ]
         + (step_scratch + [((reach, neighbors * atoms), bf16)]) * (not ahead),
-        [*cots, *feats, out_weight, own_radial, slope, columns, offsets, *made[::2]],
+        [
+            held_feats,
+            hop(held_feats, "fsdp", 1),
+            dagg,
+            own_radial,
+            columns,
+            offsets,
+            *made[::2],
+        ],
         4,
         memory,
     )
-    grad_out, out_code = run(
-        functools.partial(out_grad_kernel, n),
-        [((1, rows, channels), bf16), ((rows + SLOT, FRAG), bf16)],
-        [((LANES, channels), f32)],
-        [fragment, weighted, *cots],
+    near, far = from_chips(grad_sends)
+    *sums, own_part, give_part = run(
+        functools.partial(chip_kernel, n, margin, neighbors, width),
+        [((atoms, channels), bf16)] * m + [((rows, channels), f32), ((rows, channels), bf16)],
+        [],
+        [columns, keep, other_act, out_weight, other_weight, grad_sends[0], *cots],
         1,
         memory,
+    )
+    grad_msg, grad_out, code = run(
+        functools.partial(grads_kernel, n),
+        [((1, rows, channels), bf16)] * 2 + [((2 * (rows + SLOT), FRAG), bf16)],
+        [((n, rows, LANES), bf16), ((rows, channels), f32)],
+        [fragment, *near, *far, own_part, hop(give_part, "fsdp", 1)],
+        1,
+        memory,
         scalars=1,
-    )
-    near, far = from_chips(grad_sends)
-    grad_msg, msg_code = run(
-        functools.partial(msg_grad_kernel, n),
-        [((1, rows, channels), bf16), ((rows + SLOT, FRAG), bf16)],
-        [((n, rows, LANES), bf16)],
-        [fragment, *near, *far],
-        1,
-        memory,
-        scalars=1,
-    )
-    sums = run(
-        functools.partial(partial_kernel, n, width),
-        [((atoms, channels), bf16)] * m,
-        [],
-        [keep, hop(give, "fsdp", 1), out_weight, hop(out_weight, "fsdp", 1)],
-        1,
-        memory,
     )
     (node_out,) = run(
         node_kernel,
@@ -562,14 +652,24 @@
         1,
         memory,
     )
-    codes = [
-        piece if d == 0 else hop(piece, "replica", d)
-        for piece in (msg_code, out_code)
-        for d in range(replicas)
-    ]
+    step = 1
+    codes = [code]
+    if replicas > 1:
+        codes.append(hop(code, "replica", step))
     (outer_sum,) = run(
-        functools.partial(outer_kernel, replicas), [((2, rows, FRAG), f32)], [], codes, 1, memory
-    )
+        pair_kernel, [((2, rows, FRAG), f32 if replicas <= 2 else bf16)], [], codes, 0, memory
+    )
+    while 2 * step < replicas:
+        step = 2 * step
+        last = 2 * step >= replicas
+        (outer_sum,) = run(
+            outer_kernel,
+            [((2, rows, FRAG), f32 if last else bf16)],
+            [],
+            [outer_sum, hop(outer_sum, "replica", step)],
+            0,
+            memory,
+        )
     return node_out, grad_msg, grad_out, outer_sum
 
 

time: 81.9 us -> 65.7 us (0.80)
  waiting for transfers between devices: 30.2 us -> 20.7 us
  starting transfers between devices: 29.4 us -> 24.9 us
  local copies, waits for them, and re-layouts: 3.76 us -> 1.57 us
    ppermute x39 -> x27, waiting for transfers between devices: 30.2 us -> 20.7 us  [hop(): return lax.ppermute(value, axis, [(i, i ^ step) for i in range(count)])]
    ppermute x39 -> x27, starting transfers between devices: 29.4 us -> 24.9 us  [hop(): return lax.ppermute(value, axis, [(i, i ^ step) for i in range(count)])]
    unnamed x16 -> x10, local copies, waits for them, and re-layouts: 3.76 us -> 1.57 us
    pallas_call x9 -> x11, Pallas kernels: 16.8 us -> 17 us  [run(): pl.pallas_call(kernel, out_shape=[jax.ShapeDtypeStruct(shape, dtype) for...]
  transfers between devices with their start and end apart: 39 -> 27, of which waited for: 13 -> 13; matrix products, arithmetic and copies ran while one was open for 0% -> 0% of each run, Pallas kernels for 19% -> 21%
where the time goes in v3:
time: 65.7 us; the launch traced here: 65.5 us
  starting transfers between devices  24.9 us (38%)
  waiting for transfers between devices  20.7 us (32%)
  Pallas kernels  17 us (26%)
  local copies, waits for them, and re-layouts  1.57 us (2%)
  between operations  1.45 us (2%)
    ppermute x27, starting transfers between devices, hop(): return lax.ppermute(value, axis, [(i, i ^ step) for i in range(count)])  24.9 us
    ppermute x27, waiting for transfers between devices, hop(): return lax.ppermute(value, axis, [(i, i ^ step) for i in range(count)])  20.7 us
    pallas_call x11, Pallas kernels, run(): pl.pallas_call(kernel, out_shape=[jax.ShapeDtypeStruct(shape, dtype) for...  17 us
    unnamed x10, local copies, waits for them, and re-layouts  1.57 us
  transfers between devices with their start and end apart: 27, of which 13 were waited for; matrix products, arithmetic and copies ran while one was open for 0% of the time, Pallas kernels for 21%

profile of v3, /device:TPU:0, one launch (start us, length us, event | category | flops | bytes accessed | tf_op | source)
XLA Modules:
  0.0 65.5 jit_solution(4389498386072306234)
XLA Ops:
  0.7 3.0 %collective-permute-start.3 = (bf16[128,1024]{1,0:T(8,128)(2,1)}, bf16[128,1024]{1,0:T(8,128)(2,1)S(1)}, u32[]{:S(2)}, u32[]{:S(2)}) collective-permute-start(bf16[128,1024]{1,0:T(8,128)(2,1)} %feats.1), channel_id=1, source_target_pairs={{0,4},{1,5},{2,6},{3,7},{4,0},{5,1},{6,2},{7,3},{8,12},{9,13},{10,... | collective-permute-start | bytes 786440 | tf_op jit(solution)/shard_map/ppermute | solution.py:469
  3.7 1.5 %collective-permute-start.4 = (bf16[128,1024]{1,0:T(8,128)(2,1)}, bf16[128,1024]{1,0:T(8,128)(2,1)S(1)}, u32[]{:S(2)}, u32[]{:S(2)}) collective-permute-start(bf16[128,1024]{1,0:T(8,128)(2,1)} %refs_6_.1), channel_id=1, source_target_pairs={{0,2},{1,3},{2,0},{3,1},{4,6},{5,7},{6,4},{7,5},{8,10},{9,11},{10,... | collective-permute-start | bytes 786440 | tf_op jit(solution)/shard_map/ppermute | solution.py:469
  5.2 1.8 %shard_map.120 = (bf16[320,128]{1,0:T(8,128)(2,1)}, bf16[320,128]{1,0:T(8,128)(2,1)}, bf16[320,128]{1,0:T(8,128)(2,1)}, bf16[320,128]{1,0:T(8,128)(2,1)}, f32[8,128]{1,0:T(8,128)}) custom-call(bf16[128,1024]{1,0:T(8,128)(2,1)} %refs_0_.2, s32[12,128]{1,0:T(8,128)} %refs_1_.1, f32[12,128]{1,0:T(8,128)} %refs_2_.1, s32[1,128]{1,0:T(1,128)} %refs_3_.2, ...), custom_call_target="tpu_custom_call" | custom-call | flops 1000000000 | bytes 3000000 | tf_op jit(solution)/shard_map/pallas_call | solution.py:449
  7.7 2.9 %collective-permute-start.2 = (bf16[320,128]{1,0:T(8,128)(2,1)}, bf16[320,128]{1,0:T(8,128)(2,1)S(1)}, u32[]{:S(2)}, u32[]{:S(2)}) collective-permute-start(bf16[320,128]{1,0:T(8,128)(2,1)} %get-tuple-element.37), channel_id=1, source_target_pairs={{0,6},{1,7},{2,4},{3,5},{4,2},{5,3},{6,0},{7,1},{8,14},{9,15},{10,... | collective-permute-start | bytes 245768 | tf_op jit(solution)/shard_map/ppermute | solution.py:469
  10.5 3.8 %collective-permute-done.refs_1_ = bf16[320,128]{1,0:T(8,128)(2,1)S(1)} collective-permute-done((bf16[320,128]{1,0:T(8,128)(2,1)}, bf16[320,128]{1,0:T(8,128)(2,1)S(1)}, u32[]{:S(2)}, u32[]{:S(2)}) %collective-permute-start) | collective-permute-done | bytes 81952 | tf_op jit(solution)/shard_map/ppermute | solution.py:469
  16.0 1.7 %collective-permute-start.7 = (bf16[128,1024]{1,0:T(8,128)(2,1)S(1)}, bf16[128,1024]{1,0:T(8,128)(2,1)S(1)}, u32[]{:S(2)}, u32[]{:S(2)}) collective-permute-start(bf16[128,1024]{1,0:T(8,128)(2,1)S(1)} %copy-done.4), channel_id=1, source_target_pairs={{0,2},{1,3},{2,0},{3,1},{4,6},{5,7},{6,4},{7,5},{8,10},{9,11},{10,... | collective-permute-start | bytes 786440 | tf_op jit(solution)/shard_map/ppermute | solution.py:469
  17.9 1.5 %collective-permute-start.9 = (bf16[128,1024]{1,0:T(8,128)(2,1)S(1)}, bf16[128,1024]{1,0:T(8,128)(2,1)S(1)}, u32[]{:S(2)}, u32[]{:S(2)}) collective-permute-start(bf16[128,1024]{1,0:T(8,128)(2,1)S(1)} %copy-done.2), channel_id=1, source_target_pairs={{0,4},{1,5},{2,6},{3,7},{4,0},{5,1},{6,2},{7,3},{8,12},{9,13},{10,... | collective-permute-start | bytes 786440 | tf_op jit(solution)/shard_map/ppermute | solution.py:469
  21.0 4.9 %shard_map.122 = (bf16[1024,256]{1,0:T(8,128)(2,1)S(1)}, f32[1024,128]{1,0:T(8,128)S(1)}, f32[128,128]{1,0:T(8,128)S(1)}, f32[1024,1536]{1,0:T(8,128)S(1)}, bf16...) custom-call(bf16[320,128]{1,0:T(8,128)(2,1)S(1)} %copy-done, ...), custom_call_target="tpu_custom_call" | custom-call | tf_op jit(solution)/shard_map/pallas_call | solution.py:449
  25.8 1.1 %collective-permute-done.9.refs_6_.refs_8_ = bf16[128,1024]{1,0:T(8,128)(2,1)S(1)} collective-permute-done((bf16[128,1024]{1,0:T(8,128)(2,1)S(1)}, bf16[128,1024]{1,0:T(8,128)(2,1)S(1)}, u32[]{:S(2)}, u32[]{:S(2)}) %collective-permute-start.9) | collective-permute-done | bytes 262176 | tf_op jit(solution)/shard_map/ppermute | solution.py:469
  27.0 3.3 %collective-permute-done.8.refs_3_ = bf16[128,1024]{1,0:T(8,128)(2,1)S(1)} collective-permute-done((bf16[128,1024]{1,0:T(8,128)(2,1)S(1)}, bf16[128,1024]{1,0:T(8,128)(2,1)S(1)}, u32[]{:S(2)}, u32[]{:S(2)}) %collective-permute-start.8) | collective-permute-done | bytes 262176 | tf_op jit(solution)/shard_map/ppermute | solution.py:469
  30.3 1.7 %collective-permute-done.10.refs_7_.refs_9_ = bf16[128,1024]{1,0:T(8,128)(2,1)S(1)} collective-permute-done((bf16[128,1024]{1,0:T(8,128)(2,1)S(1)}, bf16[128,1024]{1,0:T(8,128)(2,1)S(1)}, u32[]{:S(2)}, u32[]{:S(2)}) %collective-permute-start.10) | collective-permute-done | bytes 262176 | tf_op jit(solution)/shard_map/ppermute | solution.py:469
  33.2 1.5 %collective-permute-done.11.refs_1_._after = bf16[1024,128]{1,0:T(8,128)(2,1)S(1)} collective-permute-done((bf16[1024,128]{1,0:T(8,128)(2,1)S(1)}, bf16[1024,128]{1,0:T(8,128)(2,1)S(1)}, u32[]{:S(2)}, u32[]{:S(2)}) %collective-permute-start.11) | collective-permute-done | bytes 262176 | tf_op jit(solution)/shard_map/ppermute | solution.py:469
  34.9 3.1 %shard_map.124 = (bf16[512,128]{1,0:T(8,128)(2,1)S(1)}, bf16[512,128]{1,0:T(8,128)(2,1)S(1)}, f32[1024,128]{1,0:T(8,128)S(1)}) custom-call(bf16[1024,128]{1,0:T(8,128)(2,1)S(1)} %get-tuple-element.41.refs_0_, bf16[1024,128]{1,0:T(8,128)(2,1)S(1)} %collective-permute-done.11.refs_1_._after, f32[1024,128]{1,0:T(8,128)S(1)} %get-tuple-element.39.refs_2_.refs_4_.refs_0_, ...), custom_call_target="tpu_custom_call" | custom-call | flops 1000000000 | bytes 3000000 | tf_op jit(solution)/shard_map/pallas_call | solution.py:449
  38.4 2.2 %shard_map.126 = (bf16[256,128]{1,0:T(8,128)(2,1)S(1)}, bf16[256,128]{1,0:T(8,128)(2,1)S(1)}, bf16[256,128]{1,0:T(8,128)(2,1)S(1)}, bf16[256,128]{1,0:T(8,128)(2,1)S(1)}) custom-call(bf16[512,1024]{1,0:T(8,128)(2,1)S(1)} %shard_map.125.refs_0_, bf16[512,1024]{1,0:T(8,128)(2,1)S(1)} %collective-permute-done.13.refs_1_, ...), custom_call_target="tpu_custom_call" | custom-call | flops 4000000000 | bytes 12000000 | tf_op jit(solution)/shard_map/pallas_call | solution.py:449
  40.6 1.3 %shard_map.127 = (bf16[128,1024]{1,0:T(8,128)(2,1)S(1)}, bf16[128,1024]{1,0:T(8,128)(2,1)S(1)}, bf16[128,1024]{1,0:T(8,128)(2,1)S(1)}, bf16[128,1024]{1,0:T(8,12...) custom-call(f32[1024,128]{1,0:T(8,128)S(1)} %get-tuple-element.39.refs_2_.refs_4_.refs_0_, ...), custom_call_target="tpu_custom_call" | custom-call | flops 1000000000 | bytes 3000000 | tf_op jit(solution)/shard_map/pallas_call | solution.py:449
  42.5 1.7 %collective-permute-start.18 = (bf16[256,128]{1,0:T(8,128)(2,1)S(1)}, bf16[256,128]{1,0:T(8,128)(2,1)S(1)}, u32[]{:S(2)}, u32[]{:S(2)}) collective-permute-start(bf16[256,128]{1,0:T(8,128)(2,1)S(1)} %get-tuple-element.57), channel_id=1, source_target_pairs={{0,4},{1,5},{2,6},{3,7},{4,0},{5,1},{6,2},{7,3},{8,12},{9,13},{10,... | collective-permute-start | bytes 196616 | tf_op jit(solution)/shard_map/ppermute | solution.py:469
  44.2 1.4 %collective-permute-start.19 = (bf16[256,128]{1,0:T(8,128)(2,1)S(1)}, bf16[256,128]{1,0:T(8,128)(2,1)S(1)}, u32[]{:S(2)}, u32[]{:S(2)}) collective-permute-start(bf16[256,128]{1,0:T(8,128)(2,1)S(1)} %get-tuple-element.58), channel_id=1, source_target_pairs={{0,6},{1,7},{2,4},{3,5},{4,2},{5,3},{6,0},{7,1},{8,14},{9,15},{10,... | collective-permute-start | bytes 196616 | tf_op jit(solution)/shard_map/ppermute | solution.py:469
  47.2 2.2 %collective-permute-done.19.refs_3_ = bf16[256,128]{1,0:T(8,128)(2,1)S(1)} collective-permute-done((bf16[256,128]{1,0:T(8,128)(2,1)S(1)}, bf16[256,128]{1,0:T(8,128)(2,1)S(1)}, u32[]{:S(2)}, u32[]{:S(2)}) %collective-permute-start.19) | collective-permute-done | bytes 65568 | tf_op jit(solution)/shard_map/ppermute | solution.py:469
  49.4 1.5 %collective-permute-start.14 = (bf16[128,1024]{1,0:T(8,128)(2,1)S(1)}, bf16[128,1024]{1,0:T(8,128)(2,1)S(1)}, u32[]{:S(2)}, u32[]{:S(2)}) collective-permute-start(bf16[128,1024]{1,0:T(8,128)(2,1)S(1)} %get-tuple-element.53), channel_id=1, source_target_pairs={{0,2},{1,3},{2,0},{3,1},{4,6},{5,7},{6,4},{7,5},{8,10},{9,11},{10,... | collective-permute-start | bytes 786440 | tf_op jit(solution)/shard_map/ppermute | solution.py:469
  51.4 1.5 %collective-permute-start.16 = (bf16[128,1024]{1,0:T(8,128)(2,1)S(1)}, bf16[128,1024]{1,0:T(8,128)(2,1)S(1)}, u32[]{:S(2)}, u32[]{:S(2)}) collective-permute-start(bf16[128,1024]{1,0:T(8,128)(2,1)S(1)} %get-tuple-element.55), channel_id=1, source_target_pairs={{0,6},{1,7},{2,4},{3,5},{4,2},{5,3},{6,0},{7,1},{8,14},{9,15},{10,... | collective-permute-start | bytes 786440 | tf_op jit(solution)/shard_map/ppermute | solution.py:469
  55.1 1.6 %collective-permute-start.25 = (bf16[288,128]{1,0:T(8,128)(2,1)S(1)}, bf16[288,128]{1,0:T(8,128)(2,1)S(1)}, u32[]{:S(2)}, u32[]{:S(2)}) collective-permute-start(bf16[288,128]{1,0:T(8,128)(2,1)S(1)} %get-tuple-element.63.refs_0_), channel_id=1, source_target_pairs={{0,8},{8,0},{16,24},{24,16},{1,9},{9,1},{17,25},{25,17},{2,10},{10... | collective-permute-start | bytes 221192 | tf_op jit(solution)/shard_map/ppermute | solution.py:469
  56.7 2.8 %collective-permute-done.25.refs_1_ = bf16[288,128]{1,0:T(8,128)(2,1)S(1)} collective-permute-done((bf16[288,128]{1,0:T(8,128)(2,1)S(1)}, bf16[288,128]{1,0:T(8,128)(2,1)S(1)}, u32[]{:S(2)}, u32[]{:S(2)}) %collective-permute-start.25) | collective-permute-done | bytes 73760 | tf_op jit(solution)/shard_map/ppermute | solution.py:469
  59.6 2.7 %collective-permute-start.26 = (bf16[2,128,128]{2,1,0:T(8,128)(2,1)S(1)}, bf16[2,128,128]{2,1,0:T(8,128)(2,1)S(1)}, u32[]{:S(2)}, u32[]{:S(2)}) collective-permute-start(bf16[2,128,128]{2,1,0:T(8,128)(2,1)S(1)} %shard_map.130.own), channel_id=1, source_target_pairs={{0,16},{8,24},{16,0},{24,8},{1,17},{9,25},{17,1},{25,9},{2,18},{10... | collective-permute-start | bytes 196616 | tf_op jit(solution)/shard_map/ppermute | solution.py:469
  62.2 1.4 %collective-permute-done.16.refs_3_ = bf16[128,1024]{1,0:T(8,128)(2,1)S(1)} collective-permute-done((bf16[128,1024]{1,0:T(8,128)(2,1)S(1)}, bf16[128,1024]{1,0:T(8,128)(2,1)S(1)}, u32[]{:S(2)}, u32[]{:S(2)}) %collective-permute-start.16) | collective-permute-done | bytes 262176 | tf_op jit(solution)/shard_map/ppermute | solution.py:469
  (52 shorter events, 12.1 us)
Async XLA Ops:
  0.7 14.3 %collective-permute-start.3 = (bf16[128,1024]{1,0:T(8,128)(2,1)}, bf16[128,1024]{1,0:T(8,128)(2,1)S(1)}, u32[]{:S(2)}, u32[]{:S(2)}) collective-permute-start(bf16[128,1024]{1,0:T(8,128)(2,1)} %feats.1), channel_id=1, source_target_pairs={{0,4},{1,5},{2,6},{3,7},{4,0},{5,1},{6,2},{7,3},{8,12},{9,13},{10,... | collective-permute-start | bytes 786440 | tf_op jit(solution)/shard_map/ppermute | solution.py:469
  3.7 11.3 %collective-permute-start.4 = (bf16[128,1024]{1,0:T(8,128)(2,1)}, bf16[128,1024]{1,0:T(8,128)(2,1)S(1)}, u32[]{:S(2)}, u32[]{:S(2)}) collective-permute-start(bf16[128,1024]{1,0:T(8,128)(2,1)} %refs_6_.1), channel_id=1, source_target_pairs={{0,2},{1,3},{2,0},{3,1},{4,6},{5,7},{6,4},{7,5},{8,10},{9,11},{10,... | collective-permute-start | bytes 786440 | tf_op jit(solution)/shard_map/ppermute | solution.py:469
  7.0 7.3 %collective-permute-start = (bf16[320,128]{1,0:T(8,128)(2,1)}, bf16[320,128]{1,0:T(8,128)(2,1)S(1)}, u32[]{:S(2)}, u32[]{:S(2)}) collective-permute-start(bf16[320,128]{1,0:T(8,128)(2,1)} %get-tuple-element.35), channel_id=1, source_target_pairs={{0,2},{1,3},{2,0},{3,1},{4,6},{5,7},{6,4},{7,5},{8,10},{9,11},{10,... | collective-permute-start | bytes 245768 | tf_op jit(solution)/shard_map/ppermute | solution.py:469
  7.6 6.7 %collective-permute-start.1 = (bf16[320,128]{1,0:T(8,128)(2,1)}, bf16[320,128]{1,0:T(8,128)(2,1)S(1)}, u32[]{:S(2)}, u32[]{:S(2)}) collective-permute-start(bf16[320,128]{1,0:T(8,128)(2,1)} %get-tuple-element.36), channel_id=1, source_target_pairs={{0,4},{1,5},{2,6},{3,7},{4,0},{5,1},{6,2},{7,3},{8,12},{9,13},{10,... | collective-permute-start | bytes 245768 | tf_op jit(solution)/shard_map/ppermute | solution.py:469
  7.7 7.3 %collective-permute-start.2 = (bf16[320,128]{1,0:T(8,128)(2,1)}, bf16[320,128]{1,0:T(8,128)(2,1)S(1)}, u32[]{:S(2)}, u32[]{:S(2)}) collective-permute-start(bf16[320,128]{1,0:T(8,128)(2,1)} %get-tuple-element.37), channel_id=1, source_target_pairs={{0,6},{1,7},{2,4},{3,5},{4,2},{5,3},{6,0},{7,1},{8,14},{9,15},{10,... | collective-permute-start | bytes 245768 | tf_op jit(solution)/shard_map/ppermute | solution.py:469
  15.9 4.0 %collective-permute-start.5 = (bf16[1280,128]{1,0:T(8,128)(2,1)S(1)}, bf16[1280,128]{1,0:T(8,128)(2,1)S(1)}, u32[]{:S(2)}, u32[]{:S(2)}) collective-permute-start(bf16[1280,128]{1,0:T(8,128)(2,1)S(1)} %shard_map.121), channel_id=1, source_target_pairs={{0,1},{1,0},{2,3},{3,2},{4,5},{5,4},{6,7},{7,6},{8,9},{9,8},{10,11... | collective-permute-start | bytes 983048 | tf_op jit(solution)/shard_map/ppermute | solution.py:469
  16.0 9.8 %collective-permute-start.7 = (bf16[128,1024]{1,0:T(8,128)(2,1)S(1)}, bf16[128,1024]{1,0:T(8,128)(2,1)S(1)}, u32[]{:S(2)}, u32[]{:S(2)}) collective-permute-start(bf16[128,1024]{1,0:T(8,128)(2,1)S(1)} %copy-done.4), channel_id=1, source_target_pairs={{0,2},{1,3},{2,0},{3,1},{4,6},{5,7},{6,4},{7,5},{8,10},{9,11},{10,... | collective-permute-start | bytes 786440 | tf_op jit(solution)/shard_map/ppermute | solution.py:469
  17.7 8.1 %collective-permute-start.6 = (bf16[128,1024]{1,0:T(8,128)(2,1)S(1)}, bf16[128,1024]{1,0:T(8,128)(2,1)S(1)}, u32[]{:S(2)}, u32[]{:S(2)}) collective-permute-start(bf16[128,1024]{1,0:T(8,128)(2,1)S(1)} %copy-done.3), channel_id=1, source_target_pairs={{0,1},{1,0},{2,3},{3,2},{4,5},{5,4},{6,7},{7,6},{8,9},{9,8},{10,11... | collective-permute-start | bytes 786440 | tf_op jit(solution)/shard_map/ppermute | solution.py:469
  17.9 9.1 %collective-permute-start.9 = (bf16[128,1024]{1,0:T(8,128)(2,1)S(1)}, bf16[128,1024]{1,0:T(8,128)(2,1)S(1)}, u32[]{:S(2)}, u32[]{:S(2)}) collective-permute-start(bf16[128,1024]{1,0:T(8,128)(2,1)S(1)} %copy-done.2), channel_id=1, source_target_pairs={{0,4},{1,5},{2,6},{3,7},{4,0},{5,1},{6,2},{7,3},{8,12},{9,13},{10,... | collective-permute-start | bytes 786440 | tf_op jit(solution)/shard_map/ppermute | solution.py:469
  19.4 10.9 %collective-permute-start.8 = (bf16[128,1024]{1,0:T(8,128)(2,1)S(1)}, bf16[128,1024]{1,0:T(8,128)(2,1)S(1)}, u32[]{:S(2)}, u32[]{:S(2)}) collective-permute-start(bf16[128,1024]{1,0:T(8,128)(2,1)S(1)} %collective-permute-done.3.refs_4_.refs_2_), channel_id=1, source_target_pairs={{0,2},{1,3},{2,0},{3,1},{4,6},{5,7},{6,4},{7,5},{8,10},{9,11},{10,... | collective-permute-start | bytes 786440 | tf_op jit(solution)/shard_map/ppermute | solution.py:469
  19.9 12.1 %collective-permute-start.10 = (bf16[128,1024]{1,0:T(8,128)(2,1)S(1)}, bf16[128,1024]{1,0:T(8,128)(2,1)S(1)}, u32[]{:S(2)}, u32[]{:S(2)}) collective-permute-start(bf16[128,1024]{1,0:T(8,128)(2,1)S(1)} %collective-permute-done.4.refs_5_.refs_7_), channel_id=1, source_target_pairs={{0,4},{1,5},{2,6},{3,7},{4,0},{5,1},{6,2},{7,3},{8,12},{9,13},{10,... | collective-permute-start | bytes 786440 | tf_op jit(solution)/shard_map/ppermute | solution.py:469
  34.8 3.7 %collective-permute-start.13 = (bf16[512,1024]{1,0:T(8,128)(2,1)S(1)}, bf16[512,1024]{1,0:T(8,128)(2,1)S(1)}, u32[]{:S(2)}, u32[]{:S(2)}) collective-permute-start(bf16[512,1024]{1,0:T(8,128)(2,1)S(1)} %shard_map.125.refs_0_), channel_id=1, source_target_pairs={{0,1},{1,0},{2,3},{3,2},{4,5},{5,4},{6,7},{7,6},{8,9},{9,8},{10,11... | collective-permute-start | bytes 3145736 | tf_op jit(solution)/shard_map/ppermute | solution.py:469
  41.9 12.2 %collective-permute-start.24 = (bf16[128,1024]{1,0:T(8,128)(2,1)S(1)}, bf16[128,1024]{1,0:T(8,128)(2,1)S(1)}, u32[]{:S(2)}, u32[]{:S(2)}) collective-permute-start(bf16[128,1024]{1,0:T(8,128)(2,1)S(1)} %get-tuple-element.60), channel_id=1, source_target_pairs={{0,1},{1,0},{2,3},{3,2},{4,5},{5,4},{6,7},{7,6},{8,9},{9,8},{10,11... | collective-permute-start | bytes 786440 | tf_op jit(solution)/shard_map/ppermute | solution.py:469
  42.1 4.5 %collective-permute-start.17 = (bf16[256,128]{1,0:T(8,128)(2,1)S(1)}, bf16[256,128]{1,0:T(8,128)(2,1)S(1)}, u32[]{:S(2)}, u32[]{:S(2)}) collective-permute-start(bf16[256,128]{1,0:T(8,128)(2,1)S(1)} %get-tuple-element.56), channel_id=1, source_target_pairs={{0,2},{1,3},{2,0},{3,1},{4,6},{5,7},{6,4},{7,5},{8,10},{9,11},{10,... | collective-permute-start | bytes 196616 | tf_op jit(solution)/shard_map/ppermute | solution.py:469
  42.5 4.3 %collective-permute-start.18 = (bf16[256,128]{1,0:T(8,128)(2,1)S(1)}, bf16[256,128]{1,0:T(8,128)(2,1)S(1)}, u32[]{:S(2)}, u32[]{:S(2)}) collective-permute-start(bf16[256,128]{1,0:T(8,128)(2,1)S(1)} %get-tuple-element.57), channel_id=1, source_target_pairs={{0,4},{1,5},{2,6},{3,7},{4,0},{5,1},{6,2},{7,3},{8,12},{9,13},{10,... | collective-permute-start | bytes 196616 | tf_op jit(solution)/shard_map/ppermute | solution.py:469
  44.2 5.2 %collective-permute-start.19 = (bf16[256,128]{1,0:T(8,128)(2,1)S(1)}, bf16[256,128]{1,0:T(8,128)(2,1)S(1)}, u32[]{:S(2)}, u32[]{:S(2)}) collective-permute-start(bf16[256,128]{1,0:T(8,128)(2,1)S(1)} %get-tuple-element.58), channel_id=1, source_target_pairs={{0,6},{1,7},{2,4},{3,5},{4,2},{5,3},{6,0},{7,1},{8,14},{9,15},{10,... | collective-permute-start | bytes 196616 | tf_op jit(solution)/shard_map/ppermute | solution.py:469
  45.6 5.2 %collective-permute-start.20 = (bf16[256,128]{1,0:T(8,128)(2,1)S(1)}, bf16[256,128]{1,0:T(8,128)(2,1)S(1)}, u32[]{:S(2)}, u32[]{:S(2)}) collective-permute-start(bf16[256,128]{1,0:T(8,128)(2,1)S(1)} %get-tuple-element.51.refs_5_.refs_0_), channel_id=1, source_target_pairs={{0,1},{1,0},{2,3},{3,2},{4,5},{5,4},{6,7},{7,6},{8,9},{9,8},{10,11... | collective-permute-start | bytes 196616 | tf_op jit(solution)/shard_map/ppermute | solution.py:469
  46.7 4.7 %collective-permute-start.21 = (bf16[256,128]{1,0:T(8,128)(2,1)S(1)}, bf16[256,128]{1,0:T(8,128)(2,1)S(1)}, u32[]{:S(2)}, u32[]{:S(2)}) collective-permute-start(bf16[256,128]{1,0:T(8,128)(2,1)S(1)} %collective-permute-done.17.refs_1_), channel_id=1, source_target_pairs={{0,1},{1,0},{2,3},{3,2},{4,5},{5,4},{6,7},{7,6},{8,9},{9,8},{10,11... | collective-permute-start | bytes 196616 | tf_op jit(solution)/shard_map/ppermute | solution.py:469
  46.8 6.1 %collective-permute-start.22 = (bf16[256,128]{1,0:T(8,128)(2,1)S(1)}, bf16[256,128]{1,0:T(8,128)(2,1)S(1)}, u32[]{:S(2)}, u32[]{:S(2)}) collective-permute-start(bf16[256,128]{1,0:T(8,128)(2,1)S(1)} %collective-permute-done.18.refs_2_), channel_id=1, source_target_pairs={{0,1},{1,0},{2,3},{3,2},{4,5},{5,4},{6,7},{7,6},{8,9},{9,8},{10,11... | collective-permute-start | bytes 196616 | tf_op jit(solution)/shard_map/ppermute | solution.py:469
  49.4 12.9 %collective-permute-start.14 = (bf16[128,1024]{1,0:T(8,128)(2,1)S(1)}, bf16[128,1024]{1,0:T(8,128)(2,1)S(1)}, u32[]{:S(2)}, u32[]{:S(2)}) collective-permute-start(bf16[128,1024]{1,0:T(8,128)(2,1)S(1)} %get-tuple-element.53), channel_id=1, source_target_pairs={{0,2},{1,3},{2,0},{3,1},{4,6},{5,7},{6,4},{7,5},{8,10},{9,11},{10,... | collective-permute-start | bytes 786440 | tf_op jit(solution)/shard_map/ppermute | solution.py:469
  50.8 11.4 %collective-permute-start.15 = (bf16[128,1024]{1,0:T(8,128)(2,1)S(1)}, bf16[128,1024]{1,0:T(8,128)(2,1)S(1)}, u32[]{:S(2)}, u32[]{:S(2)}) collective-permute-start(bf16[128,1024]{1,0:T(8,128)(2,1)S(1)} %get-tuple-element.54), channel_id=1, source_target_pairs={{0,4},{1,5},{2,6},{3,7},{4,0},{5,1},{6,2},{7,3},{8,12},{9,13},{10,... | collective-permute-start | bytes 786440 | tf_op jit(solution)/shard_map/ppermute | solution.py:469
  51.4 12.3 %collective-permute-start.16 = (bf16[128,1024]{1,0:T(8,128)(2,1)S(1)}, bf16[128,1024]{1,0:T(8,128)(2,1)S(1)}, u32[]{:S(2)}, u32[]{:S(2)}) collective-permute-start(bf16[128,1024]{1,0:T(8,128)(2,1)S(1)} %get-tuple-element.55), channel_id=1, source_target_pairs={{0,6},{1,7},{2,4},{3,5},{4,2},{5,3},{6,0},{7,1},{8,14},{9,15},{10,... | collective-permute-start | bytes 786440 | tf_op jit(solution)/shard_map/ppermute | solution.py:469
  55.1 4.4 %collective-permute-start.25 = (bf16[288,128]{1,0:T(8,128)(2,1)S(1)}, bf16[288,128]{1,0:T(8,128)(2,1)S(1)}, u32[]{:S(2)}, u32[]{:S(2)}) collective-permute-start(bf16[288,128]{1,0:T(8,128)(2,1)S(1)} %get-tuple-element.63.refs_0_), channel_id=1, source_target_pairs={{0,8},{8,0},{16,24},{24,16},{1,9},{9,1},{17,25},{25,17},{2,10},{10... | collective-permute-start | bytes 221192 | tf_op jit(solution)/shard_map/ppermute | solution.py:469
  59.6 5.3 %collective-permute-start.26 = (bf16[2,128,128]{2,1,0:T(8,128)(2,1)S(1)}, bf16[2,128,128]{2,1,0:T(8,128)(2,1)S(1)}, u32[]{:S(2)}, u32[]{:S(2)}) collective-permute-start(bf16[2,128,128]{2,1,0:T(8,128)(2,1)S(1)} %shard_map.130.own), channel_id=1, source_target_pairs={{0,16},{8,24},{16,0},{24,8},{1,17},{9,25},{17,1},{25,9},{2,18},{10... | collective-permute-start | bytes 196616 | tf_op jit(solution)/shard_map/ppermute | solution.py:469
  (8 other events, 56.7 us)

commit v4 on v3

--- a/solution.py
+++ b/solution.py
@@ -76,6 +76,14 @@
         out[c * rows : (c + 1) * rows] = part[...]
 
 
+def swap_kernel(*refs):
+    parts, last, out = refs[:-2], refs[-2], refs[-1]
+    rows = parts[0].shape[0] // 2
+    for c, part in enumerate(parts):
+        out[c * rows : (c + 1) * rows] = part[rows:]
+    out[len(parts) * rows :] = last[...]
+
+
 def gate_kernel(_value, _after, _out):
     pass
 
@@ -127,17 +135,21 @@
 
 
 def fill_place(margin, neighbors, offset, place):
-    atoms = offset.shape[1]
-    shape = (atoms + 2 * margin, atoms)
+    tile = 2 * margin
+    shape = (2 * tile, 2 * tile)
     shift = (
         lax.broadcasted_iota(jnp.int32, shape, 0)
-        - lax.broadcasted_iota(jnp.int32, shape, 1)
+        - lax.broadcasted_iota(jnp.int32, shape, 1) % tile
         - margin
     ).astype(f32)
-    for k in range(neighbors):
-        place[:, k * atoms : (k + 1) * atoms] = jnp.where(
-            offset[k : k + 1] == shift, 1.0, 0.0
-        ).astype(bf16)
+    for t in range(offset.shape[1] // tile):
+        for k in range(0, neighbors, 2):
+            row = jnp.concatenate(
+                [offset[k + i : k + i + 1, t * tile : (t + 1) * tile] for i in range(2)], axis=1
+            )
+            place[t * 2 * tile : (t + 1) * 2 * tile, k * tile : (k + 2) * tile] = jnp.where(
+                row == shift, 1.0, 0.0
+            ).astype(bf16)
 
 
 def lists_kernel(n, margin, neighbors, ahead, *refs):
@@ -201,18 +213,11 @@
                 margin,
                 neighbors,
                 offsets[rows_at(e, SLOT)],
-                place.at[rows_at(e, atoms + 2 * margin)],
+                place.at[rows_at(e, 2 * atoms)],
             )
             return 0
 
         lax.fori_loop(0, n, block_step, 0, unroll=2)
-
-
-def block_diagonal(first, second):
-    zero = jnp.zeros_like(first)
-    return jnp.concatenate(
-        [jnp.concatenate([first, zero], axis=1), jnp.concatenate([zero, second], axis=1)], axis=0
-    )
 
 
 def products_kernel(n, weights, own_weight, other_weight, *refs):
@@ -244,8 +249,8 @@
 def forward_kernel(n, margin, neighbors, norm, ahead, *refs):
     own, got, columns, own_radial = refs[:4]
     made = refs[4:6] if ahead else ()
-    keep, give, dagg, projected = refs[4 + len(made) : 8 + len(made)]
-    scratch = refs[8 + len(made) :]
+    keep, give, dagg, projected, act = refs[4 + len(made) : 9 + len(made)]
+    scratch = refs[9 + len(made) :]
     me = lax.axis_index("fsdp")
     core = me % 2
     atoms = columns.shape[0] // n
@@ -277,15 +282,18 @@
             fill_pick(margin, neighbors, turned, pick)
             own_pick = pick[...]
         start = pl.multiple_of(e * atoms, atoms)
-        windows = [projected[pl.ds(start + t * tile, 2 * tile)] for t in range(2)]
-        found = jnp.dot(own_pick, block_diagonal(*windows), preferred_element_type=f32)
         halves = []
         for t in range(2):
+            found = jnp.dot(
+                own_pick[:, t * 2 * tile : (t + 1) * 2 * tile],
+                projected[pl.ds(start + t * tile, 2 * tile)],
+                preferred_element_type=f32,
+            )
             total = jnp.zeros((tile, LANES), f32)
             for k in range(neighbors):
                 total = total + (
                     own_values[t * tile : (t + 1) * tile, k * LANES : (k + 1) * LANES]
-                    * found[k * tile : (k + 1) * tile, t * LANES : (t + 1) * LANES]
+                    * found[k * tile : (k + 1) * tile]
                 )
             halves.append(total)
         agg = jnp.concatenate(halves, axis=0) * norm
@@ -295,32 +303,27 @@
         graph = turned[:, at : at + 1]
         slope = sig * (1.0 + agg * (1.0 - sig)) * (graph * norm)
         dagg[rows_at(e, atoms)] = dagg[rows_at(e, atoms)] * slope
-
-        @pl.when(e % 2 == core)
-        def _():
-            keep[rows_at(e // 2, atoms)] = active
-
-        @pl.when(e % 2 != core)
-        def _():
-            give[rows_at(e // 2, atoms)] = active
-
+        act[rows_at(e, atoms)] = active
         return 0
 
     lax.fori_loop(0, n, block_step, 0, unroll=min(n, 8) if ahead else 1)
-
-
-def backward_kernel(n, margin, neighbors, channels, ahead, *refs):
+    for c in range(n // 2):
+        keep[c * atoms : (c + 1) * atoms] = act[rows_at(2 * c + core, atoms)]
+        give[c * atoms : (c + 1) * atoms] = act[rows_at(2 * c + 1 - core, atoms)]
+
+
+def backward_kernel(n, margin, neighbors, ahead, *refs):
     m = n // 2
-    feats, (dagg, own_radial, columns, offsets) = refs[:2], refs[2:6]
-    made = refs[6:8] if ahead else ()
-    refs = refs[6 + len(made) :]
-    sends, (terms, spread, turned, grads) = refs[:m], refs[m : m + 4]
-    scratch = refs[m + 4 :]
+    dagg, own_radial, columns, offsets = refs[:4]
+    made = refs[4:6] if ahead else ()
+    refs = refs[4 + len(made) :]
+    turned, terms, spread = refs[:3]
+    scratch = refs[3:]
     me = lax.axis_index("fsdp")
     atoms = columns.shape[0] // n
-    rows = channels // n
-    spread[...] = jnp.zeros_like(spread)
-    reach = atoms + 2 * margin
+    tile = 2 * margin
+    spread[0, n * atoms :] = jnp.zeros_like(spread[0, n * atoms :])
+    spread[1, :tile] = jnp.zeros_like(spread[1, :tile])
     if ahead:
         values, place = made
     else:
@@ -331,19 +334,23 @@
         flow = dagg[rows_at(e, atoms)]
         if ahead:
             own_values = values.at[rows_at(e, atoms)]
-            own_place = place[rows_at(e, reach)]
+            own_place = place.at[rows_at(e, 2 * atoms)]
         else:
             own_values = values
             fill_values(columns[rows_at(e, atoms)], filters, values)
             fill_place(margin, neighbors, offsets[rows_at(e, SLOT)], place)
-            own_place = place[...]
-        own = terms.at[e % terms.shape[0]]
-        for k in range(neighbors):
-            own[k * atoms : (k + 1) * atoms] = (
-                own_values[:, k * LANES : (k + 1) * LANES] * flow
-            ).astype(bf16)
-        window = pl.ds(pl.multiple_of(e * atoms, atoms), reach)
-        spread[window] += jnp.dot(own_place, own[...], preferred_element_type=f32)
+            own_place = place
+        for t in range(2):
+            own = terms.at[2 * (e % (terms.shape[0] // 2)) + t]
+            here = slice(t * tile, (t + 1) * tile)
+            for k in range(neighbors):
+                own[k * tile : (k + 1) * tile] = (
+                    own_values[here, k * LANES : (k + 1) * LANES] * flow[here]
+                ).astype(bf16)
+            window = pl.ds(pl.multiple_of(e * atoms + t * tile, tile), 2 * tile)
+            spread[t, window] = jnp.dot(
+                own_place[t * 2 * tile : (t + 1) * 2 * tile], own[...], preferred_element_type=f32
+            )
         return 0
 
     lax.fori_loop(0, n, block_step, 0, unroll=min(n, 8) if ahead else 1)
@@ -354,10 +361,17 @@
             e = me ^ (2 * c + k)
             start = pl.multiple_of(e * atoms + margin, margin)
             turned[:, k * half + c * atoms : k * half + (c + 1) * atoms] = (
-                spread[pl.ds(start, atoms)].T.astype(bf16)
+                (spread[0, pl.ds(start, atoms)] + spread[1, pl.ds(start, atoms)]).T.astype(bf16)
             )
-    total = jnp.dot(turned[:, :half], feats[0][...], preferred_element_type=f32)
-    total = total + jnp.dot(turned[:, half:], feats[1][...], preferred_element_type=f32)
+
+
+def gradient_kernel(n, rows, turned, own_feats, other_feats, *refs):
+    m = n // 2
+    sends, grads = refs[:m], refs[m]
+    me = lax.axis_index("fsdp")
+    half = own_feats.shape[0]
+    total = jnp.dot(turned[:, :half], own_feats[...], preferred_element_type=f32)
+    total = total + jnp.dot(turned[:, half:], other_feats[...], preferred_element_type=f32)
     for q in range(total.shape[1] // LANES):
         grads[q * LANES : (q + 1) * LANES] = total[:, q * LANES : (q + 1) * LANES].T.astype(bf16)
     for c in range(m):
@@ -381,7 +395,7 @@
     cots, sends, (own, give) = refs[6 : 6 + m], refs[6 + m : 6 + 2 * m], refs[6 + 2 * m :]
     me = lax.axis_index("fsdp")
     atoms = cots[0].shape[0]
-    rows = give.shape[0]
+    rows = own.shape[0]
     at = column_of(neighbors, neighbors)
     totals = [None, None]
     for c in range(m):
@@ -396,24 +410,28 @@
             term = jnp.dot(left, cots[c][...], preferred_element_type=f32)
             totals[i] = term if c == 0 else totals[i] + term
     own[...] = totals[0][:rows]
-    give[...] = totals[1][:rows].astype(bf16)
+    for q in range(own.shape[1] // LANES):
+        give[q * rows : (q + 1) * rows] = totals[1][:rows, q * LANES : (q + 1) * LANES].astype(bf16)
 
 
 def grads_kernel(n, fragment, *refs):
     m = n // 2
-    near, far, own_part, got_part = refs[:m], refs[m:n], refs[n], refs[n + 1]
-    msg_grad, out_grad, code, blocks, total = refs[n + 2 :]
+    near, far, own_part = refs[:m], refs[m], refs[m + 1]
+    msg_grad, out_grad, code, blocks, total = refs[m + 2 :]
     me = lax.axis_index("fsdp")
     rows = msg_grad.shape[1]
     width = msg_grad.shape[2] // n
     lanes = pl.ds(pl.multiple_of(fragment[0] * FRAG, FRAG), FRAG)
     for c in range(m):
         blocks[me ^ (2 * c)] = near[c][:rows]
-        blocks[me ^ (2 * c + 1)] = far[c][rows:]
+        blocks[me ^ (2 * c + 1)] = far[c * rows : (c + 1) * rows]
     for e in range(n):
         msg_grad[0, :, e * width : (e + 1) * width] = blocks[e][:, :width]
     write_code(msg_grad[0, :, lanes].astype(f32), code.at[: rows + SLOT])
-    total[...] = own_part[...] + got_part[...].astype(f32)
+    for q in range(total.shape[1] // LANES):
+        part = slice(q * LANES, (q + 1) * LANES)
+        start = (m + q) * rows
+        total[:, part] = own_part[:, part] + far[start : start + rows].astype(f32)
     out_grad[0] = total[...].astype(bf16)
     write_code(total[:, lanes], code.at[rows + SLOT :])
 
@@ -483,11 +501,6 @@
     return [[pieces[c] for c in range(n // 2)] for pieces in found]
 
 
-def from_chips(sends):
-    near = across_chips(sends)
-    return near, [hop(value, "fsdp", 1) for value in near]
-
-
 def shards(
     node_feats,
     neighbor_src,
@@ -508,7 +521,6 @@
     rows = msg_weight.shape[0]
     width = channels // n
     margin = atoms // 4
-    reach = atoms + 2 * margin
     norm = 1.0 / math.sqrt(neighbors)
     all_atoms = n * atoms
     lanes = neighbors * LANES
@@ -559,7 +571,7 @@
         + [
             ((all_atoms, lanes), f32),
             ((n * neighbors * 2 * margin, 8 * margin), bf16),
-            ((n * reach, neighbors * atoms), bf16),
+            ((2 * all_atoms, neighbors * 2 * margin), bf16),
         ]
         * ahead,
         [
@@ -597,49 +609,55 @@
             ((all_atoms // 2, LANES), bf16),
             ((all_atoms, LANES), f32),
         ],
-        [((all_atoms + 2 * margin, LANES), bf16)]
+        [((all_atoms + 2 * margin, LANES), bf16), ((all_atoms, LANES), bf16)]
         + (step_scratch + [((neighbors * 2 * margin, 8 * margin), bf16)]) * (not ahead),
         [own_products, got_products, columns, own_radial, *made[:2]],
         1,
         memory,
     )
     other_act = hop(give, "fsdp", 1)
+    (turned,) = run(
+        functools.partial(backward_kernel, n, margin, neighbors, ahead),
+        [((LANES, all_atoms), bf16)],
+        [
+            ((2 * min(n, 8) if ahead else 2, neighbors * 2 * margin, LANES), bf16),
+            ((2, all_atoms + 2 * margin, LANES), f32),
+        ]
+        + (step_scratch + [((2 * atoms, neighbors * 2 * margin), bf16)]) * (not ahead),
+        [dagg, own_radial, columns, offsets, *made[::2]],
+        1,
+        memory,
+    )
     grad_sends = run(
-        functools.partial(backward_kernel, n, margin, neighbors, channels, ahead),
+        functools.partial(gradient_kernel, n, rows),
         [((2 * rows, LANES), bf16)] * m,
-        [
-            ((min(n, 8) if ahead else 1, neighbors * atoms, LANES), bf16),
-            ((all_atoms + 2 * margin, LANES), f32),
-            ((LANES, all_atoms), bf16),
-            ((channels, LANES), bf16),
-        ]
-        + (step_scratch + [((reach, neighbors * atoms), bf16)]) * (not ahead),
-        [
-            held_feats,
-            hop(held_feats, "fsdp", 1),
-            dagg,
-            own_radial,
-            columns,
-            offsets,
-            *made[::2],
-        ],
-        4,
-        memory,
-    )
-    near, far = from_chips(grad_sends)
+        [((channels, LANES), bf16)],
+        [turned, held_feats, hop(held_feats, "fsdp", 1)],
+        1,
+        memory,
+    )
+    near = across_chips(grad_sends)
     *sums, own_part, give_part = run(
         functools.partial(chip_kernel, n, margin, neighbors, width),
-        [((atoms, channels), bf16)] * m + [((rows, channels), f32), ((rows, channels), bf16)],
+        [((atoms, channels), bf16)] * m + [((rows, channels), f32), ((channels // LANES * rows, LANES), bf16)],
         [],
         [columns, keep, other_act, out_weight, other_weight, grad_sends[0], *cots],
         1,
+        memory,
+    )
+    (swap,) = run(
+        swap_kernel,
+        [(((m + channels // LANES) * rows, LANES), bf16)],
+        [],
+        [*near, give_part],
+        0,
         memory,
     )
     grad_msg, grad_out, code = run(
         functools.partial(grads_kernel, n),
         [((1, rows, channels), bf16)] * 2 + [((2 * (rows + SLOT), FRAG), bf16)],
         [((n, rows, LANES), bf16), ((rows, channels), f32)],
-        [fragment, *near, *far, own_part, hop(give_part, "fsdp", 1)],
+        [fragment, *near, hop(swap, "fsdp", 1), own_part],
         1,
         memory,
         scalars=1,

time: 65.7 us -> 63.5 us (0.967)
  Pallas kernels: 17 us -> 14.3 us
  waiting for transfers between devices: 20.7 us -> 21.4 us
    pallas_call x11 -> x13, Pallas kernels: 17 us -> 14.3 us  [run(): pl.pallas_call(kernel, out_shape=[jax.ShapeDtypeStruct(shape, dtype) for...]
    ppermute x27 -> x23, waiting for transfers between devices: 20.7 us -> 21.4 us  [hop(): return lax.ppermute(value, axis, [(i, i ^ step) for i in range(count)])]
    ppermute x27 -> x23, starting transfers between devices: 24.9 us -> 24.5 us  [hop(): return lax.ppermute(value, axis, [(i, i ^ step) for i in range(count)])]
    unnamed x10 -> x12, local copies, waits for them, and re-layouts: 1.57 us -> 1.59 us
  transfers between devices with their start and end apart: 27 -> 23, of which waited for: 13 -> 9; matrix products, arithmetic and copies ran while one was open for 0% -> 0% of each run, Pallas kernels for 21% -> 20%
where the time goes in v4:
time: 63.5 us; the launch traced here: 63.3 us
  starting transfers between devices  24.5 us (39%)
  waiting for transfers between devices  21.4 us (34%)
  Pallas kernels  14.3 us (23%)
  local copies, waits for them, and re-layouts  1.59 us (3%)
  between operations  1.48 us (2%)
    ppermute x23, starting transfers between devices, hop(): return lax.ppermute(value, axis, [(i, i ^ step) for i in range(count)])  24.5 us
    ppermute x23, waiting for transfers between devices, hop(): return lax.ppermute(value, axis, [(i, i ^ step) for i in range(count)])  21.4 us
    pallas_call x13, Pallas kernels, run(): pl.pallas_call(kernel, out_shape=[jax.ShapeDtypeStruct(shape, dtype) for...  14.3 us
    unnamed x12, local copies, waits for them, and re-layouts  1.59 us
  transfers between devices with their start and end apart: 23, of which 9 were waited for; matrix products, arithmetic and copies ran while one was open for 0% of the time, Pallas kernels for 20%

profile of v4, /device:TPU:0, one launch (start us, length us, event | category | flops | bytes accessed | tf_op | source)
XLA Modules:
  0.0 63.3 jit_solution(14809859853485294075)
XLA Ops:
  0.7 3.0 %collective-permute-start.3 = (bf16[128,1024]{1,0:T(8,128)(2,1)}, bf16[128,1024]{1,0:T(8,128)(2,1)S(1)}, u32[]{:S(2)}, u32[]{:S(2)}) collective-permute-start(bf16[128,1024]{1,0:T(8,128)(2,1)} %feats.1), channel_id=1, source_target_pairs={{0,4},{1,5},{2,6},{3,7},{4,0},{5,1},{6,2},{7,3},{8,12},{9,13},{10,... | collective-permute-start | bytes 786440 | tf_op jit(solution)/shard_map/ppermute | solution.py:487
  3.7 1.5 %collective-permute-start.4 = (bf16[128,1024]{1,0:T(8,128)(2,1)}, bf16[128,1024]{1,0:T(8,128)(2,1)S(1)}, u32[]{:S(2)}, u32[]{:S(2)}) collective-permute-start(bf16[128,1024]{1,0:T(8,128)(2,1)} %refs_6_.1), channel_id=1, source_target_pairs={{0,2},{1,3},{2,0},{3,1},{4,6},{5,7},{6,4},{7,5},{8,10},{9,11},{10,... | collective-permute-start | bytes 786440 | tf_op jit(solution)/shard_map/ppermute | solution.py:487
  5.2 1.8 %shard_map.120 = (bf16[320,128]{1,0:T(8,128)(2,1)}, bf16[320,128]{1,0:T(8,128)(2,1)}, bf16[320,128]{1,0:T(8,128)(2,1)}, bf16[320,128]{1,0:T(8,128)(2,1)}, f32[8,128]{1,0:T(8,128)}) custom-call(bf16[128,1024]{1,0:T(8,128)(2,1)} %refs_0_.2, s32[12,128]{1,0:T(8,128)} %refs_1_.1, f32[12,128]{1,0:T(8,128)} %refs_2_.1, s32[1,128]{1,0:T(1,128)} %refs_3_.2, ...), custom_call_target="tpu_custom_call" | custom-call | flops 1000000000 | bytes 3000000 | tf_op jit(solution)/shard_map/pallas_call | solution.py:467
  7.7 2.9 %collective-permute-start.2 = (bf16[320,128]{1,0:T(8,128)(2,1)}, bf16[320,128]{1,0:T(8,128)(2,1)S(1)}, u32[]{:S(2)}, u32[]{:S(2)}) collective-permute-start(bf16[320,128]{1,0:T(8,128)(2,1)} %get-tuple-element.37), channel_id=1, source_target_pairs={{0,6},{1,7},{2,4},{3,5},{4,2},{5,3},{6,0},{7,1},{8,14},{9,15},{10,... | collective-permute-start | bytes 245768 | tf_op jit(solution)/shard_map/ppermute | solution.py:487
  10.5 3.8 %collective-permute-done.refs_1_ = bf16[320,128]{1,0:T(8,128)(2,1)S(1)} collective-permute-done((bf16[320,128]{1,0:T(8,128)(2,1)}, bf16[320,128]{1,0:T(8,128)(2,1)S(1)}, u32[]{:S(2)}, u32[]{:S(2)}) %collective-permute-start) | collective-permute-done | bytes 81952 | tf_op jit(solution)/shard_map/ppermute | solution.py:487
  16.0 1.7 %collective-permute-start.7 = (bf16[128,1024]{1,0:T(8,128)(2,1)S(1)}, bf16[128,1024]{1,0:T(8,128)(2,1)S(1)}, u32[]{:S(2)}, u32[]{:S(2)}) collective-permute-start(bf16[128,1024]{1,0:T(8,128)(2,1)S(1)} %copy-done.5), channel_id=1, source_target_pairs={{0,2},{1,3},{2,0},{3,1},{4,6},{5,7},{6,4},{7,5},{8,10},{9,11},{10,... | collective-permute-start | bytes 786440 | tf_op jit(solution)/shard_map/ppermute | solution.py:487
  17.9 1.5 %collective-permute-start.9 = (bf16[128,1024]{1,0:T(8,128)(2,1)S(1)}, bf16[128,1024]{1,0:T(8,128)(2,1)S(1)}, u32[]{:S(2)}, u32[]{:S(2)}) collective-permute-start(bf16[128,1024]{1,0:T(8,128)(2,1)S(1)} %copy-done.3), channel_id=1, source_target_pairs={{0,4},{1,5},{2,6},{3,7},{4,0},{5,1},{6,2},{7,3},{8,12},{9,13},{10,... | collective-permute-start | bytes 786440 | tf_op jit(solution)/shard_map/ppermute | solution.py:487
  21.0 4.1 %shard_map.122 = (bf16[1024,256]{1,0:T(8,128)(2,1)S(1)}, f32[1024,128]{1,0:T(8,128)S(1)}, f32[128,128]{1,0:T(8,128)S(1)}, f32[1024,1536]{1,0:T(8,128)S(1)}, bf16...) custom-call(bf16[320,128]{1,0:T(8,128)(2,1)S(1)} %copy-done, bf16[320,128]{1,0:T(8,128)(2,1)S(1)} %collective-permute-done.refs_1_, ...), custom_call_target="tpu_custom_call" | custom-call | tf_op jit(solution)/shard_map/pallas_call | solution.py:467
  25.2 1.8 %collective-permute-done.9.refs_6_.refs_8_ = bf16[128,1024]{1,0:T(8,128)(2,1)S(1)} collective-permute-done((bf16[128,1024]{1,0:T(8,128)(2,1)S(1)}, bf16[128,1024]{1,0:T(8,128)(2,1)S(1)}, u32[]{:S(2)}, u32[]{:S(2)}) %collective-permute-start.9) | collective-permute-done | bytes 262176 | tf_op jit(solution)/shard_map/ppermute | solution.py:487
  27.0 3.3 %collective-permute-done.8.refs_3_ = bf16[128,1024]{1,0:T(8,128)(2,1)S(1)} collective-permute-done((bf16[128,1024]{1,0:T(8,128)(2,1)S(1)}, bf16[128,1024]{1,0:T(8,128)(2,1)S(1)}, u32[]{:S(2)}, u32[]{:S(2)}) %collective-permute-start.8) | collective-permute-done | bytes 262176 | tf_op jit(solution)/shard_map/ppermute | solution.py:487
  30.3 1.7 %collective-permute-done.10.refs_7_.refs_9_ = bf16[128,1024]{1,0:T(8,128)(2,1)S(1)} collective-permute-done((bf16[128,1024]{1,0:T(8,128)(2,1)S(1)}, bf16[128,1024]{1,0:T(8,128)(2,1)S(1)}, u32[]{:S(2)}, u32[]{:S(2)}) %collective-permute-start.10) | collective-permute-done | bytes 262176 | tf_op jit(solution)/shard_map/ppermute | solution.py:487
  33.2 1.5 %collective-permute-done.11.refs_1_._after = bf16[1024,128]{1,0:T(8,128)(2,1)S(1)} collective-permute-done((bf16[1024,128]{1,0:T(8,128)(2,1)S(1)}, bf16[1024,128]{1,0:T(8,128)(2,1)S(1)}, u32[]{:S(2)}, u32[]{:S(2)}) %collective-permute-start.11) | collective-permute-done | bytes 262176 | tf_op jit(solution)/shard_map/ppermute | solution.py:487
  34.9 1.2 %shard_map.124 = (bf16[512,128]{1,0:T(8,128)(2,1)S(1)}, bf16[512,128]{1,0:T(8,128)(2,1)S(1)}, f32[1024,128]{1,0:T(8,128)S(1)}) custom-call(bf16[1024,128]{1,0:T(8,128)(2,1)S(1)} %get-tuple-element.41.refs_0_, bf16[1024,128]{1,0:T(8,128)(2,1)S(1)} %collective-permute-done.11.refs_1_._after, f32[1024,128]{1,0:T(8,128)S(1)} %get-tuple-element.39.refs_2_.refs_0_, ...), custom_call_target="tpu_custom_call" | custom-call | flops 1000000000 | bytes 3000000 | tf_op jit(solution)/shard_map/pallas_call | solution.py:467
  36.6 1.7 %shard_map.125.turned = bf16[128,1024]{1,0:T(8,128)(2,1)S(1)} custom-call(f32[1024,128]{1,0:T(8,128)S(1)} %get-tuple-element.47.refs_0_, f32[8,128]{1,0:T(8,128)S(1)} %copy-done.2, f32[1024,128]{1,0:T(8,128)S(1)} %get-tuple-element.39.refs_2_.refs_0_, f32[128,128]{1,0:T(8,128)S(1)} %get-tuple-element.48.refs_3_, f32[1024,1536]{1,0:T(8,128)S(1)} %get-tuple-element.43.refs_4_, ...), custom_call_target="tpu_custom_call" | custom-call | flops 1000000000 | bytes 3000000 | tf_op jit(solution)/shard_map/pallas_call | solution.py:467
  39.2 1.7 %collective-permute-start.18 = (bf16[256,128]{1,0:T(8,128)(2,1)S(1)}, bf16[256,128]{1,0:T(8,128)(2,1)S(1)}, u32[]{:S(2)}, u32[]{:S(2)}) collective-permute-start(bf16[256,128]{1,0:T(8,128)(2,1)S(1)} %get-tuple-element.57), channel_id=1, source_target_pairs={{0,4},{1,5},{2,6},{3,7},{4,0},{5,1},{6,2},{7,3},{8,12},{9,13},{10,... | collective-permute-start | bytes 196616 | tf_op jit(solution)/shard_map/ppermute | solution.py:487
  40.9 1.4 %collective-permute-start.19 = (bf16[256,128]{1,0:T(8,128)(2,1)S(1)}, bf16[256,128]{1,0:T(8,128)(2,1)S(1)}, u32[]{:S(2)}, u32[]{:S(2)}) collective-permute-start(bf16[256,128]{1,0:T(8,128)(2,1)S(1)} %get-tuple-element.58), channel_id=1, source_target_pairs={{0,6},{1,7},{2,4},{3,5},{4,2},{5,3},{6,0},{7,1},{8,14},{9,15},{10,... | collective-permute-start | bytes 196616 | tf_op jit(solution)/shard_map/ppermute | solution.py:487
  42.4 1.2 %shard_map.128 = (bf16[128,1024]{1,0:T(8,128)(2,1)S(1)}, bf16[128,1024]{1,0:T(8,128)(2,1)S(1)}, bf16[128,1024]{1,0:T(8,128)(2,1)S(1)}, bf16[128,1024]{1,0:T(8,12...) custom-call(f32[1024,128]{1,0:T(8,128)S(1)} %get-tuple-element.39.refs_2_.refs_0_, ...), custom_call_target="tpu_custom_call" | custom-call | flops 1000000000 | bytes 3000000 | tf_op jit(solution)/shard_map/pallas_call | solution.py:467
  43.6 2.5 %collective-permute-done.19.refs_3_ = bf16[256,128]{1,0:T(8,128)(2,1)S(1)} collective-permute-done((bf16[256,128]{1,0:T(8,128)(2,1)S(1)}, bf16[256,128]{1,0:T(8,128)(2,1)S(1)}, u32[]{:S(2)}, u32[]{:S(2)}) %collective-permute-start.19) | collective-permute-done | bytes 65568 | tf_op jit(solution)/shard_map/ppermute | solution.py:487
  46.2 1.6 %collective-permute-start.14 = (bf16[128,1024]{1,0:T(8,128)(2,1)S(1)}, bf16[128,1024]{1,0:T(8,128)(2,1)S(1)}, u32[]{:S(2)}, u32[]{:S(2)}) collective-permute-start(bf16[128,1024]{1,0:T(8,128)(2,1)S(1)} %get-tuple-element.53), channel_id=1, source_target_pairs={{0,2},{1,3},{2,0},{3,1},{4,6},{5,7},{6,4},{7,5},{8,10},{9,11},{10,... | collective-permute-start | bytes 786440 | tf_op jit(solution)/shard_map/ppermute | solution.py:487
  48.3 1.5 %collective-permute-start.16 = (bf16[128,1024]{1,0:T(8,128)(2,1)S(1)}, bf16[128,1024]{1,0:T(8,128)(2,1)S(1)}, u32[]{:S(2)}, u32[]{:S(2)}) collective-permute-start(bf16[128,1024]{1,0:T(8,128)(2,1)S(1)} %get-tuple-element.55), channel_id=1, source_target_pairs={{0,6},{1,7},{2,4},{3,5},{4,2},{5,3},{6,0},{7,1},{8,14},{9,15},{10,... | collective-permute-start | bytes 786440 | tf_op jit(solution)/shard_map/ppermute | solution.py:487
  51.3 1.6 %collective-permute-start.21 = (bf16[288,128]{1,0:T(8,128)(2,1)S(1)}, bf16[288,128]{1,0:T(8,128)(2,1)S(1)}, u32[]{:S(2)}, u32[]{:S(2)}) collective-permute-start(bf16[288,128]{1,0:T(8,128)(2,1)S(1)} %get-tuple-element.63.refs_0_), channel_id=1, source_target_pairs={{0,8},{8,0},{16,24},{24,16},{1,9},{9,1},{17,25},{25,17},{2,10},{10... | collective-permute-start | bytes 221192 | tf_op jit(solution)/shard_map/ppermute | solution.py:487
  52.9 2.8 %collective-permute-done.21.refs_1_ = bf16[288,128]{1,0:T(8,128)(2,1)S(1)} collective-permute-done((bf16[288,128]{1,0:T(8,128)(2,1)S(1)}, bf16[288,128]{1,0:T(8,128)(2,1)S(1)}, u32[]{:S(2)}, u32[]{:S(2)}) %collective-permute-start.21) | collective-permute-done | bytes 73760 | tf_op jit(solution)/shard_map/ppermute | solution.py:487
  55.8 2.7 %collective-permute-start.22 = (bf16[2,128,128]{2,1,0:T(8,128)(2,1)S(1)}, bf16[2,128,128]{2,1,0:T(8,128)(2,1)S(1)}, u32[]{:S(2)}, u32[]{:S(2)}) collective-permute-start(bf16[2,128,128]{2,1,0:T(8,128)(2,1)S(1)} %shard_map.132.own), channel_id=1, source_target_pairs={{0,16},{8,24},{16,0},{24,8},{1,17},{9,25},{17,1},{25,9},{2,18},{10... | collective-permute-start | bytes 196616 | tf_op jit(solution)/shard_map/ppermute | solution.py:487
  58.5 3.3 %collective-permute-done.15.refs_2_ = bf16[128,1024]{1,0:T(8,128)(2,1)S(1)} collective-permute-done((bf16[128,1024]{1,0:T(8,128)(2,1)S(1)}, bf16[128,1024]{1,0:T(8,128)(2,1)S(1)}, u32[]{:S(2)}, u32[]{:S(2)}) %collective-permute-start.15) | collective-permute-done | bytes 262176 | tf_op jit(solution)/shard_map/ppermute | solution.py:487
  (48 shorter events, 10.1 us)
Async XLA Ops:
  0.6 17.2 %copy-start.3 = (bf16[128,1024]{1,0:T(8,128)(2,1)S(1)}, bf16[128,1024]{1,0:T(8,128)(2,1)}, u32[]{:S(2)}) copy-start(bf16[128,1024]{1,0:T(8,128)(2,1)} %refs_6_.1) | copy-start | bytes 786436
  0.7 14.3 %collective-permute-start.3 = (bf16[128,1024]{1,0:T(8,128)(2,1)}, bf16[128,1024]{1,0:T(8,128)(2,1)S(1)}, u32[]{:S(2)}, u32[]{:S(2)}) collective-permute-start(bf16[128,1024]{1,0:T(8,128)(2,1)} %feats.1), channel_id=1, source_target_pairs={{0,4},{1,5},{2,6},{3,7},{4,0},{5,1},{6,2},{7,3},{8,12},{9,13},{10,... | collective-permute-start | bytes 786440 | tf_op jit(solution)/shard_map/ppermute | solution.py:487
  3.7 11.3 %collective-permute-start.4 = (bf16[128,1024]{1,0:T(8,128)(2,1)}, bf16[128,1024]{1,0:T(8,128)(2,1)S(1)}, u32[]{:S(2)}, u32[]{:S(2)}) collective-permute-start(bf16[128,1024]{1,0:T(8,128)(2,1)} %refs_6_.1), channel_id=1, source_target_pairs={{0,2},{1,3},{2,0},{3,1},{4,6},{5,7},{6,4},{7,5},{8,10},{9,11},{10,... | collective-permute-start | bytes 786440 | tf_op jit(solution)/shard_map/ppermute | solution.py:487
  7.0 7.3 %collective-permute-start = (bf16[320,128]{1,0:T(8,128)(2,1)}, bf16[320,128]{1,0:T(8,128)(2,1)S(1)}, u32[]{:S(2)}, u32[]{:S(2)}) collective-permute-start(bf16[320,128]{1,0:T(8,128)(2,1)} %get-tuple-element.35), channel_id=1, source_target_pairs={{0,2},{1,3},{2,0},{3,1},{4,6},{5,7},{6,4},{7,5},{8,10},{9,11},{10,... | collective-permute-start | bytes 245768 | tf_op jit(solution)/shard_map/ppermute | solution.py:487
  7.6 6.7 %collective-permute-start.1 = (bf16[320,128]{1,0:T(8,128)(2,1)}, bf16[320,128]{1,0:T(8,128)(2,1)S(1)}, u32[]{:S(2)}, u32[]{:S(2)}) collective-permute-start(bf16[320,128]{1,0:T(8,128)(2,1)} %get-tuple-element.36), channel_id=1, source_target_pairs={{0,4},{1,5},{2,6},{3,7},{4,0},{5,1},{6,2},{7,3},{8,12},{9,13},{10,... | collective-permute-start | bytes 245768 | tf_op jit(solution)/shard_map/ppermute | solution.py:487
  7.7 7.3 %collective-permute-start.2 = (bf16[320,128]{1,0:T(8,128)(2,1)}, bf16[320,128]{1,0:T(8,128)(2,1)S(1)}, u32[]{:S(2)}, u32[]{:S(2)}) collective-permute-start(bf16[320,128]{1,0:T(8,128)(2,1)} %get-tuple-element.37), channel_id=1, source_target_pairs={{0,6},{1,7},{2,4},{3,5},{4,2},{5,3},{6,0},{7,1},{8,14},{9,15},{10,... | collective-permute-start | bytes 245768 | tf_op jit(solution)/shard_map/ppermute | solution.py:487
  15.9 4.0 %collective-permute-start.5 = (bf16[1280,128]{1,0:T(8,128)(2,1)S(1)}, bf16[1280,128]{1,0:T(8,128)(2,1)S(1)}, u32[]{:S(2)}, u32[]{:S(2)}) collective-permute-start(bf16[1280,128]{1,0:T(8,128)(2,1)S(1)} %shard_map.121), channel_id=1, source_target_pairs={{0,1},{1,0},{2,3},{3,2},{4,5},{5,4},{6,7},{7,6},{8,9},{9,8},{10,11... | collective-permute-start | bytes 983048 | tf_op jit(solution)/shard_map/ppermute | solution.py:487
  16.0 9.2 %collective-permute-start.7 = (bf16[128,1024]{1,0:T(8,128)(2,1)S(1)}, bf16[128,1024]{1,0:T(8,128)(2,1)S(1)}, u32[]{:S(2)}, u32[]{:S(2)}) collective-permute-start(bf16[128,1024]{1,0:T(8,128)(2,1)S(1)} %copy-done.5), channel_id=1, source_target_pairs={{0,2},{1,3},{2,0},{3,1},{4,6},{5,7},{6,4},{7,5},{8,10},{9,11},{10,... | collective-permute-start | bytes 786440 | tf_op jit(solution)/shard_map/ppermute | solution.py:487
  17.7 7.4 %collective-permute-start.6 = (bf16[128,1024]{1,0:T(8,128)(2,1)S(1)}, bf16[128,1024]{1,0:T(8,128)(2,1)S(1)}, u32[]{:S(2)}, u32[]{:S(2)}) collective-permute-start(bf16[128,1024]{1,0:T(8,128)(2,1)S(1)} %copy-done.4), channel_id=1, source_target_pairs={{0,1},{1,0},{2,3},{3,2},{4,5},{5,4},{6,7},{7,6},{8,9},{9,8},{10,11... | collective-permute-start | bytes 786440 | tf_op jit(solution)/shard_map/ppermute | solution.py:487
  17.9 9.1 %collective-permute-start.9 = (bf16[128,1024]{1,0:T(8,128)(2,1)S(1)}, bf16[128,1024]{1,0:T(8,128)(2,1)S(1)}, u32[]{:S(2)}, u32[]{:S(2)}) collective-permute-start(bf16[128,1024]{1,0:T(8,128)(2,1)S(1)} %copy-done.3), channel_id=1, source_target_pairs={{0,4},{1,5},{2,6},{3,7},{4,0},{5,1},{6,2},{7,3},{8,12},{9,13},{10,... | collective-permute-start | bytes 786440 | tf_op jit(solution)/shard_map/ppermute | solution.py:487
  19.4 10.9 %collective-permute-start.8 = (bf16[128,1024]{1,0:T(8,128)(2,1)S(1)}, bf16[128,1024]{1,0:T(8,128)(2,1)S(1)}, u32[]{:S(2)}, u32[]{:S(2)}) collective-permute-start(bf16[128,1024]{1,0:T(8,128)(2,1)S(1)} %collective-permute-done.3.refs_4_.refs_2_), channel_id=1, source_target_pairs={{0,2},{1,3},{2,0},{3,1},{4,6},{5,7},{6,4},{7,5},{8,10},{9,11},{10,... | collective-permute-start | bytes 786440 | tf_op jit(solution)/shard_map/ppermute | solution.py:487
  19.9 12.1 %collective-permute-start.10 = (bf16[128,1024]{1,0:T(8,128)(2,1)S(1)}, bf16[128,1024]{1,0:T(8,128)(2,1)S(1)}, u32[]{:S(2)}, u32[]{:S(2)}) collective-permute-start(bf16[128,1024]{1,0:T(8,128)(2,1)S(1)} %collective-permute-done.4.refs_5_.refs_7_), channel_id=1, source_target_pairs={{0,4},{1,5},{2,6},{3,7},{4,0},{5,1},{6,2},{7,3},{8,12},{9,13},{10,... | collective-permute-start | bytes 786440 | tf_op jit(solution)/shard_map/ppermute | solution.py:487
  33.2 1.6 %collective-permute-start.11 = (bf16[1024,128]{1,0:T(8,128)(2,1)S(1)}, bf16[1024,128]{1,0:T(8,128)(2,1)S(1)}, u32[]{:S(2)}, u32[]{:S(2)}) collective-permute-start(bf16[1024,128]{1,0:T(8,128)(2,1)S(1)} %get-tuple-element.42), channel_id=1, source_target_pairs={{0,1},{1,0},{2,3},{3,2},{4,5},{5,4},{6,7},{7,6},{8,9},{9,8},{10,11... | collective-permute-start | bytes 786440 | tf_op jit(solution)/shard_map/ppermute | solution.py:487
  34.8 3.5 %collective-permute-start.13 = (bf16[512,1024]{1,0:T(8,128)(2,1)S(1)}, bf16[512,1024]{1,0:T(8,128)(2,1)S(1)}, u32[]{:S(2)}, u32[]{:S(2)}) collective-permute-start(bf16[512,1024]{1,0:T(8,128)(2,1)S(1)} %shard_map.126.own_feats), channel_id=1, source_target_pairs={{0,1},{1,0},{2,3},{3,2},{4,5},{5,4},{6,7},{7,6},{8,9},{9,8},{10,11... | collective-permute-start | bytes 3145736 | tf_op jit(solution)/shard_map/ppermute | solution.py:487
  36.1 6.2 %collective-permute-start.12 = (bf16[512,128]{1,0:T(8,128)(2,1)S(1)}, bf16[512,128]{1,0:T(8,128)(2,1)S(1)}, u32[]{:S(2)}, u32[]{:S(2)}) collective-permute-start(bf16[512,128]{1,0:T(8,128)(2,1)S(1)} %get-tuple-element.46), channel_id=1, source_target_pairs={{0,1},{1,0},{2,3},{3,2},{4,5},{5,4},{6,7},{7,6},{8,9},{9,8},{10,11... | collective-permute-start | bytes 393224 | tf_op jit(solution)/shard_map/ppermute | solution.py:487
  38.8 4.8 %collective-permute-start.17 = (bf16[256,128]{1,0:T(8,128)(2,1)S(1)}, bf16[256,128]{1,0:T(8,128)(2,1)S(1)}, u32[]{:S(2)}, u32[]{:S(2)}) collective-permute-start(bf16[256,128]{1,0:T(8,128)(2,1)S(1)} %get-tuple-element.56), channel_id=1, source_target_pairs={{0,2},{1,3},{2,0},{3,1},{4,6},{5,7},{6,4},{7,5},{8,10},{9,11},{10,... | collective-permute-start | bytes 196616 | tf_op jit(solution)/shard_map/ppermute | solution.py:487
  39.2 4.4 %collective-permute-start.18 = (bf16[256,128]{1,0:T(8,128)(2,1)S(1)}, bf16[256,128]{1,0:T(8,128)(2,1)S(1)}, u32[]{:S(2)}, u32[]{:S(2)}) collective-permute-start(bf16[256,128]{1,0:T(8,128)(2,1)S(1)} %get-tuple-element.57), channel_id=1, source_target_pairs={{0,4},{1,5},{2,6},{3,7},{4,0},{5,1},{6,2},{7,3},{8,12},{9,13},{10,... | collective-permute-start | bytes 196616 | tf_op jit(solution)/shard_map/ppermute | solution.py:487
  40.9 5.2 %collective-permute-start.19 = (bf16[256,128]{1,0:T(8,128)(2,1)S(1)}, bf16[256,128]{1,0:T(8,128)(2,1)S(1)}, u32[]{:S(2)}, u32[]{:S(2)}) collective-permute-start(bf16[256,128]{1,0:T(8,128)(2,1)S(1)} %get-tuple-element.58), channel_id=1, source_target_pairs={{0,6},{1,7},{2,4},{3,5},{4,2},{5,3},{6,0},{7,1},{8,14},{9,15},{10,... | collective-permute-start | bytes 196616 | tf_op jit(solution)/shard_map/ppermute | solution.py:487
  46.1 4.3 %collective-permute-start.20 = (bf16[1536,128]{1,0:T(8,128)(2,1)S(1)}, bf16[1536,128]{1,0:T(8,128)(2,1)S(1)}, u32[]{:S(2)}, u32[]{:S(2)}) collective-permute-start(bf16[1536,128]{1,0:T(8,128)(2,1)S(1)} %shard_map.130), channel_id=1, source_target_pairs={{0,1},{1,0},{2,3},{3,2},{4,5},{5,4},{6,7},{7,6},{8,9},{9,8},{10,11... | collective-permute-start | bytes 1179656 | tf_op jit(solution)/shard_map/ppermute | solution.py:487
  46.2 12.3 %collective-permute-start.14 = (bf16[128,1024]{1,0:T(8,128)(2,1)S(1)}, bf16[128,1024]{1,0:T(8,128)(2,1)S(1)}, u32[]{:S(2)}, u32[]{:S(2)}) collective-permute-start(bf16[128,1024]{1,0:T(8,128)(2,1)S(1)} %get-tuple-element.53), channel_id=1, source_target_pairs={{0,2},{1,3},{2,0},{3,1},{4,6},{5,7},{6,4},{7,5},{8,10},{9,11},{10,... | collective-permute-start | bytes 786440 | tf_op jit(solution)/shard_map/ppermute | solution.py:487
  47.8 14.0 %collective-permute-start.15 = (bf16[128,1024]{1,0:T(8,128)(2,1)S(1)}, bf16[128,1024]{1,0:T(8,128)(2,1)S(1)}, u32[]{:S(2)}, u32[]{:S(2)}) collective-permute-start(bf16[128,1024]{1,0:T(8,128)(2,1)S(1)} %get-tuple-element.54), channel_id=1, source_target_pairs={{0,4},{1,5},{2,6},{3,7},{4,0},{5,1},{6,2},{7,3},{8,12},{9,13},{10,... | collective-permute-start | bytes 786440 | tf_op jit(solution)/shard_map/ppermute | solution.py:487
  48.3 13.5 %collective-permute-start.16 = (bf16[128,1024]{1,0:T(8,128)(2,1)S(1)}, bf16[128,1024]{1,0:T(8,128)(2,1)S(1)}, u32[]{:S(2)}, u32[]{:S(2)}) collective-permute-start(bf16[128,1024]{1,0:T(8,128)(2,1)S(1)} %get-tuple-element.55), channel_id=1, source_target_pairs={{0,6},{1,7},{2,4},{3,5},{4,2},{5,3},{6,0},{7,1},{8,14},{9,15},{10,... | collective-permute-start | bytes 786440 | tf_op jit(solution)/shard_map/ppermute | solution.py:487
  51.3 4.4 %collective-permute-start.21 = (bf16[288,128]{1,0:T(8,128)(2,1)S(1)}, bf16[288,128]{1,0:T(8,128)(2,1)S(1)}, u32[]{:S(2)}, u32[]{:S(2)}) collective-permute-start(bf16[288,128]{1,0:T(8,128)(2,1)S(1)} %get-tuple-element.63.refs_0_), channel_id=1, source_target_pairs={{0,8},{8,0},{16,24},{24,16},{1,9},{9,1},{17,25},{25,17},{2,10},{10... | collective-permute-start | bytes 221192 | tf_op jit(solution)/shard_map/ppermute | solution.py:487
  55.8 6.8 %collective-permute-start.22 = (bf16[2,128,128]{2,1,0:T(8,128)(2,1)S(1)}, bf16[2,128,128]{2,1,0:T(8,128)(2,1)S(1)}, u32[]{:S(2)}, u32[]{:S(2)}) collective-permute-start(bf16[2,128,128]{2,1,0:T(8,128)(2,1)S(1)} %shard_map.132.own), channel_id=1, source_target_pairs={{0,16},{8,24},{16,0},{24,8},{1,17},{9,25},{17,1},{25,9},{2,18},{10... | collective-permute-start | bytes 196616 | tf_op jit(solution)/shard_map/ppermute | solution.py:487
  (5 other events, 43.8 us)

commit v5 on v4

--- a/solution.py
+++ b/solution.py
@@ -30,16 +30,22 @@
     return (k // free) * SLOT + neighbors + k % free
 
 
+def chunk_of(rows, pieces):
+    return -(-rows // (pieces * SLOT)) * SLOT
+
+
 def pack_kernel(n, width, *refs):
-    far, refs = refs[:5], refs[5:]
-    packed, own_radial, (blocks, radials, group) = refs[: n // 2], refs[n // 2], refs[n // 2 + 1 : n // 2 + 4]
-    held, done = refs[n // 2 + 4 : n // 2 + 9], refs[n // 2 + 9]
+    far, refs = refs[:7], refs[7:]
+    m = n // 2
+    packed, (feats_out, cot_out, own_radial) = refs[: m - 2], refs[m - 2 : m + 1]
+    (blocks, radials, group, bundle), refs = refs[m + 1 : m + 5], refs[m + 5 :]
+    held, done = refs[:7], refs[7]
     copies = [pltpu.make_async_copy(a, b, done.at[i]) for i, (a, b) in enumerate(zip(far, held))]
     for copy in copies:
         copy.start()
     for copy in copies:
         copy.wait()
-    weight, src, dist, ids, radial_weight = held
+    weight, src, dist, ids, radial_weight, feats, cot = held
     me = lax.axis_index("fsdp")
     rows = weight.shape[0]
     neighbors, atoms = src.shape
@@ -62,29 +68,58 @@
         part = left.astype(bf16)
         meta.append(part)
         left = left - part.astype(f32)
-    for c in range(n // 2):
-        packed[c][:rows] = blocks[me ^ (2 * c)]
-        packed[c][rows : 2 * rows] = blocks[me ^ (2 * c + 1)]
+    feats_out[:atoms] = feats[...]
+    cot_out[:atoms] = cot[...]
+    direct = 0
+    for c in range(m):
+        wide = {1: feats_out, m // 2: cot_out}.get(c)
+        if wide is None:
+            target = packed[direct]
+            direct += 1
+        else:
+            target = bundle
+        target[:rows] = blocks[me ^ (2 * c)]
+        target[rows : 2 * rows] = blocks[me ^ (2 * c + 1)]
         for i, part in enumerate(meta):
-            packed[c][2 * rows + i * SLOT : 2 * rows + (i + 1) * SLOT] = part
-
-
-def merge_kernel(m, *refs):
-    parts, out = refs[:m], refs[-1]
-    rows = parts[0].shape[0]
-    for c, part in enumerate(parts):
-        out[c * rows : (c + 1) * rows] = part[...]
-
-
-def swap_kernel(*refs):
-    parts, last, out = refs[:-2], refs[-2], refs[-1]
-    rows = parts[0].shape[0] // 2
-    for c, part in enumerate(parts):
-        out[c * rows : (c + 1) * rows] = part[rows:]
-    out[len(parts) * rows :] = last[...]
-
-
-def gate_kernel(_value, _after, _out):
+            target[2 * rows + i * SLOT : 2 * rows + (i + 1) * SLOT] = part
+        if wide is not None:
+            size = wide.shape[0] - atoms
+            for q in range(wide.shape[1] // LANES):
+                stop = min((q + 1) * size, bundle.shape[0])
+                if stop > q * size:
+                    wide[atoms : atoms + stop - q * size, q * LANES : (q + 1) * LANES] = bundle[
+                        q * size : stop
+                    ]
+
+
+def merge_kernel(m, rows, *refs):
+    direct, (feats, cot, own_weight), refs = list(refs[: m - 2]), refs[m - 2 : m + 1], refs[m + 1 :]
+    for value, held in zip(refs[:2], refs[2:4]):
+        held[...] = value[...]
+    lists, weights, bundle = refs[4:]
+    size = 4 * SLOT
+    for c in range(m):
+        wide = {1: feats, m // 2: cot}.get(c)
+        if wide is None:
+            source = direct.pop(0)
+        else:
+            source = bundle
+            height = chunk_of(bundle.shape[0], wide.shape[1] // LANES)
+            for q in range(wide.shape[1] // LANES):
+                stop = min((q + 1) * height, bundle.shape[0])
+                if stop > q * height:
+                    bundle[q * height : stop] = wide[
+                        wide.shape[0] - height : wide.shape[0] - height + stop - q * height,
+                        q * LANES : (q + 1) * LANES,
+                    ]
+        weights[2 * c * rows : 2 * (c + 1) * rows] = source[: 2 * rows]
+        lists[c * size : (c + 1) * size] = source[2 * rows :]
+    for q in range(own_weight.shape[1] // LANES):
+        start = (2 * m + q) * rows
+        weights[start : start + rows] = own_weight[:, q * LANES : (q + 1) * LANES]
+
+
+def gate_kernel(*_):
     pass
 
 
@@ -154,23 +189,16 @@
 
 def lists_kernel(n, margin, neighbors, ahead, *refs):
     m = n // 2
-    near, far, own_radial = refs[:m], refs[m], refs[m + 1]
-    weights, columns, offsets = refs[m + 2 : m + 5]
-    made = refs[m + 5 : m + 8] if ahead else ()
-    dists, graph_weight, stacked, filters = refs[m + 5 + len(made) :]
+    near, far, own_radial = refs[:3]
+    columns, offsets = refs[3:5]
+    made = refs[5:8] if ahead else ()
+    dists, graph_weight, stacked, filters = refs[5 + len(made) :]
     me = lax.axis_index("fsdp")
     basis = own_radial.shape[0]
-    rows = weights.shape[0] // n
     atoms = columns.shape[0] // n
     for d in range(n):
         e = me ^ d
-        head = 2 * rows + 4 * SLOT
-        block = near[d // 2] if d % 2 == 0 else far.at[d // 2 * head : (d // 2 + 1) * head]
-        weights[rows_at(e, rows), d % 2 * LANES : (d % 2 + 1) * LANES] = block[:rows]
-        weights[rows_at(e, rows), (1 - d % 2) * LANES : (2 - d % 2) * LANES] = block[
-            rows : 2 * rows
-        ]
-        meta = block[2 * rows :].astype(f32)
+        meta = (far if d % 2 else near)[d // 2 * 4 * SLOT : (d // 2 + 1) * 4 * SLOT].astype(f32)
         offsets[rows_at(e, SLOT)] = meta[:SLOT]
         dists[rows_at(e, SLOT)] = (
             meta[SLOT : 2 * SLOT] + meta[2 * SLOT : 3 * SLOT] + meta[3 * SLOT :]
@@ -217,12 +245,13 @@
             )
             return 0
 
-        lax.fori_loop(0, n, block_step, 0, unroll=2)
-
-
-def products_kernel(n, weights, own_weight, other_weight, *refs):
+        lax.fori_loop(0, n, block_step, 0, unroll=8)
+
+
+def products_kernel(n, near, far, own_weight, *refs):
     m = n // 2
-    feats, cots, (keep, give, held_feats, both) = refs[:m], refs[m : 2 * m], refs[2 * m :]
+    feats, cots, refs = refs[:m], refs[m : 2 * m], refs[2 * m :]
+    keep, give, held_feats, both, weights = refs
     me = lax.axis_index("fsdp")
     atoms = feats[0].shape[0]
     half = m * atoms
@@ -230,14 +259,22 @@
     if rows < LANES:
         both[...] = jnp.zeros_like(both)
     both[:rows] = own_weight[...]
-    both[LANES : LANES + rows] = other_weight[...]
+    for q in range(both.shape[1] // LANES):
+        start = (2 * m + q) * rows
+        both[LANES : LANES + rows, q * LANES : (q + 1) * LANES] = far[start : start + rows]
     for c in range(m):
-        held_feats[c * atoms : (c + 1) * atoms] = feats[c][...]
-        projected = jnp.dot(
-            feats[c][...], weights[...], preferred_element_type=f32
-        ).astype(bf16)
+        for k, source in enumerate((near, far)):
+            block = rows_at(me ^ (2 * c + k), rows)
+            for i in range(2):
+                start = (2 * c + i) * rows
+                side = slice(LANES, None) if i != k else slice(0, LANES)
+                weights[block, side] = source[start : start + rows]
+    for c in range(m):
+        piece = feats[c][:atoms]
+        held_feats[c * atoms : (c + 1) * atoms] = piece
+        projected = jnp.dot(piece, weights[...], preferred_element_type=f32).astype(bf16)
         dact = lax.dot_general(
-            cots[c][...], both[...], (((1,), (1,)), ((), ())), preferred_element_type=f32
+            cots[c][:atoms], both[...], (((1,), (1,)), ((), ())), preferred_element_type=f32
         ).astype(bf16)
         chip = (me // 2) ^ c
         keep[rows_at(chip, atoms)] = projected[:, :LANES]
@@ -367,16 +404,23 @@
 
 def gradient_kernel(n, rows, turned, own_feats, other_feats, *refs):
     m = n // 2
-    sends, grads = refs[:m], refs[m]
+    keep, give, grads = refs
     me = lax.axis_index("fsdp")
     half = own_feats.shape[0]
     total = jnp.dot(turned[:, :half], own_feats[...], preferred_element_type=f32)
     total = total + jnp.dot(turned[:, half:], other_feats[...], preferred_element_type=f32)
     for q in range(total.shape[1] // LANES):
-        grads[q * LANES : (q + 1) * LANES] = total[:, q * LANES : (q + 1) * LANES].T.astype(bf16)
+        grads[q * LANES : (q + 1) * LANES] = total[:, q * LANES : (q + 1) * LANES].T
     for c in range(m):
-        sends[c][:rows] = grads[rows_at(me ^ (2 * c), rows)]
-        sends[c][rows:] = grads[rows_at(me ^ (2 * c + 1), rows)]
+        keep[c * rows : (c + 1) * rows] = grads[rows_at(me ^ (2 * c), rows)].astype(bf16)
+        give[c * rows : (c + 1) * rows] = grads[rows_at(me ^ (2 * c + 1), rows)]
+
+
+def join_kernel(keep, got, *sends):
+    rows = sends[0].shape[0]
+    for c, send in enumerate(sends):
+        send[:, :LANES] = keep[c * rows : (c + 1) * rows]
+        send[:, LANES:] = got[c * rows : (c + 1) * rows].astype(bf16)
 
 
 def write_code(piece, code):
@@ -397,51 +441,44 @@
     atoms = cots[0].shape[0]
     rows = own.shape[0]
     at = column_of(neighbors, neighbors)
+    pieces = own_weight.shape[1] // LANES
+    first = other_weight.shape[0] - pieces * rows
+    other_weight = jnp.concatenate(
+        [other_weight[first + q * rows : first + (q + 1) * rows] for q in range(pieces)], axis=1
+    )
     totals = [None, None]
     for c in range(m):
         block = rows_at((me // 2) ^ c, atoms)
         sends[c][...] = (
             jnp.dot(keep[block][:, :width], own_weight[...], preferred_element_type=f32)
-            + jnp.dot(got[block][:, :width], other_weight[...], preferred_element_type=f32)
+            + jnp.dot(got[block][:, :width], other_weight, preferred_element_type=f32)
         ).astype(bf16)
         graph = columns[rows_at(me ^ (2 * c), atoms)][:, at : at + 1]
         for i, act in enumerate((keep, got)):
             left = (act[block].astype(f32) * graph).T.astype(bf16)
-            term = jnp.dot(left, cots[c][...], preferred_element_type=f32)
+            term = jnp.dot(left, cots[c][:atoms], preferred_element_type=f32)
             totals[i] = term if c == 0 else totals[i] + term
     own[...] = totals[0][:rows]
-    for q in range(own.shape[1] // LANES):
-        give[q * rows : (q + 1) * rows] = totals[1][:rows, q * LANES : (q + 1) * LANES].astype(bf16)
+    give[...] = totals[1][:rows].astype(bf16)
 
 
 def grads_kernel(n, fragment, *refs):
     m = n // 2
-    near, far, own_part = refs[:m], refs[m], refs[m + 1]
+    near, got_part, own_part = refs[:m], refs[m], refs[m + 1]
     msg_grad, out_grad, code, blocks, total = refs[m + 2 :]
     me = lax.axis_index("fsdp")
     rows = msg_grad.shape[1]
     width = msg_grad.shape[2] // n
     lanes = pl.ds(pl.multiple_of(fragment[0] * FRAG, FRAG), FRAG)
     for c in range(m):
-        blocks[me ^ (2 * c)] = near[c][:rows]
-        blocks[me ^ (2 * c + 1)] = far[c * rows : (c + 1) * rows]
+        blocks[me ^ (2 * c)] = near[c][:, :LANES]
+        blocks[me ^ (2 * c + 1)] = near[c][:, LANES:]
     for e in range(n):
         msg_grad[0, :, e * width : (e + 1) * width] = blocks[e][:, :width]
     write_code(msg_grad[0, :, lanes].astype(f32), code.at[: rows + SLOT])
-    for q in range(total.shape[1] // LANES):
-        part = slice(q * LANES, (q + 1) * LANES)
-        start = (m + q) * rows
-        total[:, part] = own_part[:, part] + far[start : start + rows].astype(f32)
+    total[...] = own_part[...] + got_part[...].astype(f32)
     out_grad[0] = total[...].astype(bf16)
     write_code(total[:, lanes], code.at[rows + SLOT :])
-
-
-def node_kernel(feats, *refs):
-    parts, out = refs[:-1], refs[-1]
-    total = feats[...].astype(f32)
-    for part in parts:
-        total = total + part[...].astype(f32)
-    out[...] = total.astype(bf16)
 
 
 def pair_kernel(*refs):
@@ -458,6 +495,15 @@
 
 def outer_kernel(own, other, out):
     out[...] = (own[...].astype(f32) + other[...].astype(f32)).astype(out.dtype)
+
+
+def last_kernel(count, *refs):
+    pair, (feats, *parts), (outer, node) = refs[:count], refs[count:-2], refs[-2:]
+    outer[...] = functools.reduce(jnp.add, [value[...].astype(f32) for value in pair])
+    total = feats[...].astype(f32)
+    for part in parts:
+        total = total + part[...].astype(f32)
+    node[...] = total.astype(bf16)
 
 
 def run(kernel, outs, scratch, args, micros, memory=16, scalars=0, outside=0):
@@ -482,6 +528,21 @@
     )(*args)
 
 
+def after(values, other, micros):
+    anywhere = pl.BlockSpec(memory_space=pl.ANY)
+    return pl.pallas_call(
+        gate_kernel,
+        out_shape=[jax.ShapeDtypeStruct(value.shape, value.dtype) for value in values],
+        in_specs=[anywhere] * (len(values) + 1),
+        out_specs=[anywhere] * len(values),
+        input_output_aliases={i: i for i in range(len(values))},
+        compiler_params=pltpu.CompilerParams(vmem_limit_bytes=1 << 20),
+        cost_estimate=pl.CostEstimate(
+            flops=int(micros * 1e9), bytes_accessed=int(micros * 3e6), transcendentals=0
+        ),
+    )(*values, other)
+
+
 def hop(value, axis, step):
     count = lax.axis_size(axis)
     return lax.ppermute(value, axis, [(i, i ^ step) for i in range(count)])
@@ -491,14 +552,13 @@
     return [sends[0]] + [hop(sends[c], "fsdp", 2 * c) for c in range(1, len(sends))]
 
 
-def exchanged(first, second, n):
-    bits = [1 << i for i in range((n // 2).bit_length() - 1)]
-    found = [{0: value} for value in (first, second)]
-    for c in range(1, n // 2):
-        used = [bit for bit in bits if c & bit]
-        for pieces, bit in zip(found, (used[0], used[-1])):
-            pieces[c] = hop(pieces[c ^ bit], "fsdp", 2 * bit)
-    return [[pieces[c] for c in range(n // 2)] for pieces in found]
+def exchanged(value, held, m, side):
+    pieces = {0: value, **held}
+    for c in range(1, m):
+        if c not in pieces:
+            used = [1 << i for i in range(m.bit_length()) if c >> i & 1][side]
+            pieces[c] = hop(pieces[c ^ used], "fsdp", 2 * used)
+    return [pieces[c] for c in range(m)]
 
 
 def shards(
@@ -537,12 +597,20 @@
         distances,
         graph_ids,
         radial_weight,
+        node_feats,
+        cotangent,
     ]
     bundle = 2 * rows + 4 * SLOT
-    *packed, own_radial = run(
+    wide = (atoms + chunk_of(bundle, channels // LANES), channels)
+    *packed, wide_feats, wide_cot, own_radial = run(
         functools.partial(pack_kernel, n, width),
-        [((bundle, LANES), bf16)] * m + [((basis, LANES), f32)],
-        [((n, rows, LANES), bf16), ((n, basis, LANES), f32), ((SLOT, LANES), f32)]
+        [((bundle, LANES), bf16)] * (m - 2) + [(wide, bf16)] * 2 + [((basis, LANES), f32)],
+        [
+            ((n, rows, LANES), bf16),
+            ((n, basis, LANES), f32),
+            ((SLOT, LANES), f32),
+            ((bundle, LANES), bf16),
+        ]
         + [(piece.shape, piece.dtype) for piece in pack_inputs]
         + [((len(pack_inputs),), None)],
         pack_inputs,
@@ -550,21 +618,27 @@
         60,
         outside=len(pack_inputs),
     )
-    near = across_chips(packed)
-    feats, cots = exchanged(node_feats, cotangent, n)
-    (give_lists,) = run(
-        functools.partial(merge_kernel, m),
-        [((m * bundle, LANES), bf16)],
-        [],
-        [*near, feats[m // 2], cots[1]],
+    others = [c for c in range(1, m) if c not in (1, m // 2)]
+    feats = exchanged(node_feats, {1: hop(wide_feats, "fsdp", 2)}, m, 0)
+    cots = exchanged(cotangent, {m // 2: hop(wide_cot, "fsdp", 2 * (m // 2))}, m, -1)
+    own_feats, own_cot, near_lists, near_weights = run(
+        functools.partial(merge_kernel, m, rows),
+        [((atoms, channels), bf16)] * 2
+        + [
+            ((m * 4 * SLOT, LANES), bf16),
+            (((2 * m + channels // LANES) * rows, LANES), bf16),
+        ],
+        [((bundle, LANES), bf16)],
+        [packed[0]]
+        + list(after([hop(value, "fsdp", 2 * c) for c, value in zip(others, packed[1:])], own_radial, 10))
+        + [feats[1], cots[m // 2], out_weight, node_feats, cotangent],
         0,
         memory,
     )
-    far = hop(give_lists, "fsdp", 1)
-    weights, columns, offsets, *made = run(
+    far_weights = hop(near_weights, "fsdp", 1)
+    columns, offsets, *made = run(
         functools.partial(lists_kernel, n, margin, neighbors, ahead),
         [
-            ((channels, 2 * LANES), bf16),
             ((all_atoms, LANES), f32),
             ((n * SLOT, LANES), f32),
         ]
@@ -580,28 +654,25 @@
             ((min(n, 8), basis * SLOT, LANES), f32),
             ((2 * basis * SLOT, lanes), bf16),
         ],
-        [*near, far, own_radial],
+        [near_lists, hop(near_lists, "fsdp", 1), own_radial],
         0,
         memory,
     )
-    other_weight = hop(out_weight, "fsdp", 1)
+    feats[0], cots[0] = own_feats, own_cot
+    passed = [(pieces, c) for pieces in (feats, cots) for c in range(1, m) if c & (c - 1)]
+    held = after([pieces[c] for pieces, c in passed], offsets, 10)
+    for (pieces, c), value in zip(passed, held):
+        pieces[c] = value
     own_products, give_products, held_feats = run(
         functools.partial(products_kernel, n),
         [((all_atoms, LANES), bf16)] * 2 + [((all_atoms // 2, channels), bf16)],
-        [((2 * LANES, channels), bf16)],
-        [weights, out_weight, other_weight, *feats, *cots],
+        [((2 * LANES, channels), bf16), ((channels, 2 * LANES), bf16)],
+        [near_weights, far_weights, out_weight, *feats, *cots],
         1,
         memory,
     )
     got_products = hop(give_products, "fsdp", 1)
-    held_feats = pl.pallas_call(
-        gate_kernel,
-        out_shape=jax.ShapeDtypeStruct(held_feats.shape, bf16),
-        in_specs=[pl.BlockSpec(memory_space=pl.ANY)] * 2,
-        out_specs=pl.BlockSpec(memory_space=pl.ANY),
-        input_output_aliases={0: 0},
-        compiler_params=pltpu.CompilerParams(vmem_limit_bytes=1 << 20),
-    )(held_feats, got_products)
+    (held_feats,) = after([held_feats], got_products, 0)
     keep, give, dagg = run(
         functools.partial(forward_kernel, n, margin, neighbors, norm, ahead),
         [
@@ -628,48 +699,41 @@
         1,
         memory,
     )
-    grad_sends = run(
+    keep_grads, give_grads = run(
         functools.partial(gradient_kernel, n, rows),
-        [((2 * rows, LANES), bf16)] * m,
-        [((channels, LANES), bf16)],
+        [((m * rows, LANES), bf16), ((m * rows, LANES), f32)],
+        [((channels, LANES), f32)],
         [turned, held_feats, hop(held_feats, "fsdp", 1)],
         1,
         memory,
     )
-    near = across_chips(grad_sends)
     *sums, own_part, give_part = run(
         functools.partial(chip_kernel, n, margin, neighbors, width),
-        [((atoms, channels), bf16)] * m + [((rows, channels), f32), ((channels // LANES * rows, LANES), bf16)],
+        [((atoms, channels), bf16)] * m + [((rows, channels), f32), ((rows, channels), bf16)],
         [],
-        [columns, keep, other_act, out_weight, other_weight, grad_sends[0], *cots],
+        [columns, keep, other_act, out_weight, far_weights, give_grads, *cots],
         1,
         memory,
     )
-    (swap,) = run(
-        swap_kernel,
-        [(((m + channels // LANES) * rows, LANES), bf16)],
+    grad_sends = run(
+        join_kernel,
+        [((rows, 2 * LANES), bf16)] * m,
         [],
-        [*near, give_part],
+        [keep_grads, hop(give_grads, "fsdp", 1)],
         0,
         memory,
     )
+    near = across_chips(grad_sends)
     grad_msg, grad_out, code = run(
         functools.partial(grads_kernel, n),
         [((1, rows, channels), bf16)] * 2 + [((2 * (rows + SLOT), FRAG), bf16)],
         [((n, rows, LANES), bf16), ((rows, channels), f32)],
-        [fragment, *near, hop(swap, "fsdp", 1), own_part],
-        1,
+        [fragment, *near, hop(give_part, "fsdp", 1), own_part],
+        4,
         memory,
         scalars=1,
     )
-    (node_out,) = run(
-        node_kernel,
-        [((atoms, channels), bf16)],
-        [],
-        [node_feats, sums[0]] + [hop(sums[c], "fsdp", 2 * c) for c in range(1, m)],
-        1,
-        memory,
-    )
+    sums = across_chips(sums)
     step = 1
     codes = [code]
     if replicas > 1:
@@ -677,17 +741,27 @@
     (outer_sum,) = run(
         pair_kernel, [((2, rows, FRAG), f32 if replicas <= 2 else bf16)], [], codes, 0, memory
     )
-    while 2 * step < replicas:
+    while 4 * step < replicas:
         step = 2 * step
-        last = 2 * step >= replicas
         (outer_sum,) = run(
             outer_kernel,
-            [((2, rows, FRAG), f32 if last else bf16)],
+            [((2, rows, FRAG), bf16)],
             [],
             [outer_sum, hop(outer_sum, "replica", step)],
             0,
             memory,
         )
+    pair = [outer_sum]
+    if replicas > 2:
+        pair.append(hop(outer_sum, "replica", 2 * step))
+    outer_sum, node_out = run(
+        functools.partial(last_kernel, len(pair)),
+        [((2, rows, FRAG), f32), ((atoms, channels), bf16)],
+        [],
+        [*pair, node_feats, *sums],
+        0,
+        memory,
+    )
     return node_out, grad_msg, grad_out, outer_sum
 
 

time: 63.5 us -> 55.3 us (0.87)
  waiting for transfers between devices: 21.4 us -> 16.1 us
  Pallas kernels: 14.3 us -> 13.3 us
  starting transfers between devices: 24.5 us -> 23.5 us
  local copies, waits for them, and re-layouts: 1.59 us -> 0.7 us
    ppermute x23 -> x22, waiting for transfers between devices: 21.4 us -> 16.1 us  [hop(): return lax.ppermute(value, axis, [(i, i ^ step) for i in range(count)])]
    ppermute x23 -> x22, starting transfers between devices: 24.5 us -> 23.5 us  [hop(): return lax.ppermute(value, axis, [(i, i ^ step) for i in range(count)])]
    pallas_call x13 -> x12, Pallas kernels: 14.3 us -> 13.3 us  [run(): pl.pallas_call(kernel, out_shape=[jax.ShapeDtypeStruct(shape, dtype) for...]
    unnamed x12 -> x10, local copies, waits for them, and re-layouts: 1.59 us -> 0.7 us
  transfers between devices with their start and end apart: 23 -> 22, of which waited for: 9 -> 9; matrix products, arithmetic and copies ran while one was open for 0% -> 0% of each run, Pallas kernels for 20% -> 21%
where the time goes in v5:
time: 55.3 us; the launch traced here: 55.1 us
  starting transfers between devices  23.5 us (42%)
  waiting for transfers between devices  16.1 us (29%)
  Pallas kernels  13.3 us (24%)
  between operations  1.42 us (3%)
  local copies, waits for them, and re-layouts  0.7 us (1%)
    ppermute x22, starting transfers between devices, hop(): return lax.ppermute(value, axis, [(i, i ^ step) for i in range(count)])  23.5 us
    ppermute x22, waiting for transfers between devices, hop(): return lax.ppermute(value, axis, [(i, i ^ step) for i in range(count)])  16.1 us
    pallas_call x12, Pallas kernels, run(): pl.pallas_call(kernel, out_shape=[jax.ShapeDtypeStruct(shape, dtype) for...  13.3 us
  transfers between devices with their start and end apart: 22, of which 9 were waited for; matrix products, arithmetic and copies ran while one was open for 0% of the time, Pallas kernels for 21%

profile of v5, /device:TPU:0, one launch (start us, length us, event | category | flops | bytes accessed | tf_op | source)
XLA Modules:
  0.0 55.1 jit_solution(6385540736964756244)
XLA Ops:
  0.6 3.0 %collective-permute-start.6 = (bf16[128,1024]{1,0:T(8,128)(2,1)}, bf16[128,1024]{1,0:T(8,128)(2,1)S(1)}, u32[]{:S(2)}, u32[]{:S(2)}) collective-permute-start(bf16[128,1024]{1,0:T(8,128)(2,1)} %refs_6_.3), channel_id=1, source_target_pairs={{0,2},{1,3},{2,0},{3,1},{4,6},{5,7},{6,4},{7,5},{8,10},{9,11},{10,... | collective-permute-start | bytes 786440 | tf_op jit(solution)/shard_map/ppermute | solution.py:548
  3.6 1.5 %collective-permute-start.4 = (bf16[128,1024]{1,0:T(8,128)(2,1)}, bf16[128,1024]{1,0:T(8,128)(2,1)S(1)}, u32[]{:S(2)}, u32[]{:S(2)}) collective-permute-start(bf16[128,1024]{1,0:T(8,128)(2,1)} %refs_2_.3), channel_id=1, source_target_pairs={{0,4},{1,5},{2,6},{3,7},{4,0},{5,1},{6,2},{7,3},{8,12},{9,13},{10,... | collective-permute-start | bytes 786440 | tf_op jit(solution)/shard_map/ppermute | solution.py:548
  5.2 2.2 %shard_map.120 = (bf16[320,128]{1,0:T(8,128)(2,1)}, bf16[320,128]{1,0:T(8,128)(2,1)}, bf16[176,1024]{1,0:T(8,128)(2,1)}, bf16[176,1024]{1,0:T(8,128)(2,1)}, f32[8,128]{1,0:T(8,128)}) custom-call(bf16[128,1024]{1,0:T(8,128)(2,1)} %refs_0_.1, s32[12,128]{1,0:T(8,128)} %refs_1_.1, f32[12,128]{1,0:T(8,128)} %refs_2_.2, s32[1,128]{1,0:T(1,128)} %refs_3_.2, ...), custom_call_target="tpu_custom_call" | custom-call | flops 1000000000 | bytes 3000000 | tf_op jit(solution)/shard_map/pallas_call | solution.py:513
  7.5 1.9 %collective-permute-start.1 = (bf16[176,1024]{1,0:T(8,128)(2,1)}, bf16[176,1024]{1,0:T(8,128)(2,1)S(1)}, u32[]{:S(2)}, u32[]{:S(2)}) collective-permute-start(bf16[176,1024]{1,0:T(8,128)(2,1)} %get-tuple-element.46), channel_id=1, source_target_pairs={{0,2},{1,3},{2,0},{3,1},{4,6},{5,7},{6,4},{7,5},{8,10},{9,11},{10,... | collective-permute-start | bytes 1081352 | tf_op jit(solution)/shard_map/ppermute | solution.py:548
  9.4 1.5 %collective-permute-start.2 = (bf16[176,1024]{1,0:T(8,128)(2,1)}, bf16[176,1024]{1,0:T(8,128)(2,1)S(1)}, u32[]{:S(2)}, u32[]{:S(2)}) collective-permute-start(bf16[176,1024]{1,0:T(8,128)(2,1)} %get-tuple-element.47), channel_id=1, source_target_pairs={{0,4},{1,5},{2,6},{3,7},{4,0},{5,1},{6,2},{7,3},{8,12},{9,13},{10,... | collective-permute-start | bytes 1081352 | tf_op jit(solution)/shard_map/ppermute | solution.py:548
  11.0 1.8 %collective-permute-start.7 = (bf16[128,1024]{1,0:T(8,128)(2,1)S(1)}, bf16[128,1024]{1,0:T(8,128)(2,1)S(1)}, u32[]{:S(2)}, u32[]{:S(2)}) collective-permute-start(bf16[128,1024]{1,0:T(8,128)(2,1)S(1)} %collective-permute-done.6.refs_5_.refs_7_), channel_id=1, source_target_pairs={{0,4},{1,5},{2,6},{3,7},{4,0},{5,1},{6,2},{7,3},{8,12},{9,13},{10,... | collective-permute-start | bytes 786440 | tf_op jit(solution)/shard_map/ppermute | solution.py:548
  12.8 1.4 %collective-permute-done.4.refs_2_ = bf16[128,1024]{1,0:T(8,128)(2,1)S(1)} collective-permute-done((bf16[128,1024]{1,0:T(8,128)(2,1)}, bf16[128,1024]{1,0:T(8,128)(2,1)S(1)}, u32[]{:S(2)}, u32[]{:S(2)}) %collective-permute-start.4) | collective-permute-done | bytes 262176 | tf_op jit(solution)/shard_map/ppermute | solution.py:548
  15.3 5.4 %collective-permute-done.1.refs_2_.refs_1_ = bf16[176,1024]{1,0:T(8,128)(2,1)S(1)} collective-permute-done((bf16[176,1024]{1,0:T(8,128)(2,1)}, bf16[176,1024]{1,0:T(8,128)(2,1)S(1)}, u32[]{:S(2)}, u32[]{:S(2)}) %collective-permute-start.1) | collective-permute-done | bytes 360480 | tf_op jit(solution)/shard_map/ppermute | solution.py:548
  20.7 1.2 %collective-permute-done.2.refs_3_.refs_6_.refs_8_ = bf16[176,1024]{1,0:T(8,128)(2,1)S(1)} collective-permute-done((bf16[176,1024]{1,0:T(8,128)(2,1)}, bf16[176,1024]{1,0:T(8,128)(2,1)S(1)}, u32[]{:S(2)}, u32[]{:S(2)}) %collective-permute-start.2) | collective-permute-done | bytes 360480 | tf_op jit(solution)/shard_map/ppermute | solution.py:548
  23.4 3.1 %shard_map.123 = (f32[1024,128]{1,0:T(8,128)S(1)}, f32[128,128]{1,0:T(8,128)S(1)}, f32[1024,1536]{1,0:T(8,128)S(1)}, bf16[6144,256]{1,0:T(8,128)(2,1)S(1)}, bf16[2048,768]{1,0:T(8,128)(2,1)S(1)}) custom-call(bf16[256,128]{1,0:T(8,128)(2,1)S(1)} %get-tuple-element.50.refs_0_, bf16[256,128]{1,0:T(8,128)(2,1)S(1)} %collective-permute-done.8.refs_1_, ...), custom_call_target="tpu_custom_call" | custom-call | tf_op jit(solution)/shard_map/pallas_call | solution.py:513
  26.7 1.1 %shard_map.125 = (bf16[1024,128]{1,0:T(8,128)(2,1)S(1)}, bf16[1024,128]{1,0:T(8,128)(2,1)S(1)}, bf16[512,1024]{1,0:T(8,128)(2,1)S(1)}) custom-call(bf16[2048,128]{1,0:T(8,128)(2,1)S(1)} %get-tuple-element.48.near, bf16[2048,128]{1,0:T(8,128)(2,1)S(1)} %collective-permute-done.3.far.refs_4_, bf16[128,1024]{1,0:T(8,128)(2,1)S(1)} %copy-done.2, ...), custom_call_target="tpu_custom_call" | custom-call | flops 1000000000 | bytes 3000000 | tf_op jit(solution)/shard_map/pallas_call | solution.py:513
  27.9 1.5 %collective-permute-done.9.refs_1_.__1_ = bf16[1024,128]{1,0:T(8,128)(2,1)S(1)} collective-permute-done((bf16[1024,128]{1,0:T(8,128)(2,1)S(1)}, bf16[1024,128]{1,0:T(8,128)(2,1)S(1)}, u32[]{:S(2)}, u32[]{:S(2)}) %collective-permute-start.9) | collective-permute-done | bytes 262176 | tf_op jit(solution)/shard_map/ppermute | solution.py:548
  29.6 1.2 %shard_map.126 = (bf16[512,128]{1,0:T(8,128)(2,1)S(1)}, bf16[512,128]{1,0:T(8,128)(2,1)S(1)}, f32[1024,128]{1,0:T(8,128)S(1)}) custom-call(bf16[1024,128]{1,0:T(8,128)(2,1)S(1)} %get-tuple-element.55.refs_0_, bf16[1024,128]{1,0:T(8,128)(2,1)S(1)} %collective-permute-done.9.refs_1_.__1_, f32[1024,128]{1,0:T(8,128)S(1)} %get-tuple-element.57.refs_2_.refs_0_, ...), custom_call_target="tpu_custom_call" | custom-call | flops 1000000000 | bytes 3000000 | tf_op jit(solution)/shard_map/pallas_call | solution.py:513
  31.2 1.7 %shard_map.127.turned = bf16[128,1024]{1,0:T(8,128)(2,1)S(1)} custom-call(f32[1024,128]{1,0:T(8,128)S(1)} %get-tuple-element.60.refs_0_, f32[8,128]{1,0:T(8,128)S(1)} %copy-done.4, f32[1024,128]{1,0:T(8,128)S(1)} %get-tuple-element.57.refs_2_.refs_0_, f32[128,128]{1,0:T(8,128)S(1)} %get-tuple-element.51.__2_.refs_3_, ...), custom_call_target="tpu_custom_call" | custom-call | flops 1000000000 | bytes 3000000 | tf_op jit(solution)/shard_map/pallas_call | solution.py:513
  33.7 1.2 %shard_map.131 = (bf16[128,1024]{1,0:T(8,128)(2,1)S(1)}, bf16[128,1024]{1,0:T(8,128)(2,1)S(1)}, bf16[128,1024]{1,0:T(8,128)(2,1)S(1)}, bf16[128,1024]{1,0:T(8,12...) custom-call(f32[1024,128]{1,0:T(8,128)S(1)} %get-tuple-element.57.refs_2_.refs_0_, ...), custom_call_target="tpu_custom_call" | custom-call | flops 1000000000 | bytes 3000000 | tf_op jit(solution)/shard_map/pallas_call | solution.py:513
  36.0 1.6 %collective-permute-start.13 = (bf16[128,256]{1,0:T(8,128)(2,1)S(1)}, bf16[128,256]{1,0:T(8,128)(2,1)S(1)}, u32[]{:S(2)}, u32[]{:S(2)}) collective-permute-start(bf16[128,256]{1,0:T(8,128)(2,1)S(1)} %get-tuple-element.67), channel_id=1, source_target_pairs={{0,4},{1,5},{2,6},{3,7},{4,0},{5,1},{6,2},{7,3},{8,12},{9,13},{10,... | collective-permute-start | bytes 196616 | tf_op jit(solution)/shard_map/ppermute | solution.py:548
  37.6 1.4 %collective-permute-start.14 = (bf16[128,256]{1,0:T(8,128)(2,1)S(1)}, bf16[128,256]{1,0:T(8,128)(2,1)S(1)}, u32[]{:S(2)}, u32[]{:S(2)}) collective-permute-start(bf16[128,256]{1,0:T(8,128)(2,1)S(1)} %get-tuple-element.68), channel_id=1, source_target_pairs={{0,6},{1,7},{2,4},{3,5},{4,2},{5,3},{6,0},{7,1},{8,14},{9,15},{10,... | collective-permute-start | bytes 196616 | tf_op jit(solution)/shard_map/ppermute | solution.py:548
  40.2 1.6 %collective-permute-start.20 = (bf16[128,1024]{1,0:T(8,128)(2,1)S(1)}, bf16[128,1024]{1,0:T(8,128)(2,1)S(1)}, u32[]{:S(2)}, u32[]{:S(2)}) collective-permute-start(bf16[128,1024]{1,0:T(8,128)(2,1)S(1)} %get-tuple-element.76), channel_id=1, source_target_pairs={{0,4},{1,5},{2,6},{3,7},{4,0},{5,1},{6,2},{7,3},{8,12},{9,13},{10,... | collective-permute-start | bytes 786440 | tf_op jit(solution)/shard_map/ppermute | solution.py:548
  41.8 1.4 %collective-permute-start.21 = (bf16[128,1024]{1,0:T(8,128)(2,1)S(1)}, bf16[128,1024]{1,0:T(8,128)(2,1)S(1)}, u32[]{:S(2)}, u32[]{:S(2)}) collective-permute-start(bf16[128,1024]{1,0:T(8,128)(2,1)S(1)} %get-tuple-element.77), channel_id=1, source_target_pairs={{0,6},{1,7},{2,4},{3,5},{4,2},{5,3},{6,0},{7,1},{8,14},{9,15},{10,... | collective-permute-start | bytes 786440 | tf_op jit(solution)/shard_map/ppermute | solution.py:548
  44.2 1.6 %collective-permute-start.17 = (bf16[288,128]{1,0:T(8,128)(2,1)S(1)}, bf16[288,128]{1,0:T(8,128)(2,1)S(1)}, u32[]{:S(2)}, u32[]{:S(2)}) collective-permute-start(bf16[288,128]{1,0:T(8,128)(2,1)S(1)} %get-tuple-element.73.refs_0_), channel_id=1, source_target_pairs={{0,8},{8,0},{16,24},{24,16},{1,9},{9,1},{17,25},{25,17},{2,10},{10... | collective-permute-start | bytes 221192 | tf_op jit(solution)/shard_map/ppermute | solution.py:548
  45.8 2.8 %collective-permute-done.17.refs_1_ = bf16[288,128]{1,0:T(8,128)(2,1)S(1)} collective-permute-done((bf16[288,128]{1,0:T(8,128)(2,1)S(1)}, bf16[288,128]{1,0:T(8,128)(2,1)S(1)}, u32[]{:S(2)}, u32[]{:S(2)}) %collective-permute-start.17) | collective-permute-done | bytes 73760 | tf_op jit(solution)/shard_map/ppermute | solution.py:548
  48.7 2.7 %collective-permute-start.18 = (bf16[2,128,128]{2,1,0:T(8,128)(2,1)S(1)}, bf16[2,128,128]{2,1,0:T(8,128)(2,1)S(1)}, u32[]{:S(2)}, u32[]{:S(2)}) collective-permute-start(bf16[2,128,128]{2,1,0:T(8,128)(2,1)S(1)} %shard_map.133.refs_0_), channel_id=1, source_target_pairs={{0,16},{8,24},{16,0},{24,8},{1,17},{9,25},{17,1},{25,9},{2,18},{10... | collective-permute-start | bytes 196616 | tf_op jit(solution)/shard_map/ppermute | solution.py:548
  51.4 1.0 %collective-permute-done.20.refs_5_ = bf16[128,1024]{1,0:T(8,128)(2,1)S(1)} collective-permute-done((bf16[128,1024]{1,0:T(8,128)(2,1)S(1)}, bf16[128,1024]{1,0:T(8,128)(2,1)S(1)}, u32[]{:S(2)}, u32[]{:S(2)}) %collective-permute-start.20) | collective-permute-done | bytes 262176 | tf_op jit(solution)/shard_map/ppermute | solution.py:548
  52.4 1.8 %collective-permute-done.21.refs_6_ = bf16[128,1024]{1,0:T(8,128)(2,1)S(1)} collective-permute-done((bf16[128,1024]{1,0:T(8,128)(2,1)S(1)}, bf16[128,1024]{1,0:T(8,128)(2,1)S(1)}, u32[]{:S(2)}, u32[]{:S(2)}) %collective-permute-start.21) | collective-permute-done | bytes 262176 | tf_op jit(solution)/shard_map/ppermute | solution.py:548
  (45 shorter events, 7.8 us)
Async XLA Ops:
  0.6 10.3 %collective-permute-start.6 = (bf16[128,1024]{1,0:T(8,128)(2,1)}, bf16[128,1024]{1,0:T(8,128)(2,1)S(1)}, u32[]{:S(2)}, u32[]{:S(2)}) collective-permute-start(bf16[128,1024]{1,0:T(8,128)(2,1)} %refs_6_.3), channel_id=1, source_target_pairs={{0,2},{1,3},{2,0},{3,1},{4,6},{5,7},{6,4},{7,5},{8,10},{9,11},{10,... | collective-permute-start | bytes 786440 | tf_op jit(solution)/shard_map/ppermute | solution.py:548
  3.6 10.5 %collective-permute-start.4 = (bf16[128,1024]{1,0:T(8,128)(2,1)}, bf16[128,1024]{1,0:T(8,128)(2,1)S(1)}, u32[]{:S(2)}, u32[]{:S(2)}) collective-permute-start(bf16[128,1024]{1,0:T(8,128)(2,1)} %refs_2_.3), channel_id=1, source_target_pairs={{0,4},{1,5},{2,6},{3,7},{4,0},{5,1},{6,2},{7,3},{8,12},{9,13},{10,... | collective-permute-start | bytes 786440 | tf_op jit(solution)/shard_map/ppermute | solution.py:548
  7.4 7.2 %collective-permute-start = (bf16[320,128]{1,0:T(8,128)(2,1)}, bf16[320,128]{1,0:T(8,128)(2,1)S(1)}, u32[]{:S(2)}, u32[]{:S(2)}) collective-permute-start(bf16[320,128]{1,0:T(8,128)(2,1)} %get-tuple-element.44), channel_id=1, source_target_pairs={{0,6},{1,7},{2,4},{3,5},{4,2},{5,3},{6,0},{7,1},{8,14},{9,15},{10,... | collective-permute-start | bytes 245768 | tf_op jit(solution)/shard_map/ppermute | solution.py:548
  7.5 13.2 %collective-permute-start.1 = (bf16[176,1024]{1,0:T(8,128)(2,1)}, bf16[176,1024]{1,0:T(8,128)(2,1)S(1)}, u32[]{:S(2)}, u32[]{:S(2)}) collective-permute-start(bf16[176,1024]{1,0:T(8,128)(2,1)} %get-tuple-element.46), channel_id=1, source_target_pairs={{0,2},{1,3},{2,0},{3,1},{4,6},{5,7},{6,4},{7,5},{8,10},{9,11},{10,... | collective-permute-start | bytes 1081352 | tf_op jit(solution)/shard_map/ppermute | solution.py:548
  9.4 12.5 %collective-permute-start.2 = (bf16[176,1024]{1,0:T(8,128)(2,1)}, bf16[176,1024]{1,0:T(8,128)(2,1)S(1)}, u32[]{:S(2)}, u32[]{:S(2)}) collective-permute-start(bf16[176,1024]{1,0:T(8,128)(2,1)} %get-tuple-element.47), channel_id=1, source_target_pairs={{0,4},{1,5},{2,6},{3,7},{4,0},{5,1},{6,2},{7,3},{8,12},{9,13},{10,... | collective-permute-start | bytes 1081352 | tf_op jit(solution)/shard_map/ppermute | solution.py:548
  11.0 15.8 %collective-permute-start.7 = (bf16[128,1024]{1,0:T(8,128)(2,1)S(1)}, bf16[128,1024]{1,0:T(8,128)(2,1)S(1)}, u32[]{:S(2)}, u32[]{:S(2)}) collective-permute-start(bf16[128,1024]{1,0:T(8,128)(2,1)S(1)} %collective-permute-done.6.refs_5_.refs_7_), channel_id=1, source_target_pairs={{0,4},{1,5},{2,6},{3,7},{4,0},{5,1},{6,2},{7,3},{8,12},{9,13},{10,... | collective-permute-start | bytes 786440 | tf_op jit(solution)/shard_map/ppermute | solution.py:548
  14.2 12.5 %collective-permute-start.5 = (bf16[128,1024]{1,0:T(8,128)(2,1)S(1)}, bf16[128,1024]{1,0:T(8,128)(2,1)S(1)}, u32[]{:S(2)}, u32[]{:S(2)}) collective-permute-start(bf16[128,1024]{1,0:T(8,128)(2,1)S(1)} %collective-permute-done.4.refs_2_), channel_id=1, source_target_pairs={{0,2},{1,3},{2,0},{3,1},{4,6},{5,7},{6,4},{7,5},{8,10},{9,11},{10,... | collective-permute-start | bytes 786440 | tf_op jit(solution)/shard_map/ppermute | solution.py:548
  15.3 6.7 %copy-start.2 = (bf16[128,1024]{1,0:T(8,128)(2,1)S(1)}, bf16[128,1024]{1,0:T(8,128)(2,1)}, u32[]{:S(2)}) copy-start(bf16[128,1024]{1,0:T(8,128)(2,1)} %refs_3_.3) | copy-start | bytes 786436
  15.3 6.7 %copy-start.3 = (bf16[320,128]{1,0:T(8,128)(2,1)S(1)}, bf16[320,128]{1,0:T(8,128)(2,1)}, u32[]{:S(2)}) copy-start(bf16[320,128]{1,0:T(8,128)(2,1)} %get-tuple-element.43.refs_0_) | copy-start | bytes 245764
  22.1 1.3 %collective-permute-start.8 = (bf16[256,128]{1,0:T(8,128)(2,1)S(1)}, bf16[256,128]{1,0:T(8,128)(2,1)S(1)}, u32[]{:S(2)}, u32[]{:S(2)}) collective-permute-start(bf16[256,128]{1,0:T(8,128)(2,1)S(1)} %get-tuple-element.50.refs_0_), channel_id=1, source_target_pairs={{0,1},{1,0},{2,3},{3,2},{4,5},{5,4},{6,7},{7,6},{8,9},{9,8},{10,11... | collective-permute-start | bytes 196616 | tf_op jit(solution)/shard_map/ppermute | solution.py:548
  22.2 4.6 %collective-permute-start.3 = (bf16[2048,128]{1,0:T(8,128)(2,1)S(1)}, bf16[2048,128]{1,0:T(8,128)(2,1)S(1)}, u32[]{:S(2)}, u32[]{:S(2)}) collective-permute-start(bf16[2048,128]{1,0:T(8,128)(2,1)S(1)} %get-tuple-element.48.near), channel_id=1, source_target_pairs={{0,1},{1,0},{2,3},{3,2},{4,5},{5,4},{6,7},{7,6},{8,9},{9,8},{10,11... | collective-permute-start | bytes 1572872 | tf_op jit(solution)/shard_map/ppermute | solution.py:548
  27.8 1.6 %collective-permute-start.9 = (bf16[1024,128]{1,0:T(8,128)(2,1)S(1)}, bf16[1024,128]{1,0:T(8,128)(2,1)S(1)}, u32[]{:S(2)}, u32[]{:S(2)}) collective-permute-start(bf16[1024,128]{1,0:T(8,128)(2,1)S(1)} %get-tuple-element.56), channel_id=1, source_target_pairs={{0,1},{1,0},{2,3},{3,2},{4,5},{5,4},{6,7},{7,6},{8,9},{9,8},{10,11... | collective-permute-start | bytes 786440 | tf_op jit(solution)/shard_map/ppermute | solution.py:548
  29.4 3.5 %collective-permute-start.10 = (bf16[512,1024]{1,0:T(8,128)(2,1)S(1)}, bf16[512,1024]{1,0:T(8,128)(2,1)S(1)}, u32[]{:S(2)}, u32[]{:S(2)}) collective-permute-start(bf16[512,1024]{1,0:T(8,128)(2,1)S(1)} %shard_map.128.own_feats), channel_id=1, source_target_pairs={{0,1},{1,0},{2,3},{3,2},{4,5},{5,4},{6,7},{7,6},{8,9},{9,8},{10,11... | collective-permute-start | bytes 3145736 | tf_op jit(solution)/shard_map/ppermute | solution.py:548
  30.8 2.9 %collective-permute-start.15 = (bf16[512,128]{1,0:T(8,128)(2,1)S(1)}, bf16[512,128]{1,0:T(8,128)(2,1)S(1)}, u32[]{:S(2)}, u32[]{:S(2)}) collective-permute-start(bf16[512,128]{1,0:T(8,128)(2,1)S(1)} %get-tuple-element.70), channel_id=1, source_target_pairs={{0,1},{1,0},{2,3},{3,2},{4,5},{5,4},{6,7},{7,6},{8,9},{9,8},{10,11... | collective-permute-start | bytes 393224 | tf_op jit(solution)/shard_map/ppermute | solution.py:548
  33.5 1.9 %collective-permute-start.11 = (f32[512,128]{1,0:T(8,128)S(1)}, f32[512,128]{1,0:T(8,128)S(1)}, u32[]{:S(2)}, u32[]{:S(2)}) collective-permute-start(f32[512,128]{1,0:T(8,128)S(1)} %get-tuple-element.64.refs_5_), channel_id=1, source_target_pairs={{0,1},{1,0},{2,3},{3,2},{4,5},{5,4},{6,7},{7,6},{8,9},{9,8},{10,11... | collective-permute-start | bytes 786440 | tf_op jit(solution)/shard_map/ppermute | solution.py:548
  35.0 5.2 %collective-permute-start.16 = (bf16[128,1024]{1,0:T(8,128)(2,1)S(1)}, bf16[128,1024]{1,0:T(8,128)(2,1)S(1)}, u32[]{:S(2)}, u32[]{:S(2)}) collective-permute-start(bf16[128,1024]{1,0:T(8,128)(2,1)S(1)} %get-tuple-element.71), channel_id=1, source_target_pairs={{0,1},{1,0},{2,3},{3,2},{4,5},{5,4},{6,7},{7,6},{8,9},{9,8},{10,11... | collective-permute-start | bytes 786440 | tf_op jit(solution)/shard_map/ppermute | solution.py:548
  35.5 6.3 %collective-permute-start.12 = (bf16[128,256]{1,0:T(8,128)(2,1)S(1)}, bf16[128,256]{1,0:T(8,128)(2,1)S(1)}, u32[]{:S(2)}, u32[]{:S(2)}) collective-permute-start(bf16[128,256]{1,0:T(8,128)(2,1)S(1)} %get-tuple-element.66), channel_id=1, source_target_pairs={{0,2},{1,3},{2,0},{3,1},{4,6},{5,7},{6,4},{7,5},{8,10},{9,11},{10,... | collective-permute-start | bytes 196616 | tf_op jit(solution)/shard_map/ppermute | solution.py:548
  36.0 7.3 %collective-permute-start.13 = (bf16[128,256]{1,0:T(8,128)(2,1)S(1)}, bf16[128,256]{1,0:T(8,128)(2,1)S(1)}, u32[]{:S(2)}, u32[]{:S(2)}) collective-permute-start(bf16[128,256]{1,0:T(8,128)(2,1)S(1)} %get-tuple-element.67), channel_id=1, source_target_pairs={{0,4},{1,5},{2,6},{3,7},{4,0},{5,1},{6,2},{7,3},{8,12},{9,13},{10,... | collective-permute-start | bytes 196616 | tf_op jit(solution)/shard_map/ppermute | solution.py:548
  37.6 5.7 %collective-permute-start.14 = (bf16[128,256]{1,0:T(8,128)(2,1)S(1)}, bf16[128,256]{1,0:T(8,128)(2,1)S(1)}, u32[]{:S(2)}, u32[]{:S(2)}) collective-permute-start(bf16[128,256]{1,0:T(8,128)(2,1)S(1)} %get-tuple-element.68), channel_id=1, source_target_pairs={{0,6},{1,7},{2,4},{3,5},{4,2},{5,3},{6,0},{7,1},{8,14},{9,15},{10,... | collective-permute-start | bytes 196616 | tf_op jit(solution)/shard_map/ppermute | solution.py:548
  39.7 11.7 %collective-permute-start.19 = (bf16[128,1024]{1,0:T(8,128)(2,1)S(1)}, bf16[128,1024]{1,0:T(8,128)(2,1)S(1)}, u32[]{:S(2)}, u32[]{:S(2)}) collective-permute-start(bf16[128,1024]{1,0:T(8,128)(2,1)S(1)} %get-tuple-element.75), channel_id=1, source_target_pairs={{0,2},{1,3},{2,0},{3,1},{4,6},{5,7},{6,4},{7,5},{8,10},{9,11},{10,... | collective-permute-start | bytes 786440 | tf_op jit(solution)/shard_map/ppermute | solution.py:548
  40.2 12.2 %collective-permute-start.20 = (bf16[128,1024]{1,0:T(8,128)(2,1)S(1)}, bf16[128,1024]{1,0:T(8,128)(2,1)S(1)}, u32[]{:S(2)}, u32[]{:S(2)}) collective-permute-start(bf16[128,1024]{1,0:T(8,128)(2,1)S(1)} %get-tuple-element.76), channel_id=1, source_target_pairs={{0,4},{1,5},{2,6},{3,7},{4,0},{5,1},{6,2},{7,3},{8,12},{9,13},{10,... | collective-permute-start | bytes 786440 | tf_op jit(solution)/shard_map/ppermute | solution.py:548
  41.8 12.4 %collective-permute-start.21 = (bf16[128,1024]{1,0:T(8,128)(2,1)S(1)}, bf16[128,1024]{1,0:T(8,128)(2,1)S(1)}, u32[]{:S(2)}, u32[]{:S(2)}) collective-permute-start(bf16[128,1024]{1,0:T(8,128)(2,1)S(1)} %get-tuple-element.77), channel_id=1, source_target_pairs={{0,6},{1,7},{2,4},{3,5},{4,2},{5,3},{6,0},{7,1},{8,14},{9,15},{10,... | collective-permute-start | bytes 786440 | tf_op jit(solution)/shard_map/ppermute | solution.py:548
  44.2 4.4 %collective-permute-start.17 = (bf16[288,128]{1,0:T(8,128)(2,1)S(1)}, bf16[288,128]{1,0:T(8,128)(2,1)S(1)}, u32[]{:S(2)}, u32[]{:S(2)}) collective-permute-start(bf16[288,128]{1,0:T(8,128)(2,1)S(1)} %get-tuple-element.73.refs_0_), channel_id=1, source_target_pairs={{0,8},{8,0},{16,24},{24,16},{1,9},{9,1},{17,25},{25,17},{2,10},{10... | collective-permute-start | bytes 221192 | tf_op jit(solution)/shard_map/ppermute | solution.py:548
  48.7 5.5 %collective-permute-start.18 = (bf16[2,128,128]{2,1,0:T(8,128)(2,1)S(1)}, bf16[2,128,128]{2,1,0:T(8,128)(2,1)S(1)}, u32[]{:S(2)}, u32[]{:S(2)}) collective-permute-start(bf16[2,128,128]{2,1,0:T(8,128)(2,1)S(1)} %shard_map.133.refs_0_), channel_id=1, source_target_pairs={{0,16},{8,24},{16,0},{24,8},{1,17},{9,25},{17,1},{25,9},{2,18},{10... | collective-permute-start | bytes 196616 | tf_op jit(solution)/shard_map/ppermute | solution.py:548
  (3 other events, 14.0 us)

commit v6 on v5

--- a/solution.py
+++ b/solution.py
@@ -270,17 +270,19 @@
                 side = slice(LANES, None) if i != k else slice(0, LANES)
                 weights[block, side] = source[start : start + rows]
     for c in range(m):
-        piece = feats[c][:atoms]
-        held_feats[c * atoms : (c + 1) * atoms] = piece
-        projected = jnp.dot(piece, weights[...], preferred_element_type=f32).astype(bf16)
-        dact = lax.dot_general(
-            cots[c][:atoms], both[...], (((1,), (1,)), ((), ())), preferred_element_type=f32
-        ).astype(bf16)
+        held_feats[c * atoms : (c + 1) * atoms] = feats[c][:atoms]
+    projected = jnp.dot(held_feats[...], weights[...], preferred_element_type=f32).astype(bf16)
+    flow = jnp.concatenate([cots[c][:atoms] for c in range(m)], axis=0)
+    dact = lax.dot_general(
+        flow, both[...], (((1,), (1,)), ((), ())), preferred_element_type=f32
+    ).astype(bf16)
+    for c in range(m):
         chip = (me // 2) ^ c
-        keep[rows_at(chip, atoms)] = projected[:, :LANES]
-        give[rows_at(chip, atoms)] = projected[:, LANES:]
-        keep[rows_at(chip + m, atoms)] = dact[:, :LANES]
-        give[rows_at(chip + m, atoms)] = dact[:, LANES:]
+        here = slice(c * atoms, (c + 1) * atoms)
+        keep[rows_at(chip, atoms)] = projected[here, :LANES]
+        give[rows_at(chip, atoms)] = projected[here, LANES:]
+        keep[rows_at(chip + m, atoms)] = dact[here, :LANES]
+        give[rows_at(chip + m, atoms)] = dact[here, LANES:]
 
 
 def forward_kernel(n, margin, neighbors, norm, ahead, *refs):
@@ -446,20 +448,23 @@
     other_weight = jnp.concatenate(
         [other_weight[first + q * rows : first + (q + 1) * rows] for q in range(pieces)], axis=1
     )
-    totals = [None, None]
+    acts = [
+        jnp.concatenate([act[rows_at((me // 2) ^ c, atoms)] for c in range(m)], axis=0)
+        for act in (keep, got)
+    ]
+    total = jnp.dot(acts[0][:, :width], own_weight[...], preferred_element_type=f32) + jnp.dot(
+        acts[1][:, :width], other_weight, preferred_element_type=f32
+    )
     for c in range(m):
-        block = rows_at((me // 2) ^ c, atoms)
-        sends[c][...] = (
-            jnp.dot(keep[block][:, :width], own_weight[...], preferred_element_type=f32)
-            + jnp.dot(got[block][:, :width], other_weight, preferred_element_type=f32)
-        ).astype(bf16)
-        graph = columns[rows_at(me ^ (2 * c), atoms)][:, at : at + 1]
-        for i, act in enumerate((keep, got)):
-            left = (act[block].astype(f32) * graph).T.astype(bf16)
-            term = jnp.dot(left, cots[c][:atoms], preferred_element_type=f32)
-            totals[i] = term if c == 0 else totals[i] + term
-    own[...] = totals[0][:rows]
-    give[...] = totals[1][:rows].astype(bf16)
+        sends[c][...] = total[c * atoms : (c + 1) * atoms].astype(bf16)
+    graph = jnp.concatenate(
+        [columns[rows_at(me ^ (2 * c), atoms)][:, at : at + 1] for c in range(m)], axis=0
+    )
+    left = jnp.concatenate([(act.astype(f32) * graph).T.astype(bf16) for act in acts], axis=0)
+    flow = jnp.concatenate([cots[c][:atoms] for c in range(m)], axis=0)
+    parts = jnp.dot(left, flow, preferred_element_type=f32)
+    own[...] = parts[:rows]
+    give[...] = parts[LANES : LANES + rows].astype(bf16)
 
 
 def grads_kernel(n, fragment, *refs):

time: 55.3 us -> 54.8 us (level)
  transfers between devices with their start and end apart: 22 -> 22, of which waited for: 9 -> 9; matrix products, arithmetic and copies ran while one was open for 0% -> 0% of each run, Pallas kernels for 21% -> 20%
where the time goes in v6:
time: 54.8 us; the launch traced here: 54.6 us
  starting transfers between devices  23.5 us (43%)
  waiting for transfers between devices  16.2 us (30%)
  Pallas kernels  12.8 us (23%)
  between operations  1.42 us (3%)
  local copies, waits for them, and re-layouts  0.7 us (1%)
    ppermute x22, starting transfers between devices, hop(): return lax.ppermute(value, axis, [(i, i ^ step) for i in range(count)])  23.5 us
    ppermute x22, waiting for transfers between devices, hop(): return lax.ppermute(value, axis, [(i, i ^ step) for i in range(count)])  16.2 us
    pallas_call x12, Pallas kernels, run(): pl.pallas_call(kernel, out_shape=[jax.ShapeDtypeStruct(shape, dtype) for...  12.8 us
  transfers between devices with their start and end apart: 22, of which 9 were waited for; matrix products, arithmetic and copies ran while one was open for 0% of the time, Pallas kernels for 20%

profile of v6, /device:TPU:0, one launch (start us, length us, event | category | flops | bytes accessed | tf_op | source)
XLA Modules:
  0.0 54.6 jit_solution(4781761717108977180)
XLA Ops:
  0.6 3.0 %collective-permute-start.6 = (bf16[128,1024]{1,0:T(8,128)(2,1)}, bf16[128,1024]{1,0:T(8,128)(2,1)S(1)}, u32[]{:S(2)}, u32[]{:S(2)}) collective-permute-start(bf16[128,1024]{1,0:T(8,128)(2,1)} %refs_6_.3), channel_id=1, source_target_pairs={{0,2},{1,3},{2,0},{3,1},{4,6},{5,7},{6,4},{7,5},{8,10},{9,11},{10,... | collective-permute-start | bytes 786440 | tf_op jit(solution)/shard_map/ppermute | solution.py:553
  3.6 1.5 %collective-permute-start.4 = (bf16[128,1024]{1,0:T(8,128)(2,1)}, bf16[128,1024]{1,0:T(8,128)(2,1)S(1)}, u32[]{:S(2)}, u32[]{:S(2)}) collective-permute-start(bf16[128,1024]{1,0:T(8,128)(2,1)} %refs_2_.3), channel_id=1, source_target_pairs={{0,4},{1,5},{2,6},{3,7},{4,0},{5,1},{6,2},{7,3},{8,12},{9,13},{10,... | collective-permute-start | bytes 786440 | tf_op jit(solution)/shard_map/ppermute | solution.py:553
  5.2 2.2 %shard_map.120 = (bf16[320,128]{1,0:T(8,128)(2,1)}, bf16[320,128]{1,0:T(8,128)(2,1)}, bf16[176,1024]{1,0:T(8,128)(2,1)}, bf16[176,1024]{1,0:T(8,128)(2,1)}, f32[8,128]{1,0:T(8,128)}) custom-call(bf16[128,1024]{1,0:T(8,128)(2,1)} %refs_0_.1, s32[12,128]{1,0:T(8,128)} %refs_1_.1, f32[12,128]{1,0:T(8,128)} %refs_2_.2, s32[1,128]{1,0:T(1,128)} %refs_3_.2, ...), custom_call_target="tpu_custom_call" | custom-call | flops 1000000000 | bytes 3000000 | tf_op jit(solution)/shard_map/pallas_call | solution.py:518
  7.5 1.9 %collective-permute-start.1 = (bf16[176,1024]{1,0:T(8,128)(2,1)}, bf16[176,1024]{1,0:T(8,128)(2,1)S(1)}, u32[]{:S(2)}, u32[]{:S(2)}) collective-permute-start(bf16[176,1024]{1,0:T(8,128)(2,1)} %get-tuple-element.46), channel_id=1, source_target_pairs={{0,2},{1,3},{2,0},{3,1},{4,6},{5,7},{6,4},{7,5},{8,10},{9,11},{10,... | collective-permute-start | bytes 1081352 | tf_op jit(solution)/shard_map/ppermute | solution.py:553
  9.4 1.5 %collective-permute-start.2 = (bf16[176,1024]{1,0:T(8,128)(2,1)}, bf16[176,1024]{1,0:T(8,128)(2,1)S(1)}, u32[]{:S(2)}, u32[]{:S(2)}) collective-permute-start(bf16[176,1024]{1,0:T(8,128)(2,1)} %get-tuple-element.47), channel_id=1, source_target_pairs={{0,4},{1,5},{2,6},{3,7},{4,0},{5,1},{6,2},{7,3},{8,12},{9,13},{10,... | collective-permute-start | bytes 1081352 | tf_op jit(solution)/shard_map/ppermute | solution.py:553
  11.0 1.8 %collective-permute-start.7 = (bf16[128,1024]{1,0:T(8,128)(2,1)S(1)}, bf16[128,1024]{1,0:T(8,128)(2,1)S(1)}, u32[]{:S(2)}, u32[]{:S(2)}) collective-permute-start(bf16[128,1024]{1,0:T(8,128)(2,1)S(1)} %collective-permute-done.6.refs_5_.refs_7_), channel_id=1, source_target_pairs={{0,4},{1,5},{2,6},{3,7},{4,0},{5,1},{6,2},{7,3},{8,12},{9,13},{10,... | collective-permute-start | bytes 786440 | tf_op jit(solution)/shard_map/ppermute | solution.py:553
  12.8 1.4 %collective-permute-done.4.refs_2_ = bf16[128,1024]{1,0:T(8,128)(2,1)S(1)} collective-permute-done((bf16[128,1024]{1,0:T(8,128)(2,1)}, bf16[128,1024]{1,0:T(8,128)(2,1)S(1)}, u32[]{:S(2)}, u32[]{:S(2)}) %collective-permute-start.4) | collective-permute-done | bytes 262176 | tf_op jit(solution)/shard_map/ppermute | solution.py:553
  15.3 5.4 %collective-permute-done.1.refs_2_.refs_1_ = bf16[176,1024]{1,0:T(8,128)(2,1)S(1)} collective-permute-done((bf16[176,1024]{1,0:T(8,128)(2,1)}, bf16[176,1024]{1,0:T(8,128)(2,1)S(1)}, u32[]{:S(2)}, u32[]{:S(2)}) %collective-permute-start.1) | collective-permute-done | bytes 360480 | tf_op jit(solution)/shard_map/ppermute | solution.py:553
  20.7 1.2 %collective-permute-done.2.refs_3_.refs_6_.refs_8_ = bf16[176,1024]{1,0:T(8,128)(2,1)S(1)} collective-permute-done((bf16[176,1024]{1,0:T(8,128)(2,1)}, bf16[176,1024]{1,0:T(8,128)(2,1)S(1)}, u32[]{:S(2)}, u32[]{:S(2)}) %collective-permute-start.2) | collective-permute-done | bytes 360480 | tf_op jit(solution)/shard_map/ppermute | solution.py:553
  23.4 3.1 %shard_map.123 = (f32[1024,128]{1,0:T(8,128)S(1)}, f32[128,128]{1,0:T(8,128)S(1)}, f32[1024,1536]{1,0:T(8,128)S(1)}, bf16[6144,256]{1,0:T(8,128)(2,1)S(1)}, bf16[2048,768]{1,0:T(8,128)(2,1)S(1)}) custom-call(bf16[256,128]{1,0:T(8,128)(2,1)S(1)} %get-tuple-element.50.refs_0_, bf16[256,128]{1,0:T(8,128)(2,1)S(1)} %collective-permute-done.8.refs_1_, ...), custom_call_target="tpu_custom_call" | custom-call | tf_op jit(solution)/shard_map/pallas_call | solution.py:518
  27.7 1.5 %collective-permute-done.9.refs_1_.__1_ = bf16[1024,128]{1,0:T(8,128)(2,1)S(1)} collective-permute-done((bf16[1024,128]{1,0:T(8,128)(2,1)S(1)}, bf16[1024,128]{1,0:T(8,128)(2,1)S(1)}, u32[]{:S(2)}, u32[]{:S(2)}) %collective-permute-start.9) | collective-permute-done | bytes 262176 | tf_op jit(solution)/shard_map/ppermute | solution.py:553
  29.4 1.2 %shard_map.126 = (bf16[512,128]{1,0:T(8,128)(2,1)S(1)}, bf16[512,128]{1,0:T(8,128)(2,1)S(1)}, f32[1024,128]{1,0:T(8,128)S(1)}) custom-call(bf16[1024,128]{1,0:T(8,128)(2,1)S(1)} %get-tuple-element.55.refs_0_, bf16[1024,128]{1,0:T(8,128)(2,1)S(1)} %collective-permute-done.9.refs_1_.__1_, f32[1024,128]{1,0:T(8,128)S(1)} %get-tuple-element.57.refs_2_.refs_0_, ...), custom_call_target="tpu_custom_call" | custom-call | flops 1000000000 | bytes 3000000 | tf_op jit(solution)/shard_map/pallas_call | solution.py:518
  31.0 1.7 %shard_map.127.turned = bf16[128,1024]{1,0:T(8,128)(2,1)S(1)} custom-call(f32[1024,128]{1,0:T(8,128)S(1)} %get-tuple-element.60.refs_0_, f32[8,128]{1,0:T(8,128)S(1)} %copy-done.4, f32[1024,128]{1,0:T(8,128)S(1)} %get-tuple-element.57.refs_2_.refs_0_, f32[128,128]{1,0:T(8,128)S(1)} %get-tuple-element.51.__2_.refs_3_, ...), custom_call_target="tpu_custom_call" | custom-call | flops 1000000000 | bytes 3000000 | tf_op jit(solution)/shard_map/pallas_call | solution.py:518
  33.5 1.0 %shard_map.131 = (bf16[128,1024]{1,0:T(8,128)(2,1)S(1)}, bf16[128,1024]{1,0:T(8,128)(2,1)S(1)}, bf16[128,1024]{1,0:T(8,128)(2,1)S(1)}, bf16[128,1024]{1,0:T(8,12...) custom-call(f32[1024,128]{1,0:T(8,128)S(1)} %get-tuple-element.57.refs_2_.refs_0_, ...), custom_call_target="tpu_custom_call" | custom-call | flops 1000000000 | bytes 3000000 | tf_op jit(solution)/shard_map/pallas_call | solution.py:518
  35.5 1.6 %collective-permute-start.13 = (bf16[128,256]{1,0:T(8,128)(2,1)S(1)}, bf16[128,256]{1,0:T(8,128)(2,1)S(1)}, u32[]{:S(2)}, u32[]{:S(2)}) collective-permute-start(bf16[128,256]{1,0:T(8,128)(2,1)S(1)} %get-tuple-element.67), channel_id=1, source_target_pairs={{0,4},{1,5},{2,6},{3,7},{4,0},{5,1},{6,2},{7,3},{8,12},{9,13},{10,... | collective-permute-start | bytes 196616 | tf_op jit(solution)/shard_map/ppermute | solution.py:553
  37.1 1.4 %collective-permute-start.14 = (bf16[128,256]{1,0:T(8,128)(2,1)S(1)}, bf16[128,256]{1,0:T(8,128)(2,1)S(1)}, u32[]{:S(2)}, u32[]{:S(2)}) collective-permute-start(bf16[128,256]{1,0:T(8,128)(2,1)S(1)} %get-tuple-element.68), channel_id=1, source_target_pairs={{0,6},{1,7},{2,4},{3,5},{4,2},{5,3},{6,0},{7,1},{8,14},{9,15},{10,... | collective-permute-start | bytes 196616 | tf_op jit(solution)/shard_map/ppermute | solution.py:553
  39.7 1.6 %collective-permute-start.20 = (bf16[128,1024]{1,0:T(8,128)(2,1)S(1)}, bf16[128,1024]{1,0:T(8,128)(2,1)S(1)}, u32[]{:S(2)}, u32[]{:S(2)}) collective-permute-start(bf16[128,1024]{1,0:T(8,128)(2,1)S(1)} %get-tuple-element.76), channel_id=1, source_target_pairs={{0,4},{1,5},{2,6},{3,7},{4,0},{5,1},{6,2},{7,3},{8,12},{9,13},{10,... | collective-permute-start | bytes 786440 | tf_op jit(solution)/shard_map/ppermute | solution.py:553
  41.3 1.4 %collective-permute-start.21 = (bf16[128,1024]{1,0:T(8,128)(2,1)S(1)}, bf16[128,1024]{1,0:T(8,128)(2,1)S(1)}, u32[]{:S(2)}, u32[]{:S(2)}) collective-permute-start(bf16[128,1024]{1,0:T(8,128)(2,1)S(1)} %get-tuple-element.77), channel_id=1, source_target_pairs={{0,6},{1,7},{2,4},{3,5},{4,2},{5,3},{6,0},{7,1},{8,14},{9,15},{10,... | collective-permute-start | bytes 786440 | tf_op jit(solution)/shard_map/ppermute | solution.py:553
  42.7 1.0 %shard_map.132 = (bf16[1,128,1024]{2,1,0:T(8,128)(2,1)}, bf16[1,128,1024]{2,1,0:T(8,128)(2,1)}, bf16[288,128]{1,0:T(8,128)(2,1)S(1)}) custom-call(s32[1]{0:T(128)S(6)} %copy.21.fragment, bf16[128,256]{1,0:T(8,128)(2,1)S(1)} %get-tuple-element.65.refs_0_, bf16[128,256]{1,0:T(8,128)(2,1)S(1)} %collective-permute-done.12.refs_1_, ...), custom_call_target="tpu_custom_call" | custom-call | flops 4000000000 | bytes 12000000 | tf_op jit(solution)/shard_map/pallas_call | solution.py:518
  43.7 1.6 %collective-permute-start.17 = (bf16[288,128]{1,0:T(8,128)(2,1)S(1)}, bf16[288,128]{1,0:T(8,128)(2,1)S(1)}, u32[]{:S(2)}, u32[]{:S(2)}) collective-permute-start(bf16[288,128]{1,0:T(8,128)(2,1)S(1)} %get-tuple-element.73.refs_0_), channel_id=1, source_target_pairs={{0,8},{8,0},{16,24},{24,16},{1,9},{9,1},{17,25},{25,17},{2,10},{10... | collective-permute-start | bytes 221192 | tf_op jit(solution)/shard_map/ppermute | solution.py:553
  45.3 2.8 %collective-permute-done.17.refs_1_ = bf16[288,128]{1,0:T(8,128)(2,1)S(1)} collective-permute-done((bf16[288,128]{1,0:T(8,128)(2,1)S(1)}, bf16[288,128]{1,0:T(8,128)(2,1)S(1)}, u32[]{:S(2)}, u32[]{:S(2)}) %collective-permute-start.17) | collective-permute-done | bytes 73760 | tf_op jit(solution)/shard_map/ppermute | solution.py:553
  48.2 2.7 %collective-permute-start.18 = (bf16[2,128,128]{2,1,0:T(8,128)(2,1)S(1)}, bf16[2,128,128]{2,1,0:T(8,128)(2,1)S(1)}, u32[]{:S(2)}, u32[]{:S(2)}) collective-permute-start(bf16[2,128,128]{2,1,0:T(8,128)(2,1)S(1)} %shard_map.133.refs_0_), channel_id=1, source_target_pairs={{0,16},{8,24},{16,0},{24,8},{1,17},{9,25},{17,1},{25,9},{2,18},{10... | collective-permute-start | bytes 196616 | tf_op jit(solution)/shard_map/ppermute | solution.py:553
  50.9 1.0 %collective-permute-done.20.refs_5_ = bf16[128,1024]{1,0:T(8,128)(2,1)S(1)} collective-permute-done((bf16[128,1024]{1,0:T(8,128)(2,1)S(1)}, bf16[128,1024]{1,0:T(8,128)(2,1)S(1)}, u32[]{:S(2)}, u32[]{:S(2)}) %collective-permute-start.20) | collective-permute-done | bytes 262176 | tf_op jit(solution)/shard_map/ppermute | solution.py:553
  51.9 1.8 %collective-permute-done.21.refs_6_ = bf16[128,1024]{1,0:T(8,128)(2,1)S(1)} collective-permute-done((bf16[128,1024]{1,0:T(8,128)(2,1)S(1)}, bf16[128,1024]{1,0:T(8,128)(2,1)S(1)}, u32[]{:S(2)}, u32[]{:S(2)}) %collective-permute-start.21) | collective-permute-done | bytes 262176 | tf_op jit(solution)/shard_map/ppermute | solution.py:553
  (45 shorter events, 7.7 us)
Async XLA Ops:
  0.6 10.3 %collective-permute-start.6 = (bf16[128,1024]{1,0:T(8,128)(2,1)}, bf16[128,1024]{1,0:T(8,128)(2,1)S(1)}, u32[]{:S(2)}, u32[]{:S(2)}) collective-permute-start(bf16[128,1024]{1,0:T(8,128)(2,1)} %refs_6_.3), channel_id=1, source_target_pairs={{0,2},{1,3},{2,0},{3,1},{4,6},{5,7},{6,4},{7,5},{8,10},{9,11},{10,... | collective-permute-start | bytes 786440 | tf_op jit(solution)/shard_map/ppermute | solution.py:553
  3.6 10.5 %collective-permute-start.4 = (bf16[128,1024]{1,0:T(8,128)(2,1)}, bf16[128,1024]{1,0:T(8,128)(2,1)S(1)}, u32[]{:S(2)}, u32[]{:S(2)}) collective-permute-start(bf16[128,1024]{1,0:T(8,128)(2,1)} %refs_2_.3), channel_id=1, source_target_pairs={{0,4},{1,5},{2,6},{3,7},{4,0},{5,1},{6,2},{7,3},{8,12},{9,13},{10,... | collective-permute-start | bytes 786440 | tf_op jit(solution)/shard_map/ppermute | solution.py:553
  7.4 7.2 %collective-permute-start = (bf16[320,128]{1,0:T(8,128)(2,1)}, bf16[320,128]{1,0:T(8,128)(2,1)S(1)}, u32[]{:S(2)}, u32[]{:S(2)}) collective-permute-start(bf16[320,128]{1,0:T(8,128)(2,1)} %get-tuple-element.44), channel_id=1, source_target_pairs={{0,6},{1,7},{2,4},{3,5},{4,2},{5,3},{6,0},{7,1},{8,14},{9,15},{10,... | collective-permute-start | bytes 245768 | tf_op jit(solution)/shard_map/ppermute | solution.py:553
  7.5 13.2 %collective-permute-start.1 = (bf16[176,1024]{1,0:T(8,128)(2,1)}, bf16[176,1024]{1,0:T(8,128)(2,1)S(1)}, u32[]{:S(2)}, u32[]{:S(2)}) collective-permute-start(bf16[176,1024]{1,0:T(8,128)(2,1)} %get-tuple-element.46), channel_id=1, source_target_pairs={{0,2},{1,3},{2,0},{3,1},{4,6},{5,7},{6,4},{7,5},{8,10},{9,11},{10,... | collective-permute-start | bytes 1081352 | tf_op jit(solution)/shard_map/ppermute | solution.py:553
  9.4 12.5 %collective-permute-start.2 = (bf16[176,1024]{1,0:T(8,128)(2,1)}, bf16[176,1024]{1,0:T(8,128)(2,1)S(1)}, u32[]{:S(2)}, u32[]{:S(2)}) collective-permute-start(bf16[176,1024]{1,0:T(8,128)(2,1)} %get-tuple-element.47), channel_id=1, source_target_pairs={{0,4},{1,5},{2,6},{3,7},{4,0},{5,1},{6,2},{7,3},{8,12},{9,13},{10,... | collective-permute-start | bytes 1081352 | tf_op jit(solution)/shard_map/ppermute | solution.py:553
  11.0 15.8 %collective-permute-start.7 = (bf16[128,1024]{1,0:T(8,128)(2,1)S(1)}, bf16[128,1024]{1,0:T(8,128)(2,1)S(1)}, u32[]{:S(2)}, u32[]{:S(2)}) collective-permute-start(bf16[128,1024]{1,0:T(8,128)(2,1)S(1)} %collective-permute-done.6.refs_5_.refs_7_), channel_id=1, source_target_pairs={{0,4},{1,5},{2,6},{3,7},{4,0},{5,1},{6,2},{7,3},{8,12},{9,13},{10,... | collective-permute-start | bytes 786440 | tf_op jit(solution)/shard_map/ppermute | solution.py:553
  14.2 12.5 %collective-permute-start.5 = (bf16[128,1024]{1,0:T(8,128)(2,1)S(1)}, bf16[128,1024]{1,0:T(8,128)(2,1)S(1)}, u32[]{:S(2)}, u32[]{:S(2)}) collective-permute-start(bf16[128,1024]{1,0:T(8,128)(2,1)S(1)} %collective-permute-done.4.refs_2_), channel_id=1, source_target_pairs={{0,2},{1,3},{2,0},{3,1},{4,6},{5,7},{6,4},{7,5},{8,10},{9,11},{10,... | collective-permute-start | bytes 786440 | tf_op jit(solution)/shard_map/ppermute | solution.py:553
  15.3 6.7 %copy-start.2 = (bf16[128,1024]{1,0:T(8,128)(2,1)S(1)}, bf16[128,1024]{1,0:T(8,128)(2,1)}, u32[]{:S(2)}) copy-start(bf16[128,1024]{1,0:T(8,128)(2,1)} %refs_3_.3) | copy-start | bytes 786436
  15.3 6.7 %copy-start.3 = (bf16[320,128]{1,0:T(8,128)(2,1)S(1)}, bf16[320,128]{1,0:T(8,128)(2,1)}, u32[]{:S(2)}) copy-start(bf16[320,128]{1,0:T(8,128)(2,1)} %get-tuple-element.43.refs_0_) | copy-start | bytes 245764
  22.1 1.3 %collective-permute-start.8 = (bf16[256,128]{1,0:T(8,128)(2,1)S(1)}, bf16[256,128]{1,0:T(8,128)(2,1)S(1)}, u32[]{:S(2)}, u32[]{:S(2)}) collective-permute-start(bf16[256,128]{1,0:T(8,128)(2,1)S(1)} %get-tuple-element.50.refs_0_), channel_id=1, source_target_pairs={{0,1},{1,0},{2,3},{3,2},{4,5},{5,4},{6,7},{7,6},{8,9},{9,8},{10,11... | collective-permute-start | bytes 196616 | tf_op jit(solution)/shard_map/ppermute | solution.py:553
  22.2 4.6 %collective-permute-start.3 = (bf16[2048,128]{1,0:T(8,128)(2,1)S(1)}, bf16[2048,128]{1,0:T(8,128)(2,1)S(1)}, u32[]{:S(2)}, u32[]{:S(2)}) collective-permute-start(bf16[2048,128]{1,0:T(8,128)(2,1)S(1)} %get-tuple-element.48.near), channel_id=1, source_target_pairs={{0,1},{1,0},{2,3},{3,2},{4,5},{5,4},{6,7},{7,6},{8,9},{9,8},{10,11... | collective-permute-start | bytes 1572872 | tf_op jit(solution)/shard_map/ppermute | solution.py:553
  27.6 1.6 %collective-permute-start.9 = (bf16[1024,128]{1,0:T(8,128)(2,1)S(1)}, bf16[1024,128]{1,0:T(8,128)(2,1)S(1)}, u32[]{:S(2)}, u32[]{:S(2)}) collective-permute-start(bf16[1024,128]{1,0:T(8,128)(2,1)S(1)} %get-tuple-element.56), channel_id=1, source_target_pairs={{0,1},{1,0},{2,3},{3,2},{4,5},{5,4},{6,7},{7,6},{8,9},{9,8},{10,11... | collective-permute-start | bytes 786440 | tf_op jit(solution)/shard_map/ppermute | solution.py:553
  29.2 3.5 %collective-permute-start.10 = (bf16[512,1024]{1,0:T(8,128)(2,1)S(1)}, bf16[512,1024]{1,0:T(8,128)(2,1)S(1)}, u32[]{:S(2)}, u32[]{:S(2)}) collective-permute-start(bf16[512,1024]{1,0:T(8,128)(2,1)S(1)} %shard_map.128.own_feats), channel_id=1, source_target_pairs={{0,1},{1,0},{2,3},{3,2},{4,5},{5,4},{6,7},{7,6},{8,9},{9,8},{10,11... | collective-permute-start | bytes 3145736 | tf_op jit(solution)/shard_map/ppermute | solution.py:553
  30.6 2.9 %collective-permute-start.15 = (bf16[512,128]{1,0:T(8,128)(2,1)S(1)}, bf16[512,128]{1,0:T(8,128)(2,1)S(1)}, u32[]{:S(2)}, u32[]{:S(2)}) collective-permute-start(bf16[512,128]{1,0:T(8,128)(2,1)S(1)} %get-tuple-element.70), channel_id=1, source_target_pairs={{0,1},{1,0},{2,3},{3,2},{4,5},{5,4},{6,7},{7,6},{8,9},{9,8},{10,11... | collective-permute-start | bytes 393224 | tf_op jit(solution)/shard_map/ppermute | solution.py:553
  33.3 1.6 %collective-permute-start.11 = (f32[512,128]{1,0:T(8,128)S(1)}, f32[512,128]{1,0:T(8,128)S(1)}, u32[]{:S(2)}, u32[]{:S(2)}) collective-permute-start(f32[512,128]{1,0:T(8,128)S(1)} %get-tuple-element.64.refs_5_), channel_id=1, source_target_pairs={{0,1},{1,0},{2,3},{3,2},{4,5},{5,4},{6,7},{7,6},{8,9},{9,8},{10,11... | collective-permute-start | bytes 786440 | tf_op jit(solution)/shard_map/ppermute | solution.py:553
  34.5 5.2 %collective-permute-start.16 = (bf16[128,1024]{1,0:T(8,128)(2,1)S(1)}, bf16[128,1024]{1,0:T(8,128)(2,1)S(1)}, u32[]{:S(2)}, u32[]{:S(2)}) collective-permute-start(bf16[128,1024]{1,0:T(8,128)(2,1)S(1)} %get-tuple-element.71), channel_id=1, source_target_pairs={{0,1},{1,0},{2,3},{3,2},{4,5},{5,4},{6,7},{7,6},{8,9},{9,8},{10,11... | collective-permute-start | bytes 786440 | tf_op jit(solution)/shard_map/ppermute | solution.py:553
  35.0 6.3 %collective-permute-start.12 = (bf16[128,256]{1,0:T(8,128)(2,1)S(1)}, bf16[128,256]{1,0:T(8,128)(2,1)S(1)}, u32[]{:S(2)}, u32[]{:S(2)}) collective-permute-start(bf16[128,256]{1,0:T(8,128)(2,1)S(1)} %get-tuple-element.66), channel_id=1, source_target_pairs={{0,2},{1,3},{2,0},{3,1},{4,6},{5,7},{6,4},{7,5},{8,10},{9,11},{10,... | collective-permute-start | bytes 196616 | tf_op jit(solution)/shard_map/ppermute | solution.py:553
  35.5 7.3 %collective-permute-start.13 = (bf16[128,256]{1,0:T(8,128)(2,1)S(1)}, bf16[128,256]{1,0:T(8,128)(2,1)S(1)}, u32[]{:S(2)}, u32[]{:S(2)}) collective-permute-start(bf16[128,256]{1,0:T(8,128)(2,1)S(1)} %get-tuple-element.67), channel_id=1, source_target_pairs={{0,4},{1,5},{2,6},{3,7},{4,0},{5,1},{6,2},{7,3},{8,12},{9,13},{10,... | collective-permute-start | bytes 196616 | tf_op jit(solution)/shard_map/ppermute | solution.py:553
  37.1 5.6 %collective-permute-start.14 = (bf16[128,256]{1,0:T(8,128)(2,1)S(1)}, bf16[128,256]{1,0:T(8,128)(2,1)S(1)}, u32[]{:S(2)}, u32[]{:S(2)}) collective-permute-start(bf16[128,256]{1,0:T(8,128)(2,1)S(1)} %get-tuple-element.68), channel_id=1, source_target_pairs={{0,6},{1,7},{2,4},{3,5},{4,2},{5,3},{6,0},{7,1},{8,14},{9,15},{10,... | collective-permute-start | bytes 196616 | tf_op jit(solution)/shard_map/ppermute | solution.py:553
  39.2 11.7 %collective-permute-start.19 = (bf16[128,1024]{1,0:T(8,128)(2,1)S(1)}, bf16[128,1024]{1,0:T(8,128)(2,1)S(1)}, u32[]{:S(2)}, u32[]{:S(2)}) collective-permute-start(bf16[128,1024]{1,0:T(8,128)(2,1)S(1)} %get-tuple-element.75), channel_id=1, source_target_pairs={{0,2},{1,3},{2,0},{3,1},{4,6},{5,7},{6,4},{7,5},{8,10},{9,11},{10,... | collective-permute-start | bytes 786440 | tf_op jit(solution)/shard_map/ppermute | solution.py:553
  39.7 12.2 %collective-permute-start.20 = (bf16[128,1024]{1,0:T(8,128)(2,1)S(1)}, bf16[128,1024]{1,0:T(8,128)(2,1)S(1)}, u32[]{:S(2)}, u32[]{:S(2)}) collective-permute-start(bf16[128,1024]{1,0:T(8,128)(2,1)S(1)} %get-tuple-element.76), channel_id=1, source_target_pairs={{0,4},{1,5},{2,6},{3,7},{4,0},{5,1},{6,2},{7,3},{8,12},{9,13},{10,... | collective-permute-start | bytes 786440 | tf_op jit(solution)/shard_map/ppermute | solution.py:553
  41.3 12.4 %collective-permute-start.21 = (bf16[128,1024]{1,0:T(8,128)(2,1)S(1)}, bf16[128,1024]{1,0:T(8,128)(2,1)S(1)}, u32[]{:S(2)}, u32[]{:S(2)}) collective-permute-start(bf16[128,1024]{1,0:T(8,128)(2,1)S(1)} %get-tuple-element.77), channel_id=1, source_target_pairs={{0,6},{1,7},{2,4},{3,5},{4,2},{5,3},{6,0},{7,1},{8,14},{9,15},{10,... | collective-permute-start | bytes 786440 | tf_op jit(solution)/shard_map/ppermute | solution.py:553
  43.7 4.4 %collective-permute-start.17 = (bf16[288,128]{1,0:T(8,128)(2,1)S(1)}, bf16[288,128]{1,0:T(8,128)(2,1)S(1)}, u32[]{:S(2)}, u32[]{:S(2)}) collective-permute-start(bf16[288,128]{1,0:T(8,128)(2,1)S(1)} %get-tuple-element.73.refs_0_), channel_id=1, source_target_pairs={{0,8},{8,0},{16,24},{24,16},{1,9},{9,1},{17,25},{25,17},{2,10},{10... | collective-permute-start | bytes 221192 | tf_op jit(solution)/shard_map/ppermute | solution.py:553
  48.2 5.5 %collective-permute-start.18 = (bf16[2,128,128]{2,1,0:T(8,128)(2,1)S(1)}, bf16[2,128,128]{2,1,0:T(8,128)(2,1)S(1)}, u32[]{:S(2)}, u32[]{:S(2)}) collective-permute-start(bf16[2,128,128]{2,1,0:T(8,128)(2,1)S(1)} %shard_map.133.refs_0_), channel_id=1, source_target_pairs={{0,16},{8,24},{16,0},{24,8},{1,17},{9,25},{17,1},{25,9},{2,18},{10... | collective-permute-start | bytes 196616 | tf_op jit(solution)/shard_map/ppermute | solution.py:553
  (3 other events, 14.0 us)

commit v7 on v6

--- a/solution.py
+++ b/solution.py
@@ -356,8 +356,8 @@
     dagg, own_radial, columns, offsets = refs[:4]
     made = refs[4:6] if ahead else ()
     refs = refs[4 + len(made) :]
-    turned, terms, spread = refs[:3]
-    scratch = refs[3:]
+    turned, spread = refs[:2]
+    scratch = refs[2:]
     me = lax.axis_index("fsdp")
     atoms = columns.shape[0] // n
     tile = 2 * margin
@@ -380,15 +380,17 @@
             fill_place(margin, neighbors, offsets[rows_at(e, SLOT)], place)
             own_place = place
         for t in range(2):
-            own = terms.at[2 * (e % (terms.shape[0] // 2)) + t]
             here = slice(t * tile, (t + 1) * tile)
-            for k in range(neighbors):
-                own[k * tile : (k + 1) * tile] = (
-                    own_values[here, k * LANES : (k + 1) * LANES] * flow[here]
-                ).astype(bf16)
+            own = jnp.concatenate(
+                [
+                    (own_values[here, k * LANES : (k + 1) * LANES] * flow[here]).astype(bf16)
+                    for k in range(neighbors)
+                ],
+                axis=0,
+            )
             window = pl.ds(pl.multiple_of(e * atoms + t * tile, tile), 2 * tile)
             spread[t, window] = jnp.dot(
-                own_place[t * 2 * tile : (t + 1) * 2 * tile], own[...], preferred_element_type=f32
+                own_place[t * 2 * tile : (t + 1) * 2 * tile], own, preferred_element_type=f32
             )
         return 0
 
@@ -696,7 +698,6 @@
         functools.partial(backward_kernel, n, margin, neighbors, ahead),
         [((LANES, all_atoms), bf16)],
         [
-            ((2 * min(n, 8) if ahead else 2, neighbors * 2 * margin, LANES), bf16),
             ((2, all_atoms + 2 * margin, LANES), f32),
         ]
         + (step_scratch + [((2 * atoms, neighbors * 2 * margin), bf16)]) * (not ahead),

time: 54.8 us -> 54.2 us (0.989)
  transfers between devices with their start and end apart: 22 -> 22, of which waited for: 9 -> 9; matrix products, arithmetic and copies ran while one was open for 0% -> 0% of each run, Pallas kernels for 20% -> 19%
where the time goes in v7:
time: 54.2 us; the launch traced here: 54 us
  starting transfers between devices  23.5 us (43%)
  waiting for transfers between devices  16.2 us (30%)
  Pallas kernels  12.3 us (23%)
  between operations  1.42 us (3%)
  local copies, waits for them, and re-layouts  0.7 us (1%)
    ppermute x22, starting transfers between devices, hop(): return lax.ppermute(value, axis, [(i, i ^ step) for i in range(count)])  23.5 us
    ppermute x22, waiting for transfers between devices, hop(): return lax.ppermute(value, axis, [(i, i ^ step) for i in range(count)])  16.2 us
    pallas_call x12, Pallas kernels, run(): pl.pallas_call(kernel, out_shape=[jax.ShapeDtypeStruct(shape, dtype) for...  12.3 us
  transfers between devices with their start and end apart: 22, of which 9 were waited for; matrix products, arithmetic and copies ran while one was open for 0% of the time, Pallas kernels for 19%

profile of v7, /device:TPU:0, one launch (start us, length us, event | category | flops | bytes accessed | tf_op | source)
XLA Modules:
  0.0 54.0 jit_solution(4079191695286453953)
XLA Ops:
  0.6 3.0 %collective-permute-start.6 = (bf16[128,1024]{1,0:T(8,128)(2,1)}, bf16[128,1024]{1,0:T(8,128)(2,1)S(1)}, u32[]{:S(2)}, u32[]{:S(2)}) collective-permute-start(bf16[128,1024]{1,0:T(8,128)(2,1)} %refs_6_.3), channel_id=1, source_target_pairs={{0,2},{1,3},{2,0},{3,1},{4,6},{5,7},{6,4},{7,5},{8,10},{9,11},{10,... | collective-permute-start | bytes 786440 | tf_op jit(solution)/shard_map/ppermute | solution.py:555
  3.6 1.5 %collective-permute-start.4 = (bf16[128,1024]{1,0:T(8,128)(2,1)}, bf16[128,1024]{1,0:T(8,128)(2,1)S(1)}, u32[]{:S(2)}, u32[]{:S(2)}) collective-permute-start(bf16[128,1024]{1,0:T(8,128)(2,1)} %refs_2_.3), channel_id=1, source_target_pairs={{0,4},{1,5},{2,6},{3,7},{4,0},{5,1},{6,2},{7,3},{8,12},{9,13},{10,... | collective-permute-start | bytes 786440 | tf_op jit(solution)/shard_map/ppermute | solution.py:555
  5.2 2.2 %shard_map.120 = (bf16[320,128]{1,0:T(8,128)(2,1)}, bf16[320,128]{1,0:T(8,128)(2,1)}, bf16[176,1024]{1,0:T(8,128)(2,1)}, bf16[176,1024]{1,0:T(8,128)(2,1)}, f32[8,128]{1,0:T(8,128)}) custom-call(bf16[128,1024]{1,0:T(8,128)(2,1)} %refs_0_.1, s32[12,128]{1,0:T(8,128)} %refs_1_.1, f32[12,128]{1,0:T(8,128)} %refs_2_.2, s32[1,128]{1,0:T(1,128)} %refs_3_.2, ...), custom_call_target="tpu_custom_call" | custom-call | flops 1000000000 | bytes 3000000 | tf_op jit(solution)/shard_map/pallas_call | solution.py:520
  7.5 1.9 %collective-permute-start.1 = (bf16[176,1024]{1,0:T(8,128)(2,1)}, bf16[176,1024]{1,0:T(8,128)(2,1)S(1)}, u32[]{:S(2)}, u32[]{:S(2)}) collective-permute-start(bf16[176,1024]{1,0:T(8,128)(2,1)} %get-tuple-element.46), channel_id=1, source_target_pairs={{0,2},{1,3},{2,0},{3,1},{4,6},{5,7},{6,4},{7,5},{8,10},{9,11},{10,... | collective-permute-start | bytes 1081352 | tf_op jit(solution)/shard_map/ppermute | solution.py:555
  9.4 1.5 %collective-permute-start.2 = (bf16[176,1024]{1,0:T(8,128)(2,1)}, bf16[176,1024]{1,0:T(8,128)(2,1)S(1)}, u32[]{:S(2)}, u32[]{:S(2)}) collective-permute-start(bf16[176,1024]{1,0:T(8,128)(2,1)} %get-tuple-element.47), channel_id=1, source_target_pairs={{0,4},{1,5},{2,6},{3,7},{4,0},{5,1},{6,2},{7,3},{8,12},{9,13},{10,... | collective-permute-start | bytes 1081352 | tf_op jit(solution)/shard_map/ppermute | solution.py:555
  11.0 1.8 %collective-permute-start.7 = (bf16[128,1024]{1,0:T(8,128)(2,1)S(1)}, bf16[128,1024]{1,0:T(8,128)(2,1)S(1)}, u32[]{:S(2)}, u32[]{:S(2)}) collective-permute-start(bf16[128,1024]{1,0:T(8,128)(2,1)S(1)} %collective-permute-done.6.refs_5_.refs_7_), channel_id=1, source_target_pairs={{0,4},{1,5},{2,6},{3,7},{4,0},{5,1},{6,2},{7,3},{8,12},{9,13},{10,... | collective-permute-start | bytes 786440 | tf_op jit(solution)/shard_map/ppermute | solution.py:555
  12.8 1.4 %collective-permute-done.4.refs_2_ = bf16[128,1024]{1,0:T(8,128)(2,1)S(1)} collective-permute-done((bf16[128,1024]{1,0:T(8,128)(2,1)}, bf16[128,1024]{1,0:T(8,128)(2,1)S(1)}, u32[]{:S(2)}, u32[]{:S(2)}) %collective-permute-start.4) | collective-permute-done | bytes 262176 | tf_op jit(solution)/shard_map/ppermute | solution.py:555
  15.3 5.4 %collective-permute-done.1.refs_2_.refs_1_ = bf16[176,1024]{1,0:T(8,128)(2,1)S(1)} collective-permute-done((bf16[176,1024]{1,0:T(8,128)(2,1)}, bf16[176,1024]{1,0:T(8,128)(2,1)S(1)}, u32[]{:S(2)}, u32[]{:S(2)}) %collective-permute-start.1) | collective-permute-done | bytes 360480 | tf_op jit(solution)/shard_map/ppermute | solution.py:555
  20.7 1.2 %collective-permute-done.2.refs_3_.refs_6_.refs_8_ = bf16[176,1024]{1,0:T(8,128)(2,1)S(1)} collective-permute-done((bf16[176,1024]{1,0:T(8,128)(2,1)}, bf16[176,1024]{1,0:T(8,128)(2,1)S(1)}, u32[]{:S(2)}, u32[]{:S(2)}) %collective-permute-start.2) | collective-permute-done | bytes 360480 | tf_op jit(solution)/shard_map/ppermute | solution.py:555
  23.4 3.1 %shard_map.123 = (f32[1024,128]{1,0:T(8,128)S(1)}, f32[128,128]{1,0:T(8,128)S(1)}, f32[1024,1536]{1,0:T(8,128)S(1)}, bf16[6144,256]{1,0:T(8,128)(2,1)S(1)}, bf16[2048,768]{1,0:T(8,128)(2,1)S(1)}) custom-call(bf16[256,128]{1,0:T(8,128)(2,1)S(1)} %get-tuple-element.50.refs_0_, bf16[256,128]{1,0:T(8,128)(2,1)S(1)} %collective-permute-done.8.refs_1_, ...), custom_call_target="tpu_custom_call" | custom-call | tf_op jit(solution)/shard_map/pallas_call | solution.py:520
  27.7 1.5 %collective-permute-done.9.refs_1_.__1_ = bf16[1024,128]{1,0:T(8,128)(2,1)S(1)} collective-permute-done((bf16[1024,128]{1,0:T(8,128)(2,1)S(1)}, bf16[1024,128]{1,0:T(8,128)(2,1)S(1)}, u32[]{:S(2)}, u32[]{:S(2)}) %collective-permute-start.9) | collective-permute-done | bytes 262176 | tf_op jit(solution)/shard_map/ppermute | solution.py:555
  29.4 1.2 %shard_map.126 = (bf16[512,128]{1,0:T(8,128)(2,1)S(1)}, bf16[512,128]{1,0:T(8,128)(2,1)S(1)}, f32[1024,128]{1,0:T(8,128)S(1)}) custom-call(bf16[1024,128]{1,0:T(8,128)(2,1)S(1)} %get-tuple-element.55.refs_0_, bf16[1024,128]{1,0:T(8,128)(2,1)S(1)} %collective-permute-done.9.refs_1_.__1_, f32[1024,128]{1,0:T(8,128)S(1)} %get-tuple-element.57.refs_2_.refs_0_, ...), custom_call_target="tpu_custom_call" | custom-call | flops 1000000000 | bytes 3000000 | tf_op jit(solution)/shard_map/pallas_call | solution.py:520
  31.0 1.1 %shard_map.127.turned = bf16[128,1024]{1,0:T(8,128)(2,1)S(1)} custom-call(f32[1024,128]{1,0:T(8,128)S(1)} %get-tuple-element.60.refs_0_, f32[8,128]{1,0:T(8,128)S(1)} %copy-done.4, f32[1024,128]{1,0:T(8,128)S(1)} %get-tuple-element.57.refs_2_.refs_0_, f32[128,128]{1,0:T(8,128)S(1)} %get-tuple-element.51.__2_.refs_3_, ...), custom_call_target="tpu_custom_call" | custom-call | flops 1000000000 | bytes 3000000 | tf_op jit(solution)/shard_map/pallas_call | solution.py:520
  33.0 1.0 %shard_map.131 = (bf16[128,1024]{1,0:T(8,128)(2,1)S(1)}, bf16[128,1024]{1,0:T(8,128)(2,1)S(1)}, bf16[128,1024]{1,0:T(8,128)(2,1)S(1)}, bf16[128,1024]{1,0:T(8,12...) custom-call(f32[1024,128]{1,0:T(8,128)S(1)} %get-tuple-element.57.refs_2_.refs_0_, ...), custom_call_target="tpu_custom_call" | custom-call | flops 1000000000 | bytes 3000000 | tf_op jit(solution)/shard_map/pallas_call | solution.py:520
  34.9 1.6 %collective-permute-start.13 = (bf16[128,256]{1,0:T(8,128)(2,1)S(1)}, bf16[128,256]{1,0:T(8,128)(2,1)S(1)}, u32[]{:S(2)}, u32[]{:S(2)}) collective-permute-start(bf16[128,256]{1,0:T(8,128)(2,1)S(1)} %get-tuple-element.67), channel_id=1, source_target_pairs={{0,4},{1,5},{2,6},{3,7},{4,0},{5,1},{6,2},{7,3},{8,12},{9,13},{10,... | collective-permute-start | bytes 196616 | tf_op jit(solution)/shard_map/ppermute | solution.py:555
  36.6 1.4 %collective-permute-start.14 = (bf16[128,256]{1,0:T(8,128)(2,1)S(1)}, bf16[128,256]{1,0:T(8,128)(2,1)S(1)}, u32[]{:S(2)}, u32[]{:S(2)}) collective-permute-start(bf16[128,256]{1,0:T(8,128)(2,1)S(1)} %get-tuple-element.68), channel_id=1, source_target_pairs={{0,6},{1,7},{2,4},{3,5},{4,2},{5,3},{6,0},{7,1},{8,14},{9,15},{10,... | collective-permute-start | bytes 196616 | tf_op jit(solution)/shard_map/ppermute | solution.py:555
  39.1 1.6 %collective-permute-start.20 = (bf16[128,1024]{1,0:T(8,128)(2,1)S(1)}, bf16[128,1024]{1,0:T(8,128)(2,1)S(1)}, u32[]{:S(2)}, u32[]{:S(2)}) collective-permute-start(bf16[128,1024]{1,0:T(8,128)(2,1)S(1)} %get-tuple-element.76), channel_id=1, source_target_pairs={{0,4},{1,5},{2,6},{3,7},{4,0},{5,1},{6,2},{7,3},{8,12},{9,13},{10,... | collective-permute-start | bytes 786440 | tf_op jit(solution)/shard_map/ppermute | solution.py:555
  40.8 1.4 %collective-permute-start.21 = (bf16[128,1024]{1,0:T(8,128)(2,1)S(1)}, bf16[128,1024]{1,0:T(8,128)(2,1)S(1)}, u32[]{:S(2)}, u32[]{:S(2)}) collective-permute-start(bf16[128,1024]{1,0:T(8,128)(2,1)S(1)} %get-tuple-element.77), channel_id=1, source_target_pairs={{0,6},{1,7},{2,4},{3,5},{4,2},{5,3},{6,0},{7,1},{8,14},{9,15},{10,... | collective-permute-start | bytes 786440 | tf_op jit(solution)/shard_map/ppermute | solution.py:555
  42.2 1.0 %shard_map.132 = (bf16[1,128,1024]{2,1,0:T(8,128)(2,1)}, bf16[1,128,1024]{2,1,0:T(8,128)(2,1)}, bf16[288,128]{1,0:T(8,128)(2,1)S(1)}) custom-call(s32[1]{0:T(128)S(6)} %copy.21.fragment, bf16[128,256]{1,0:T(8,128)(2,1)S(1)} %get-tuple-element.65.refs_0_, bf16[128,256]{1,0:T(8,128)(2,1)S(1)} %collective-permute-done.12.refs_1_, ...), custom_call_target="tpu_custom_call" | custom-call | flops 4000000000 | bytes 12000000 | tf_op jit(solution)/shard_map/pallas_call | solution.py:520
  43.2 1.6 %collective-permute-start.17 = (bf16[288,128]{1,0:T(8,128)(2,1)S(1)}, bf16[288,128]{1,0:T(8,128)(2,1)S(1)}, u32[]{:S(2)}, u32[]{:S(2)}) collective-permute-start(bf16[288,128]{1,0:T(8,128)(2,1)S(1)} %get-tuple-element.73.refs_0_), channel_id=1, source_target_pairs={{0,8},{8,0},{16,24},{24,16},{1,9},{9,1},{17,25},{25,17},{2,10},{10... | collective-permute-start | bytes 221192 | tf_op jit(solution)/shard_map/ppermute | solution.py:555
  44.8 2.8 %collective-permute-done.17.refs_1_ = bf16[288,128]{1,0:T(8,128)(2,1)S(1)} collective-permute-done((bf16[288,128]{1,0:T(8,128)(2,1)S(1)}, bf16[288,128]{1,0:T(8,128)(2,1)S(1)}, u32[]{:S(2)}, u32[]{:S(2)}) %collective-permute-start.17) | collective-permute-done | bytes 73760 | tf_op jit(solution)/shard_map/ppermute | solution.py:555
  47.7 2.7 %collective-permute-start.18 = (bf16[2,128,128]{2,1,0:T(8,128)(2,1)S(1)}, bf16[2,128,128]{2,1,0:T(8,128)(2,1)S(1)}, u32[]{:S(2)}, u32[]{:S(2)}) collective-permute-start(bf16[2,128,128]{2,1,0:T(8,128)(2,1)S(1)} %shard_map.133.refs_0_), channel_id=1, source_target_pairs={{0,16},{8,24},{16,0},{24,8},{1,17},{9,25},{17,1},{25,9},{2,18},{10... | collective-permute-start | bytes 196616 | tf_op jit(solution)/shard_map/ppermute | solution.py:555
  50.3 1.0 %collective-permute-done.20.refs_5_ = bf16[128,1024]{1,0:T(8,128)(2,1)S(1)} collective-permute-done((bf16[128,1024]{1,0:T(8,128)(2,1)S(1)}, bf16[128,1024]{1,0:T(8,128)(2,1)S(1)}, u32[]{:S(2)}, u32[]{:S(2)}) %collective-permute-start.20) | collective-permute-done | bytes 262176 | tf_op jit(solution)/shard_map/ppermute | solution.py:555
  51.4 1.8 %collective-permute-done.21.refs_6_ = bf16[128,1024]{1,0:T(8,128)(2,1)S(1)} collective-permute-done((bf16[128,1024]{1,0:T(8,128)(2,1)S(1)}, bf16[128,1024]{1,0:T(8,128)(2,1)S(1)}, u32[]{:S(2)}, u32[]{:S(2)}) %collective-permute-start.21) | collective-permute-done | bytes 262176 | tf_op jit(solution)/shard_map/ppermute | solution.py:555
  (45 shorter events, 7.7 us)
Async XLA Ops:
  0.6 10.3 %collective-permute-start.6 = (bf16[128,1024]{1,0:T(8,128)(2,1)}, bf16[128,1024]{1,0:T(8,128)(2,1)S(1)}, u32[]{:S(2)}, u32[]{:S(2)}) collective-permute-start(bf16[128,1024]{1,0:T(8,128)(2,1)} %refs_6_.3), channel_id=1, source_target_pairs={{0,2},{1,3},{2,0},{3,1},{4,6},{5,7},{6,4},{7,5},{8,10},{9,11},{10,... | collective-permute-start | bytes 786440 | tf_op jit(solution)/shard_map/ppermute | solution.py:555
  3.6 10.5 %collective-permute-start.4 = (bf16[128,1024]{1,0:T(8,128)(2,1)}, bf16[128,1024]{1,0:T(8,128)(2,1)S(1)}, u32[]{:S(2)}, u32[]{:S(2)}) collective-permute-start(bf16[128,1024]{1,0:T(8,128)(2,1)} %refs_2_.3), channel_id=1, source_target_pairs={{0,4},{1,5},{2,6},{3,7},{4,0},{5,1},{6,2},{7,3},{8,12},{9,13},{10,... | collective-permute-start | bytes 786440 | tf_op jit(solution)/shard_map/ppermute | solution.py:555
  7.4 7.2 %collective-permute-start = (bf16[320,128]{1,0:T(8,128)(2,1)}, bf16[320,128]{1,0:T(8,128)(2,1)S(1)}, u32[]{:S(2)}, u32[]{:S(2)}) collective-permute-start(bf16[320,128]{1,0:T(8,128)(2,1)} %get-tuple-element.44), channel_id=1, source_target_pairs={{0,6},{1,7},{2,4},{3,5},{4,2},{5,3},{6,0},{7,1},{8,14},{9,15},{10,... | collective-permute-start | bytes 245768 | tf_op jit(solution)/shard_map/ppermute | solution.py:555
  7.5 13.2 %collective-permute-start.1 = (bf16[176,1024]{1,0:T(8,128)(2,1)}, bf16[176,1024]{1,0:T(8,128)(2,1)S(1)}, u32[]{:S(2)}, u32[]{:S(2)}) collective-permute-start(bf16[176,1024]{1,0:T(8,128)(2,1)} %get-tuple-element.46), channel_id=1, source_target_pairs={{0,2},{1,3},{2,0},{3,1},{4,6},{5,7},{6,4},{7,5},{8,10},{9,11},{10,... | collective-permute-start | bytes 1081352 | tf_op jit(solution)/shard_map/ppermute | solution.py:555
  9.4 12.5 %collective-permute-start.2 = (bf16[176,1024]{1,0:T(8,128)(2,1)}, bf16[176,1024]{1,0:T(8,128)(2,1)S(1)}, u32[]{:S(2)}, u32[]{:S(2)}) collective-permute-start(bf16[176,1024]{1,0:T(8,128)(2,1)} %get-tuple-element.47), channel_id=1, source_target_pairs={{0,4},{1,5},{2,6},{3,7},{4,0},{5,1},{6,2},{7,3},{8,12},{9,13},{10,... | collective-permute-start | bytes 1081352 | tf_op jit(solution)/shard_map/ppermute | solution.py:555
  11.0 15.8 %collective-permute-start.7 = (bf16[128,1024]{1,0:T(8,128)(2,1)S(1)}, bf16[128,1024]{1,0:T(8,128)(2,1)S(1)}, u32[]{:S(2)}, u32[]{:S(2)}) collective-permute-start(bf16[128,1024]{1,0:T(8,128)(2,1)S(1)} %collective-permute-done.6.refs_5_.refs_7_), channel_id=1, source_target_pairs={{0,4},{1,5},{2,6},{3,7},{4,0},{5,1},{6,2},{7,3},{8,12},{9,13},{10,... | collective-permute-start | bytes 786440 | tf_op jit(solution)/shard_map/ppermute | solution.py:555
  14.2 12.5 %collective-permute-start.5 = (bf16[128,1024]{1,0:T(8,128)(2,1)S(1)}, bf16[128,1024]{1,0:T(8,128)(2,1)S(1)}, u32[]{:S(2)}, u32[]{:S(2)}) collective-permute-start(bf16[128,1024]{1,0:T(8,128)(2,1)S(1)} %collective-permute-done.4.refs_2_), channel_id=1, source_target_pairs={{0,2},{1,3},{2,0},{3,1},{4,6},{5,7},{6,4},{7,5},{8,10},{9,11},{10,... | collective-permute-start | bytes 786440 | tf_op jit(solution)/shard_map/ppermute | solution.py:555
  15.3 6.7 %copy-start.2 = (bf16[128,1024]{1,0:T(8,128)(2,1)S(1)}, bf16[128,1024]{1,0:T(8,128)(2,1)}, u32[]{:S(2)}) copy-start(bf16[128,1024]{1,0:T(8,128)(2,1)} %refs_3_.3) | copy-start | bytes 786436
  15.3 6.7 %copy-start.3 = (bf16[320,128]{1,0:T(8,128)(2,1)S(1)}, bf16[320,128]{1,0:T(8,128)(2,1)}, u32[]{:S(2)}) copy-start(bf16[320,128]{1,0:T(8,128)(2,1)} %get-tuple-element.43.refs_0_) | copy-start | bytes 245764
  22.1 1.3 %collective-permute-start.8 = (bf16[256,128]{1,0:T(8,128)(2,1)S(1)}, bf16[256,128]{1,0:T(8,128)(2,1)S(1)}, u32[]{:S(2)}, u32[]{:S(2)}) collective-permute-start(bf16[256,128]{1,0:T(8,128)(2,1)S(1)} %get-tuple-element.50.refs_0_), channel_id=1, source_target_pairs={{0,1},{1,0},{2,3},{3,2},{4,5},{5,4},{6,7},{7,6},{8,9},{9,8},{10,11... | collective-permute-start | bytes 196616 | tf_op jit(solution)/shard_map/ppermute | solution.py:555
  22.2 4.6 %collective-permute-start.3 = (bf16[2048,128]{1,0:T(8,128)(2,1)S(1)}, bf16[2048,128]{1,0:T(8,128)(2,1)S(1)}, u32[]{:S(2)}, u32[]{:S(2)}) collective-permute-start(bf16[2048,128]{1,0:T(8,128)(2,1)S(1)} %get-tuple-element.48.near), channel_id=1, source_target_pairs={{0,1},{1,0},{2,3},{3,2},{4,5},{5,4},{6,7},{7,6},{8,9},{9,8},{10,11... | collective-permute-start | bytes 1572872 | tf_op jit(solution)/shard_map/ppermute | solution.py:555
  27.6 1.6 %collective-permute-start.9 = (bf16[1024,128]{1,0:T(8,128)(2,1)S(1)}, bf16[1024,128]{1,0:T(8,128)(2,1)S(1)}, u32[]{:S(2)}, u32[]{:S(2)}) collective-permute-start(bf16[1024,128]{1,0:T(8,128)(2,1)S(1)} %get-tuple-element.56), channel_id=1, source_target_pairs={{0,1},{1,0},{2,3},{3,2},{4,5},{5,4},{6,7},{7,6},{8,9},{9,8},{10,11... | collective-permute-start | bytes 786440 | tf_op jit(solution)/shard_map/ppermute | solution.py:555
  29.2 2.9 %collective-permute-start.10 = (bf16[512,1024]{1,0:T(8,128)(2,1)S(1)}, bf16[512,1024]{1,0:T(8,128)(2,1)S(1)}, u32[]{:S(2)}, u32[]{:S(2)}) collective-permute-start(bf16[512,1024]{1,0:T(8,128)(2,1)S(1)} %shard_map.128.own_feats), channel_id=1, source_target_pairs={{0,1},{1,0},{2,3},{3,2},{4,5},{5,4},{6,7},{7,6},{8,9},{9,8},{10,11... | collective-permute-start | bytes 3145736 | tf_op jit(solution)/shard_map/ppermute | solution.py:555
  30.6 2.4 %collective-permute-start.15 = (bf16[512,128]{1,0:T(8,128)(2,1)S(1)}, bf16[512,128]{1,0:T(8,128)(2,1)S(1)}, u32[]{:S(2)}, u32[]{:S(2)}) collective-permute-start(bf16[512,128]{1,0:T(8,128)(2,1)S(1)} %get-tuple-element.70), channel_id=1, source_target_pairs={{0,1},{1,0},{2,3},{3,2},{4,5},{5,4},{6,7},{7,6},{8,9},{9,8},{10,11... | collective-permute-start | bytes 393224 | tf_op jit(solution)/shard_map/ppermute | solution.py:555
  32.8 1.6 %collective-permute-start.11 = (f32[512,128]{1,0:T(8,128)S(1)}, f32[512,128]{1,0:T(8,128)S(1)}, u32[]{:S(2)}, u32[]{:S(2)}) collective-permute-start(f32[512,128]{1,0:T(8,128)S(1)} %get-tuple-element.64.refs_5_), channel_id=1, source_target_pairs={{0,1},{1,0},{2,3},{3,2},{4,5},{5,4},{6,7},{7,6},{8,9},{9,8},{10,11... | collective-permute-start | bytes 786440 | tf_op jit(solution)/shard_map/ppermute | solution.py:555
  33.9 5.2 %collective-permute-start.16 = (bf16[128,1024]{1,0:T(8,128)(2,1)S(1)}, bf16[128,1024]{1,0:T(8,128)(2,1)S(1)}, u32[]{:S(2)}, u32[]{:S(2)}) collective-permute-start(bf16[128,1024]{1,0:T(8,128)(2,1)S(1)} %get-tuple-element.71), channel_id=1, source_target_pairs={{0,1},{1,0},{2,3},{3,2},{4,5},{5,4},{6,7},{7,6},{8,9},{9,8},{10,11... | collective-permute-start | bytes 786440 | tf_op jit(solution)/shard_map/ppermute | solution.py:555
  34.4 6.3 %collective-permute-start.12 = (bf16[128,256]{1,0:T(8,128)(2,1)S(1)}, bf16[128,256]{1,0:T(8,128)(2,1)S(1)}, u32[]{:S(2)}, u32[]{:S(2)}) collective-permute-start(bf16[128,256]{1,0:T(8,128)(2,1)S(1)} %get-tuple-element.66), channel_id=1, source_target_pairs={{0,2},{1,3},{2,0},{3,1},{4,6},{5,7},{6,4},{7,5},{8,10},{9,11},{10,... | collective-permute-start | bytes 196616 | tf_op jit(solution)/shard_map/ppermute | solution.py:555
  34.9 7.3 %collective-permute-start.13 = (bf16[128,256]{1,0:T(8,128)(2,1)S(1)}, bf16[128,256]{1,0:T(8,128)(2,1)S(1)}, u32[]{:S(2)}, u32[]{:S(2)}) collective-permute-start(bf16[128,256]{1,0:T(8,128)(2,1)S(1)} %get-tuple-element.67), channel_id=1, source_target_pairs={{0,4},{1,5},{2,6},{3,7},{4,0},{5,1},{6,2},{7,3},{8,12},{9,13},{10,... | collective-permute-start | bytes 196616 | tf_op jit(solution)/shard_map/ppermute | solution.py:555
  36.6 5.6 %collective-permute-start.14 = (bf16[128,256]{1,0:T(8,128)(2,1)S(1)}, bf16[128,256]{1,0:T(8,128)(2,1)S(1)}, u32[]{:S(2)}, u32[]{:S(2)}) collective-permute-start(bf16[128,256]{1,0:T(8,128)(2,1)S(1)} %get-tuple-element.68), channel_id=1, source_target_pairs={{0,6},{1,7},{2,4},{3,5},{4,2},{5,3},{6,0},{7,1},{8,14},{9,15},{10,... | collective-permute-start | bytes 196616 | tf_op jit(solution)/shard_map/ppermute | solution.py:555
  38.6 11.7 %collective-permute-start.19 = (bf16[128,1024]{1,0:T(8,128)(2,1)S(1)}, bf16[128,1024]{1,0:T(8,128)(2,1)S(1)}, u32[]{:S(2)}, u32[]{:S(2)}) collective-permute-start(bf16[128,1024]{1,0:T(8,128)(2,1)S(1)} %get-tuple-element.75), channel_id=1, source_target_pairs={{0,2},{1,3},{2,0},{3,1},{4,6},{5,7},{6,4},{7,5},{8,10},{9,11},{10,... | collective-permute-start | bytes 786440 | tf_op jit(solution)/shard_map/ppermute | solution.py:555
  39.1 12.2 %collective-permute-start.20 = (bf16[128,1024]{1,0:T(8,128)(2,1)S(1)}, bf16[128,1024]{1,0:T(8,128)(2,1)S(1)}, u32[]{:S(2)}, u32[]{:S(2)}) collective-permute-start(bf16[128,1024]{1,0:T(8,128)(2,1)S(1)} %get-tuple-element.76), channel_id=1, source_target_pairs={{0,4},{1,5},{2,6},{3,7},{4,0},{5,1},{6,2},{7,3},{8,12},{9,13},{10,... | collective-permute-start | bytes 786440 | tf_op jit(solution)/shard_map/ppermute | solution.py:555
  40.8 12.4 %collective-permute-start.21 = (bf16[128,1024]{1,0:T(8,128)(2,1)S(1)}, bf16[128,1024]{1,0:T(8,128)(2,1)S(1)}, u32[]{:S(2)}, u32[]{:S(2)}) collective-permute-start(bf16[128,1024]{1,0:T(8,128)(2,1)S(1)} %get-tuple-element.77), channel_id=1, source_target_pairs={{0,6},{1,7},{2,4},{3,5},{4,2},{5,3},{6,0},{7,1},{8,14},{9,15},{10,... | collective-permute-start | bytes 786440 | tf_op jit(solution)/shard_map/ppermute | solution.py:555
  43.2 4.4 %collective-permute-start.17 = (bf16[288,128]{1,0:T(8,128)(2,1)S(1)}, bf16[288,128]{1,0:T(8,128)(2,1)S(1)}, u32[]{:S(2)}, u32[]{:S(2)}) collective-permute-start(bf16[288,128]{1,0:T(8,128)(2,1)S(1)} %get-tuple-element.73.refs_0_), channel_id=1, source_target_pairs={{0,8},{8,0},{16,24},{24,16},{1,9},{9,1},{17,25},{25,17},{2,10},{10... | collective-permute-start | bytes 221192 | tf_op jit(solution)/shard_map/ppermute | solution.py:555
  47.7 5.5 %collective-permute-start.18 = (bf16[2,128,128]{2,1,0:T(8,128)(2,1)S(1)}, bf16[2,128,128]{2,1,0:T(8,128)(2,1)S(1)}, u32[]{:S(2)}, u32[]{:S(2)}) collective-permute-start(bf16[2,128,128]{2,1,0:T(8,128)(2,1)S(1)} %shard_map.133.refs_0_), channel_id=1, source_target_pairs={{0,16},{8,24},{16,0},{24,8},{1,17},{9,25},{17,1},{25,9},{2,18},{10... | collective-permute-start | bytes 196616 | tf_op jit(solution)/shard_map/ppermute | solution.py:555
  (3 other events, 14.0 us)

commit v8 on v7

--- a/solution.py
+++ b/solution.py
@@ -258,10 +258,10 @@
     rows = own_weight.shape[0]
     if rows < LANES:
         both[...] = jnp.zeros_like(both)
-    both[:rows] = own_weight[...]
-    for q in range(both.shape[1] // LANES):
-        start = (2 * m + q) * rows
-        both[LANES : LANES + rows, q * LANES : (q + 1) * LANES] = far[start : start + rows]
+        both[:rows] = own_weight[...]
+        for q in range(both.shape[1] // LANES):
+            start = (2 * m + q) * rows
+            both[LANES : LANES + rows, q * LANES : (q + 1) * LANES] = far[start : start + rows]
     for c in range(m):
         for k, source in enumerate((near, far)):
             block = rows_at(me ^ (2 * c + k), rows)
@@ -273,8 +273,13 @@
         held_feats[c * atoms : (c + 1) * atoms] = feats[c][:atoms]
     projected = jnp.dot(held_feats[...], weights[...], preferred_element_type=f32).astype(bf16)
     flow = jnp.concatenate([cots[c][:atoms] for c in range(m)], axis=0)
+    pieces = both.shape[1] // LANES
+    other = jnp.concatenate(
+        [far[(2 * m + q) * rows : (2 * m + q + 1) * rows] for q in range(pieces)], axis=1
+    )
+    table = both[...] if rows < LANES else jnp.concatenate([own_weight[...], other], axis=0)
     dact = lax.dot_general(
-        flow, both[...], (((1,), (1,)), ((), ())), preferred_element_type=f32
+        flow, table, (((1,), (1,)), ((), ())), preferred_element_type=f32
     ).astype(bf16)
     for c in range(m):
         chip = (me // 2) ^ c
@@ -469,23 +474,33 @@
     give[...] = parts[LANES : LANES + rows].astype(bf16)
 
 
-def grads_kernel(n, fragment, *refs):
-    m = n // 2
-    near, got_part, own_part = refs[:m], refs[m], refs[m + 1]
-    msg_grad, out_grad, code, blocks, total = refs[m + 2 :]
+def join_blocks(n, near, blocks, grad):
     me = lax.axis_index("fsdp")
-    rows = msg_grad.shape[1]
-    width = msg_grad.shape[2] // n
-    lanes = pl.ds(pl.multiple_of(fragment[0] * FRAG, FRAG), FRAG)
-    for c in range(m):
+    width = grad.shape[-1] // n
+    for c in range(n // 2):
         blocks[me ^ (2 * c)] = near[c][:, :LANES]
         blocks[me ^ (2 * c + 1)] = near[c][:, LANES:]
     for e in range(n):
-        msg_grad[0, :, e * width : (e + 1) * width] = blocks[e][:, :width]
-    write_code(msg_grad[0, :, lanes].astype(f32), code.at[: rows + SLOT])
-    total[...] = own_part[...] + got_part[...].astype(f32)
-    out_grad[0] = total[...].astype(bf16)
-    write_code(total[:, lanes], code.at[rows + SLOT :])
+        grad[:, e * width : (e + 1) * width] = blocks[e][:, :width]
+
+
+def code_kernel(n, fragment, *refs):
+    m = n // 2
+    near, (got_part, own_part, code, blocks, joined) = refs[:m], refs[m:]
+    rows = joined.shape[0]
+    lanes = pl.ds(pl.multiple_of(fragment[0] * FRAG, FRAG), FRAG)
+    join_blocks(n, near, blocks, joined)
+    write_code(joined[:, lanes].astype(f32), code.at[: rows + SLOT])
+    total = own_part[:, lanes] + got_part[:, lanes].astype(f32)
+    write_code(total, code.at[rows + SLOT :])
+
+
+def grads_kernel(n, *refs):
+    m = n // 2
+    near, (got_part, own_part, _after, msg_grad, out_grad, made, blocks) = refs[:m], refs[m:]
+    made[...] = jnp.zeros_like(made)
+    join_blocks(n, near, blocks, msg_grad.at[0])
+    out_grad[0] = (own_part[...] + got_part[...].astype(f32)).astype(bf16)
 
 
 def pair_kernel(*refs):
@@ -505,7 +520,7 @@
 
 
 def last_kernel(count, *refs):
-    pair, (feats, *parts), (outer, node) = refs[:count], refs[count:-2], refs[-2:]
+    pair, (feats, *parts), (_after, outer, node) = refs[:count], refs[count:-3], refs[-3:]
     outer[...] = functools.reduce(jnp.add, [value[...].astype(f32) for value in pair])
     total = feats[...].astype(f32)
     for part in parts:
@@ -730,14 +745,23 @@
         memory,
     )
     near = across_chips(grad_sends)
-    grad_msg, grad_out, code = run(
+    got_part = hop(give_part, "fsdp", 1)
+    (code,) = run(
+        functools.partial(code_kernel, n),
+        [((2 * (rows + SLOT), FRAG), bf16)],
+        [((n, rows, LANES), bf16), ((rows, channels), bf16)],
+        [fragment, *near, got_part, own_part],
+        4,
+        memory,
+        scalars=1,
+    )
+    grad_msg, grad_out, made = run(
         functools.partial(grads_kernel, n),
-        [((1, rows, channels), bf16)] * 2 + [((2 * (rows + SLOT), FRAG), bf16)],
-        [((n, rows, LANES), bf16), ((rows, channels), f32)],
-        [fragment, *near, hop(give_part, "fsdp", 1), own_part],
-        4,
-        memory,
-        scalars=1,
+        [((1, rows, channels), bf16)] * 2 + [((8, LANES), f32)],
+        [((n, rows, LANES), bf16)],
+        [*near, got_part, own_part, code],
+        0,
+        memory,
     )
     sums = across_chips(sums)
     step = 1
@@ -764,7 +788,7 @@
         functools.partial(last_kernel, len(pair)),
         [((2, rows, FRAG), f32), ((atoms, channels), bf16)],
         [],
-        [*pair, node_feats, *sums],
+        [*pair, node_feats, *sums, made],
         0,
         memory,
     )

time: 54.2 us -> 54.2 us (level)
    pallas_call x12 -> x13, Pallas kernels: 12.3 us -> 12.4 us  [run(): pl.pallas_call(kernel, out_shape=[jax.ShapeDtypeStruct(shape, dtype) for...]
  transfers between devices with their start and end apart: 22 -> 22, of which waited for: 9 -> 9; matrix products, arithmetic and copies ran while one was open for 0% -> 0% of each run, Pallas kernels for 19% -> 20%
where the time goes in v8:
time: 54.2 us; the launch traced here: 54 us
  starting transfers between devices  23.5 us (43%)
  waiting for transfers between devices  15.9 us (29%)
  Pallas kernels  12.5 us (23%)
  between operations  1.43 us (3%)
  local copies, waits for them, and re-layouts  0.7 us (1%)
    ppermute x22, starting transfers between devices, hop(): return lax.ppermute(value, axis, [(i, i ^ step) for i in range(count)])  23.5 us
    ppermute x22, waiting for transfers between devices, hop(): return lax.ppermute(value, axis, [(i, i ^ step) for i in range(count)])  15.9 us
    pallas_call x13, Pallas kernels, run(): pl.pallas_call(kernel, out_shape=[jax.ShapeDtypeStruct(shape, dtype) for...  12.4 us
  transfers between devices with their start and end apart: 22, of which 9 were waited for; matrix products, arithmetic and copies ran while one was open for 0% of the time, Pallas kernels for 20%

profile of v8, /device:TPU:0, one launch (start us, length us, event | category | flops | bytes accessed | tf_op | source)
XLA Modules:
  0.0 54.0 jit_solution(16820294885228090907)
XLA Ops:
  0.6 3.0 %collective-permute-start.6 = (bf16[128,1024]{1,0:T(8,128)(2,1)}, bf16[128,1024]{1,0:T(8,128)(2,1)S(1)}, u32[]{:S(2)}, u32[]{:S(2)}) collective-permute-start(bf16[128,1024]{1,0:T(8,128)(2,1)} %refs_6_.3), channel_id=1, source_target_pairs={{0,2},{1,3},{2,0},{3,1},{4,6},{5,7},{6,4},{7,5},{8,10},{9,11},{10,... | collective-permute-start | bytes 786440 | tf_op jit(solution)/shard_map/ppermute | solution.py:570
  3.6 1.5 %collective-permute-start.4 = (bf16[128,1024]{1,0:T(8,128)(2,1)}, bf16[128,1024]{1,0:T(8,128)(2,1)S(1)}, u32[]{:S(2)}, u32[]{:S(2)}) collective-permute-start(bf16[128,1024]{1,0:T(8,128)(2,1)} %refs_2_.3), channel_id=1, source_target_pairs={{0,4},{1,5},{2,6},{3,7},{4,0},{5,1},{6,2},{7,3},{8,12},{9,13},{10,... | collective-permute-start | bytes 786440 | tf_op jit(solution)/shard_map/ppermute | solution.py:570
  5.2 2.2 %shard_map.120 = (bf16[320,128]{1,0:T(8,128)(2,1)}, bf16[320,128]{1,0:T(8,128)(2,1)}, bf16[176,1024]{1,0:T(8,128)(2,1)}, bf16[176,1024]{1,0:T(8,128)(2,1)}, f32[8,128]{1,0:T(8,128)}) custom-call(bf16[128,1024]{1,0:T(8,128)(2,1)} %refs_0_.1, s32[12,128]{1,0:T(8,128)} %refs_1_.1, f32[12,128]{1,0:T(8,128)} %refs_2_.2, s32[1,128]{1,0:T(1,128)} %refs_3_.2, ...), custom_call_target="tpu_custom_call" | custom-call | flops 1000000000 | bytes 3000000 | tf_op jit(solution)/shard_map/pallas_call | solution.py:535
  7.5 1.9 %collective-permute-start.1 = (bf16[176,1024]{1,0:T(8,128)(2,1)}, bf16[176,1024]{1,0:T(8,128)(2,1)S(1)}, u32[]{:S(2)}, u32[]{:S(2)}) collective-permute-start(bf16[176,1024]{1,0:T(8,128)(2,1)} %get-tuple-element.46), channel_id=1, source_target_pairs={{0,2},{1,3},{2,0},{3,1},{4,6},{5,7},{6,4},{7,5},{8,10},{9,11},{10,... | collective-permute-start | bytes 1081352 | tf_op jit(solution)/shard_map/ppermute | solution.py:570
  9.4 1.5 %collective-permute-start.2 = (bf16[176,1024]{1,0:T(8,128)(2,1)}, bf16[176,1024]{1,0:T(8,128)(2,1)S(1)}, u32[]{:S(2)}, u32[]{:S(2)}) collective-permute-start(bf16[176,1024]{1,0:T(8,128)(2,1)} %get-tuple-element.47), channel_id=1, source_target_pairs={{0,4},{1,5},{2,6},{3,7},{4,0},{5,1},{6,2},{7,3},{8,12},{9,13},{10,... | collective-permute-start | bytes 1081352 | tf_op jit(solution)/shard_map/ppermute | solution.py:570
  11.0 1.8 %collective-permute-start.7 = (bf16[128,1024]{1,0:T(8,128)(2,1)S(1)}, bf16[128,1024]{1,0:T(8,128)(2,1)S(1)}, u32[]{:S(2)}, u32[]{:S(2)}) collective-permute-start(bf16[128,1024]{1,0:T(8,128)(2,1)S(1)} %collective-permute-done.6.refs_5_.refs_7_), channel_id=1, source_target_pairs={{0,4},{1,5},{2,6},{3,7},{4,0},{5,1},{6,2},{7,3},{8,12},{9,13},{10,... | collective-permute-start | bytes 786440 | tf_op jit(solution)/shard_map/ppermute | solution.py:570
  12.8 1.4 %collective-permute-done.4.refs_2_ = bf16[128,1024]{1,0:T(8,128)(2,1)S(1)} collective-permute-done((bf16[128,1024]{1,0:T(8,128)(2,1)}, bf16[128,1024]{1,0:T(8,128)(2,1)S(1)}, u32[]{:S(2)}, u32[]{:S(2)}) %collective-permute-start.4) | collective-permute-done | bytes 262176 | tf_op jit(solution)/shard_map/ppermute | solution.py:570
  15.3 5.4 %collective-permute-done.1.refs_2_.refs_1_ = bf16[176,1024]{1,0:T(8,128)(2,1)S(1)} collective-permute-done((bf16[176,1024]{1,0:T(8,128)(2,1)}, bf16[176,1024]{1,0:T(8,128)(2,1)S(1)}, u32[]{:S(2)}, u32[]{:S(2)}) %collective-permute-start.1) | collective-permute-done | bytes 360480 | tf_op jit(solution)/shard_map/ppermute | solution.py:570
  20.7 1.2 %collective-permute-done.2.refs_3_.refs_6_.refs_8_ = bf16[176,1024]{1,0:T(8,128)(2,1)S(1)} collective-permute-done((bf16[176,1024]{1,0:T(8,128)(2,1)}, bf16[176,1024]{1,0:T(8,128)(2,1)S(1)}, u32[]{:S(2)}, u32[]{:S(2)}) %collective-permute-start.2) | collective-permute-done | bytes 360480 | tf_op jit(solution)/shard_map/ppermute | solution.py:570
  23.4 3.1 %shard_map.123 = (f32[1024,128]{1,0:T(8,128)S(1)}, f32[128,128]{1,0:T(8,128)S(1)}, f32[1024,1536]{1,0:T(8,128)S(1)}, bf16[6144,256]{1,0:T(8,128)(2,1)S(1)}, bf16[2048,768]{1,0:T(8,128)(2,1)S(1)}) custom-call(bf16[256,128]{1,0:T(8,128)(2,1)S(1)} %get-tuple-element.50.refs_0_, bf16[256,128]{1,0:T(8,128)(2,1)S(1)} %collective-permute-done.8.refs_1_, ...), custom_call_target="tpu_custom_call" | custom-call | tf_op jit(solution)/shard_map/pallas_call | solution.py:535
  27.7 1.5 %collective-permute-done.9.refs_1_.__1_ = bf16[1024,128]{1,0:T(8,128)(2,1)S(1)} collective-permute-done((bf16[1024,128]{1,0:T(8,128)(2,1)S(1)}, bf16[1024,128]{1,0:T(8,128)(2,1)S(1)}, u32[]{:S(2)}, u32[]{:S(2)}) %collective-permute-start.9) | collective-permute-done | bytes 262176 | tf_op jit(solution)/shard_map/ppermute | solution.py:570
  29.3 1.2 %shard_map.126 = (bf16[512,128]{1,0:T(8,128)(2,1)S(1)}, bf16[512,128]{1,0:T(8,128)(2,1)S(1)}, f32[1024,128]{1,0:T(8,128)S(1)}) custom-call(bf16[1024,128]{1,0:T(8,128)(2,1)S(1)} %get-tuple-element.55.refs_0_, bf16[1024,128]{1,0:T(8,128)(2,1)S(1)} %collective-permute-done.9.refs_1_.__1_, f32[1024,128]{1,0:T(8,128)S(1)} %get-tuple-element.57.refs_2_.refs_0_, ...), custom_call_target="tpu_custom_call" | custom-call | flops 1000000000 | bytes 3000000 | tf_op jit(solution)/shard_map/pallas_call | solution.py:535
  31.0 1.1 %shard_map.127.turned = bf16[128,1024]{1,0:T(8,128)(2,1)S(1)} custom-call(f32[1024,128]{1,0:T(8,128)S(1)} %get-tuple-element.60.refs_0_, f32[8,128]{1,0:T(8,128)S(1)} %copy-done.4, f32[1024,128]{1,0:T(8,128)S(1)} %get-tuple-element.57.refs_2_.refs_0_, f32[128,128]{1,0:T(8,128)S(1)} %get-tuple-element.51.__2_.refs_3_, ...), custom_call_target="tpu_custom_call" | custom-call | flops 1000000000 | bytes 3000000 | tf_op jit(solution)/shard_map/pallas_call | solution.py:535
  32.9 1.0 %shard_map.131 = (bf16[128,1024]{1,0:T(8,128)(2,1)S(1)}, bf16[128,1024]{1,0:T(8,128)(2,1)S(1)}, bf16[128,1024]{1,0:T(8,128)(2,1)S(1)}, bf16[128,1024]{1,0:T(8,12...) custom-call(f32[1024,128]{1,0:T(8,128)S(1)} %get-tuple-element.57.refs_2_.refs_0_, ...), custom_call_target="tpu_custom_call" | custom-call | flops 1000000000 | bytes 3000000 | tf_op jit(solution)/shard_map/pallas_call | solution.py:535
  34.9 1.6 %collective-permute-start.13 = (bf16[128,256]{1,0:T(8,128)(2,1)S(1)}, bf16[128,256]{1,0:T(8,128)(2,1)S(1)}, u32[]{:S(2)}, u32[]{:S(2)}) collective-permute-start(bf16[128,256]{1,0:T(8,128)(2,1)S(1)} %get-tuple-element.67), channel_id=1, source_target_pairs={{0,4},{1,5},{2,6},{3,7},{4,0},{5,1},{6,2},{7,3},{8,12},{9,13},{10,... | collective-permute-start | bytes 196616 | tf_op jit(solution)/shard_map/ppermute | solution.py:570
  36.5 1.4 %collective-permute-start.14 = (bf16[128,256]{1,0:T(8,128)(2,1)S(1)}, bf16[128,256]{1,0:T(8,128)(2,1)S(1)}, u32[]{:S(2)}, u32[]{:S(2)}) collective-permute-start(bf16[128,256]{1,0:T(8,128)(2,1)S(1)} %get-tuple-element.68), channel_id=1, source_target_pairs={{0,6},{1,7},{2,4},{3,5},{4,2},{5,3},{6,0},{7,1},{8,14},{9,15},{10,... | collective-permute-start | bytes 196616 | tf_op jit(solution)/shard_map/ppermute | solution.py:570
  39.1 1.6 %collective-permute-start.20 = (bf16[128,1024]{1,0:T(8,128)(2,1)S(1)}, bf16[128,1024]{1,0:T(8,128)(2,1)S(1)}, u32[]{:S(2)}, u32[]{:S(2)}) collective-permute-start(bf16[128,1024]{1,0:T(8,128)(2,1)S(1)} %get-tuple-element.75), channel_id=1, source_target_pairs={{0,4},{1,5},{2,6},{3,7},{4,0},{5,1},{6,2},{7,3},{8,12},{9,13},{10,... | collective-permute-start | bytes 786440 | tf_op jit(solution)/shard_map/ppermute | solution.py:570
  40.7 1.4 %collective-permute-start.21 = (bf16[128,1024]{1,0:T(8,128)(2,1)S(1)}, bf16[128,1024]{1,0:T(8,128)(2,1)S(1)}, u32[]{:S(2)}, u32[]{:S(2)}) collective-permute-start(bf16[128,1024]{1,0:T(8,128)(2,1)S(1)} %get-tuple-element.76), channel_id=1, source_target_pairs={{0,6},{1,7},{2,4},{3,5},{4,2},{5,3},{6,0},{7,1},{8,14},{9,15},{10,... | collective-permute-start | bytes 786440 | tf_op jit(solution)/shard_map/ppermute | solution.py:570
  42.4 1.6 %collective-permute-start.17 = (bf16[288,128]{1,0:T(8,128)(2,1)S(1)}, bf16[288,128]{1,0:T(8,128)(2,1)S(1)}, u32[]{:S(2)}, u32[]{:S(2)}) collective-permute-start(bf16[288,128]{1,0:T(8,128)(2,1)S(1)} %shard_map.132.refs_0_.refs_6_), channel_id=1, source_target_pairs={{0,8},{8,0},{16,24},{24,16},{1,9},{9,1},{17,25},{25,17},{2,10},{10... | collective-permute-start | bytes 221192 | tf_op jit(solution)/shard_map/ppermute | solution.py:570
  44.1 2.8 %collective-permute-done.17.refs_1_ = bf16[288,128]{1,0:T(8,128)(2,1)S(1)} collective-permute-done((bf16[288,128]{1,0:T(8,128)(2,1)S(1)}, bf16[288,128]{1,0:T(8,128)(2,1)S(1)}, u32[]{:S(2)}, u32[]{:S(2)}) %collective-permute-start.17) | collective-permute-done | bytes 73760 | tf_op jit(solution)/shard_map/ppermute | solution.py:570
  47.0 2.7 %collective-permute-start.18 = (bf16[2,128,128]{2,1,0:T(8,128)(2,1)S(1)}, bf16[2,128,128]{2,1,0:T(8,128)(2,1)S(1)}, u32[]{:S(2)}, u32[]{:S(2)}) collective-permute-start(bf16[2,128,128]{2,1,0:T(8,128)(2,1)S(1)} %shard_map.133.refs_0_), channel_id=1, source_target_pairs={{0,16},{8,24},{16,0},{24,8},{1,17},{9,25},{17,1},{25,9},{2,18},{10... | collective-permute-start | bytes 196616 | tf_op jit(solution)/shard_map/ppermute | solution.py:570
  49.6 0.9 %shard_map.134 = (bf16[1,128,1024]{2,1,0:T(8,128)(2,1)}, bf16[1,128,1024]{2,1,0:T(8,128)(2,1)}, f32[8,128]{1,0:T(8,128)S(1)}) custom-call(bf16[128,256]{1,0:T(8,128)(2,1)S(1)} %get-tuple-element.65.refs_0_, bf16[128,256]{1,0:T(8,128)(2,1)S(1)} %collective-permute-done.12.refs_1_, bf16[128,256]{1,0:T(8,128)(2,1)S(1)} %collective-permute-done.13.refs_2_, ...), custom_call_target="tpu_custom_call" | custom-call | tf_op jit(solution)/shard_map/pallas_call | solution.py:535
  51.3 1.8 %collective-permute-done.21.refs_6_ = bf16[128,1024]{1,0:T(8,128)(2,1)S(1)} collective-permute-done((bf16[128,1024]{1,0:T(8,128)(2,1)S(1)}, bf16[128,1024]{1,0:T(8,128)(2,1)S(1)}, u32[]{:S(2)}, u32[]{:S(2)}) %collective-permute-start.21) | collective-permute-done | bytes 262176 | tf_op jit(solution)/shard_map/ppermute | solution.py:570
  53.1 0.9 %shard_map.135 = (f32[2,128,128]{2,1,0:T(8,128)}, bf16[128,1024]{1,0:T(8,128)(2,1)}) custom-call(bf16[2,128,128]{2,1,0:T(8,128)(2,1)S(1)} %shard_map.133.refs_0_, bf16[2,128,128]{2,1,0:T(8,128)(2,1)S(1)} %collective-permute-done.18.refs_1_, bf16[128,1024]{1,0:T(8,128)(2,1)S(1)} %copy-done, bf16[128,1024]{1,0:T(8,128)(2,1)S(1)} %get-tuple-element.73.refs_3_, ...), custom_call_target="tpu_custom_call" | custom-call | tf_op jit(solution)/shard_map/pallas_call | solution.py:535
  (46 shorter events, 7.9 us)
Async XLA Ops:
  0.6 10.3 %collective-permute-start.6 = (bf16[128,1024]{1,0:T(8,128)(2,1)}, bf16[128,1024]{1,0:T(8,128)(2,1)S(1)}, u32[]{:S(2)}, u32[]{:S(2)}) collective-permute-start(bf16[128,1024]{1,0:T(8,128)(2,1)} %refs_6_.3), channel_id=1, source_target_pairs={{0,2},{1,3},{2,0},{3,1},{4,6},{5,7},{6,4},{7,5},{8,10},{9,11},{10,... | collective-permute-start | bytes 786440 | tf_op jit(solution)/shard_map/ppermute | solution.py:570
  3.6 10.5 %collective-permute-start.4 = (bf16[128,1024]{1,0:T(8,128)(2,1)}, bf16[128,1024]{1,0:T(8,128)(2,1)S(1)}, u32[]{:S(2)}, u32[]{:S(2)}) collective-permute-start(bf16[128,1024]{1,0:T(8,128)(2,1)} %refs_2_.3), channel_id=1, source_target_pairs={{0,4},{1,5},{2,6},{3,7},{4,0},{5,1},{6,2},{7,3},{8,12},{9,13},{10,... | collective-permute-start | bytes 786440 | tf_op jit(solution)/shard_map/ppermute | solution.py:570
  7.4 7.2 %collective-permute-start = (bf16[320,128]{1,0:T(8,128)(2,1)}, bf16[320,128]{1,0:T(8,128)(2,1)S(1)}, u32[]{:S(2)}, u32[]{:S(2)}) collective-permute-start(bf16[320,128]{1,0:T(8,128)(2,1)} %get-tuple-element.44), channel_id=1, source_target_pairs={{0,6},{1,7},{2,4},{3,5},{4,2},{5,3},{6,0},{7,1},{8,14},{9,15},{10,... | collective-permute-start | bytes 245768 | tf_op jit(solution)/shard_map/ppermute | solution.py:570
  7.5 13.2 %collective-permute-start.1 = (bf16[176,1024]{1,0:T(8,128)(2,1)}, bf16[176,1024]{1,0:T(8,128)(2,1)S(1)}, u32[]{:S(2)}, u32[]{:S(2)}) collective-permute-start(bf16[176,1024]{1,0:T(8,128)(2,1)} %get-tuple-element.46), channel_id=1, source_target_pairs={{0,2},{1,3},{2,0},{3,1},{4,6},{5,7},{6,4},{7,5},{8,10},{9,11},{10,... | collective-permute-start | bytes 1081352 | tf_op jit(solution)/shard_map/ppermute | solution.py:570
  9.4 12.5 %collective-permute-start.2 = (bf16[176,1024]{1,0:T(8,128)(2,1)}, bf16[176,1024]{1,0:T(8,128)(2,1)S(1)}, u32[]{:S(2)}, u32[]{:S(2)}) collective-permute-start(bf16[176,1024]{1,0:T(8,128)(2,1)} %get-tuple-element.47), channel_id=1, source_target_pairs={{0,4},{1,5},{2,6},{3,7},{4,0},{5,1},{6,2},{7,3},{8,12},{9,13},{10,... | collective-permute-start | bytes 1081352 | tf_op jit(solution)/shard_map/ppermute | solution.py:570
  11.0 15.8 %collective-permute-start.7 = (bf16[128,1024]{1,0:T(8,128)(2,1)S(1)}, bf16[128,1024]{1,0:T(8,128)(2,1)S(1)}, u32[]{:S(2)}, u32[]{:S(2)}) collective-permute-start(bf16[128,1024]{1,0:T(8,128)(2,1)S(1)} %collective-permute-done.6.refs_5_.refs_7_), channel_id=1, source_target_pairs={{0,4},{1,5},{2,6},{3,7},{4,0},{5,1},{6,2},{7,3},{8,12},{9,13},{10,... | collective-permute-start | bytes 786440 | tf_op jit(solution)/shard_map/ppermute | solution.py:570
  14.2 12.5 %collective-permute-start.5 = (bf16[128,1024]{1,0:T(8,128)(2,1)S(1)}, bf16[128,1024]{1,0:T(8,128)(2,1)S(1)}, u32[]{:S(2)}, u32[]{:S(2)}) collective-permute-start(bf16[128,1024]{1,0:T(8,128)(2,1)S(1)} %collective-permute-done.4.refs_2_), channel_id=1, source_target_pairs={{0,2},{1,3},{2,0},{3,1},{4,6},{5,7},{6,4},{7,5},{8,10},{9,11},{10,... | collective-permute-start | bytes 786440 | tf_op jit(solution)/shard_map/ppermute | solution.py:570
  15.3 6.7 %copy-start.2 = (bf16[128,1024]{1,0:T(8,128)(2,1)S(1)}, bf16[128,1024]{1,0:T(8,128)(2,1)}, u32[]{:S(2)}) copy-start(bf16[128,1024]{1,0:T(8,128)(2,1)} %refs_3_.3) | copy-start | bytes 786436
  15.3 6.7 %copy-start.3 = (bf16[320,128]{1,0:T(8,128)(2,1)S(1)}, bf16[320,128]{1,0:T(8,128)(2,1)}, u32[]{:S(2)}) copy-start(bf16[320,128]{1,0:T(8,128)(2,1)} %get-tuple-element.43.refs_0_) | copy-start | bytes 245764
  22.1 1.3 %collective-permute-start.8 = (bf16[256,128]{1,0:T(8,128)(2,1)S(1)}, bf16[256,128]{1,0:T(8,128)(2,1)S(1)}, u32[]{:S(2)}, u32[]{:S(2)}) collective-permute-start(bf16[256,128]{1,0:T(8,128)(2,1)S(1)} %get-tuple-element.50.refs_0_), channel_id=1, source_target_pairs={{0,1},{1,0},{2,3},{3,2},{4,5},{5,4},{6,7},{7,6},{8,9},{9,8},{10,11... | collective-permute-start | bytes 196616 | tf_op jit(solution)/shard_map/ppermute | solution.py:570
  22.2 4.6 %collective-permute-start.3 = (bf16[2048,128]{1,0:T(8,128)(2,1)S(1)}, bf16[2048,128]{1,0:T(8,128)(2,1)S(1)}, u32[]{:S(2)}, u32[]{:S(2)}) collective-permute-start(bf16[2048,128]{1,0:T(8,128)(2,1)S(1)} %get-tuple-element.48.near), channel_id=1, source_target_pairs={{0,1},{1,0},{2,3},{3,2},{4,5},{5,4},{6,7},{7,6},{8,9},{9,8},{10,11... | collective-permute-start | bytes 1572872 | tf_op jit(solution)/shard_map/ppermute | solution.py:570
  27.6 1.6 %collective-permute-start.9 = (bf16[1024,128]{1,0:T(8,128)(2,1)S(1)}, bf16[1024,128]{1,0:T(8,128)(2,1)S(1)}, u32[]{:S(2)}, u32[]{:S(2)}) collective-permute-start(bf16[1024,128]{1,0:T(8,128)(2,1)S(1)} %get-tuple-element.56), channel_id=1, source_target_pairs={{0,1},{1,0},{2,3},{3,2},{4,5},{5,4},{6,7},{7,6},{8,9},{9,8},{10,11... | collective-permute-start | bytes 786440 | tf_op jit(solution)/shard_map/ppermute | solution.py:570
  29.2 2.9 %collective-permute-start.10 = (bf16[512,1024]{1,0:T(8,128)(2,1)S(1)}, bf16[512,1024]{1,0:T(8,128)(2,1)S(1)}, u32[]{:S(2)}, u32[]{:S(2)}) collective-permute-start(bf16[512,1024]{1,0:T(8,128)(2,1)S(1)} %shard_map.128.own_feats), channel_id=1, source_target_pairs={{0,1},{1,0},{2,3},{3,2},{4,5},{5,4},{6,7},{7,6},{8,9},{9,8},{10,11... | collective-permute-start | bytes 3145736 | tf_op jit(solution)/shard_map/ppermute | solution.py:570
  30.5 2.4 %collective-permute-start.15 = (bf16[512,128]{1,0:T(8,128)(2,1)S(1)}, bf16[512,128]{1,0:T(8,128)(2,1)S(1)}, u32[]{:S(2)}, u32[]{:S(2)}) collective-permute-start(bf16[512,128]{1,0:T(8,128)(2,1)S(1)} %get-tuple-element.70), channel_id=1, source_target_pairs={{0,1},{1,0},{2,3},{3,2},{4,5},{5,4},{6,7},{7,6},{8,9},{9,8},{10,11... | collective-permute-start | bytes 393224 | tf_op jit(solution)/shard_map/ppermute | solution.py:570
  32.7 1.6 %collective-permute-start.11 = (f32[512,128]{1,0:T(8,128)S(1)}, f32[512,128]{1,0:T(8,128)S(1)}, u32[]{:S(2)}, u32[]{:S(2)}) collective-permute-start(f32[512,128]{1,0:T(8,128)S(1)} %get-tuple-element.64.refs_5_), channel_id=1, source_target_pairs={{0,1},{1,0},{2,3},{3,2},{4,5},{5,4},{6,7},{7,6},{8,9},{9,8},{10,11... | collective-permute-start | bytes 786440 | tf_op jit(solution)/shard_map/ppermute | solution.py:570
  33.9 5.2 %collective-permute-start.16 = (bf16[128,1024]{1,0:T(8,128)(2,1)S(1)}, bf16[128,1024]{1,0:T(8,128)(2,1)S(1)}, u32[]{:S(2)}, u32[]{:S(2)}) collective-permute-start(bf16[128,1024]{1,0:T(8,128)(2,1)S(1)} %get-tuple-element.71), channel_id=1, source_target_pairs={{0,1},{1,0},{2,3},{3,2},{4,5},{5,4},{6,7},{7,6},{8,9},{9,8},{10,11... | collective-permute-start | bytes 786440 | tf_op jit(solution)/shard_map/ppermute | solution.py:570
  34.4 6.3 %collective-permute-start.12 = (bf16[128,256]{1,0:T(8,128)(2,1)S(1)}, bf16[128,256]{1,0:T(8,128)(2,1)S(1)}, u32[]{:S(2)}, u32[]{:S(2)}) collective-permute-start(bf16[128,256]{1,0:T(8,128)(2,1)S(1)} %get-tuple-element.66), channel_id=1, source_target_pairs={{0,2},{1,3},{2,0},{3,1},{4,6},{5,7},{6,4},{7,5},{8,10},{9,11},{10,... | collective-permute-start | bytes 196616 | tf_op jit(solution)/shard_map/ppermute | solution.py:570
  34.9 7.3 %collective-permute-start.13 = (bf16[128,256]{1,0:T(8,128)(2,1)S(1)}, bf16[128,256]{1,0:T(8,128)(2,1)S(1)}, u32[]{:S(2)}, u32[]{:S(2)}) collective-permute-start(bf16[128,256]{1,0:T(8,128)(2,1)S(1)} %get-tuple-element.67), channel_id=1, source_target_pairs={{0,4},{1,5},{2,6},{3,7},{4,0},{5,1},{6,2},{7,3},{8,12},{9,13},{10,... | collective-permute-start | bytes 196616 | tf_op jit(solution)/shard_map/ppermute | solution.py:570
  36.5 5.7 %collective-permute-start.14 = (bf16[128,256]{1,0:T(8,128)(2,1)S(1)}, bf16[128,256]{1,0:T(8,128)(2,1)S(1)}, u32[]{:S(2)}, u32[]{:S(2)}) collective-permute-start(bf16[128,256]{1,0:T(8,128)(2,1)S(1)} %get-tuple-element.68), channel_id=1, source_target_pairs={{0,6},{1,7},{2,4},{3,5},{4,2},{5,3},{6,0},{7,1},{8,14},{9,15},{10,... | collective-permute-start | bytes 196616 | tf_op jit(solution)/shard_map/ppermute | solution.py:570
  38.6 12.0 %collective-permute-start.19 = (bf16[128,1024]{1,0:T(8,128)(2,1)S(1)}, bf16[128,1024]{1,0:T(8,128)(2,1)S(1)}, u32[]{:S(2)}, u32[]{:S(2)}) collective-permute-start(bf16[128,1024]{1,0:T(8,128)(2,1)S(1)} %get-tuple-element.74), channel_id=1, source_target_pairs={{0,2},{1,3},{2,0},{3,1},{4,6},{5,7},{6,4},{7,5},{8,10},{9,11},{10,... | collective-permute-start | bytes 786440 | tf_op jit(solution)/shard_map/ppermute | solution.py:570
  39.1 12.2 %collective-permute-start.20 = (bf16[128,1024]{1,0:T(8,128)(2,1)S(1)}, bf16[128,1024]{1,0:T(8,128)(2,1)S(1)}, u32[]{:S(2)}, u32[]{:S(2)}) collective-permute-start(bf16[128,1024]{1,0:T(8,128)(2,1)S(1)} %get-tuple-element.75), channel_id=1, source_target_pairs={{0,4},{1,5},{2,6},{3,7},{4,0},{5,1},{6,2},{7,3},{8,12},{9,13},{10,... | collective-permute-start | bytes 786440 | tf_op jit(solution)/shard_map/ppermute | solution.py:570
  40.7 12.4 %collective-permute-start.21 = (bf16[128,1024]{1,0:T(8,128)(2,1)S(1)}, bf16[128,1024]{1,0:T(8,128)(2,1)S(1)}, u32[]{:S(2)}, u32[]{:S(2)}) collective-permute-start(bf16[128,1024]{1,0:T(8,128)(2,1)S(1)} %get-tuple-element.76), channel_id=1, source_target_pairs={{0,6},{1,7},{2,4},{3,5},{4,2},{5,3},{6,0},{7,1},{8,14},{9,15},{10,... | collective-permute-start | bytes 786440 | tf_op jit(solution)/shard_map/ppermute | solution.py:570
  42.4 4.4 %collective-permute-start.17 = (bf16[288,128]{1,0:T(8,128)(2,1)S(1)}, bf16[288,128]{1,0:T(8,128)(2,1)S(1)}, u32[]{:S(2)}, u32[]{:S(2)}) collective-permute-start(bf16[288,128]{1,0:T(8,128)(2,1)S(1)} %shard_map.132.refs_0_.refs_6_), channel_id=1, source_target_pairs={{0,8},{8,0},{16,24},{24,16},{1,9},{9,1},{17,25},{25,17},{2,10},{10... | collective-permute-start | bytes 221192 | tf_op jit(solution)/shard_map/ppermute | solution.py:570
  47.0 6.1 %collective-permute-start.18 = (bf16[2,128,128]{2,1,0:T(8,128)(2,1)S(1)}, bf16[2,128,128]{2,1,0:T(8,128)(2,1)S(1)}, u32[]{:S(2)}, u32[]{:S(2)}) collective-permute-start(bf16[2,128,128]{2,1,0:T(8,128)(2,1)S(1)} %shard_map.133.refs_0_), channel_id=1, source_target_pairs={{0,16},{8,24},{16,0},{24,8},{1,17},{9,25},{17,1},{25,9},{2,18},{10... | collective-permute-start | bytes 196616 | tf_op jit(solution)/shard_map/ppermute | solution.py:570
  (3 other events, 14.0 us)
